TPU v7x, 32 devices: a whole 2x2x4 slice. The times are simulated.
32 devices in a mesh: rows: 16 (over z, x, core), fsdp: 2 (over y).
Axes of the slice: x: 2, y: 2, z: 4, core: 2. Of those that a mesh axis runs over, the one named last changes fastest.
Arguments:
- tokens: bfloat16 [2, 4096, 512], P('fsdp', 'rows'), may hold values from -6 to 6
- w_qkv: bfloat16 [512, 1536], P(('rows', 'fsdp')), may hold values from -0.25 to 0.25
- w_out: bfloat16 [512, 512], P(('rows', 'fsdp')), may hold values from -0.75 to 0.75
- w_up: bfloat16 [512, 2048], P(('rows', 'fsdp')), may hold values from -0.25 to 0.25
- w_down: bfloat16 [2048, 512], P(('rows', 'fsdp')), may hold values from -0.125 to 0.125
- norm1_gain: bfloat16 [512], P(('rows', 'fsdp')), may hold values from 0.099609375 to 1.8984375
- norm1_bias: bfloat16 [512], P(('rows', 'fsdp')), may hold values from -4 to 4
- query_bias: bfloat16 [512], P(('rows', 'fsdp')), may hold values from -4 to 4
- value_bias: bfloat16 [512], P(('rows', 'fsdp')), may hold values from -4 to 4
- out_bias: bfloat16 [512], P(('rows', 'fsdp')), may hold values from -4 to 4
- norm2_gain: bfloat16 [512], P(('rows', 'fsdp')), may hold values from 0.099609375 to 1.8984375
- norm2_bias: bfloat16 [512], P(('rows', 'fsdp')), may hold values from -4 to 4
- up_bias: bfloat16 [2048], P(('rows', 'fsdp')), may hold values from -4 to 4
- down_bias: bfloat16 [512], P(('rows', 'fsdp')), may hold values from -4 to 4
- cotangent: bfloat16 [2, 4096, 512], P('fsdp', 'rows'), may hold values from -6 to 6
- table_start: int32 [2, 8], P('fsdp'), may hold values from 0 to 4064, as said below
- support_count: int32 [2, 8], P('fsdp'), may hold values from 1 to 2904, as said below
- query_count: int32 [2, 8], P('fsdp'), may hold values from 1 to 968, as said below
Outputs:
- outputs: bfloat16 [2, 4096, 512], P('fsdp', 'rows')
- grad_tokens: bfloat16 [2, 4096, 512], P('fsdp', 'rows')
- grad_w_qkv: float32 [512, 1536], P(('rows', 'fsdp'))
- grad_w_out: float32 [512, 512], P(('rows', 'fsdp'))
- grad_w_up: float32 [512, 2048], P(('rows', 'fsdp'))
- grad_w_down: float32 [2048, 512], P(('rows', 'fsdp'))
- grad_norm1_gain: float32 [512], P(('rows', 'fsdp'))
- grad_norm1_bias: float32 [512], P(('rows', 'fsdp'))
- grad_query_bias: float32 [512], P(('rows', 'fsdp'))
- grad_value_bias: float32 [512], P(('rows', 'fsdp'))
- grad_out_bias: float32 [512], P(('rows', 'fsdp'))
- grad_norm2_gain: float32 [512], P(('rows', 'fsdp'))
- grad_norm2_bias: float32 [512], P(('rows', 'fsdp'))
- grad_up_bias: float32 [2048], P(('rows', 'fsdp'))
- grad_down_bias: float32 [512], P(('rows', 'fsdp'))
Inputs may be any that keep to these rules, and one draw needn't show every extreme that they name: `table_start`: in each group the starts rise, the first is 0, and each table runs up to the next start (the last up to 4096); the last table of every group has 32 rows. `support_count`: at least one support row in every table. `query_count`: support plus query rows never exceed the table's rows; the rest of a table is padding.
All inputs are finite; a program needn't handle non-finite values.
Results may differ from a plain program's by a relative error of at most 0.013.
Values may be sent and summed in bfloat16 or wider, within the bound.
No kernel may reach another device: no remote copies, remote signals or barrier semaphores. Data moves between devices by JAX's collectives and lax.ppermute only.
A program may use at most 128 MiB of HBM per device.

v0:
```python
import functools
import math

import jax
import jax.numpy as jnp
import numpy as np
from jax import lax
from jax.experimental import pallas as pl
from jax.experimental.pallas import tpu as pltpu
from jax.sharding import PartitionSpec as P

HEADS = 4
HEAD_DIM = 128
EPS = 1e-05
NEG = -1e30
PLANE = 4
MIB = 1024 * 1024
BF = jnp.bfloat16
F32 = jnp.float32
I32 = jnp.int32
SCALE = 1.0 / math.sqrt(HEAD_DIM)
SCALE2 = SCALE * math.log2(math.e)
GELU_A = math.sqrt(2.0 / math.pi)
GELU_B = 0.044715

VMEM = pl.BlockSpec(memory_space=pltpu.VMEM)
SMEM = pl.BlockSpec(memory_space=pltpu.SMEM)
HBM = pl.BlockSpec(memory_space=pltpu.HBM)
ANY = pl.BlockSpec(memory_space=pl.ANY)


def after(value, *others):
    return lax.optimization_barrier((value, *others))[0]


def together(*values):
    return lax.optimization_barrier(values)


def mm(left, right):
    return jnp.dot(left, right, preferred_element_type=F32)


def mm_nt(left, right):
    return lax.dot_general(left, right, (((1,), (1,)), ((), ())), preferred_element_type=F32)


def mm_tn(left, right):
    return lax.dot_general(left, right, (((0,), (0,)), ((), ())), preferred_element_type=F32)


def call(body, outs, ins, in_specs, out_specs, scratch=(), flops=0, moved=0, trans=0, vmem=16, name=None):
    return pl.pallas_call(
        body,
        out_shape=outs,
        in_specs=in_specs,
        out_specs=out_specs,
        scratch_shapes=scratch,
        compiler_params=pltpu.CompilerParams(vmem_limit_bytes=vmem * MIB),
        cost_estimate=pl.CostEstimate(
            flops=int(flops), bytes_accessed=int(moved), transcendentals=int(trans)
        ),
        name=name,
    )(*ins)


def normalize(values):
    centre = values - jnp.mean(values, axis=-1, keepdims=True)
    spread = jnp.mean(centre * centre, axis=-1, keepdims=True)
    inverse = lax.rsqrt(spread + EPS)
    return centre * inverse, inverse


def norm_back(grad_out, plain, inverse, gain):
    scaled = grad_out * gain
    return inverse * (
        scaled
        - jnp.mean(scaled, axis=-1, keepdims=True)
        - plain * jnp.mean(scaled * plain, axis=-1, keepdims=True)
    )


def table_of(tab, count, pos):
    low = jnp.zeros_like(pos) + tab[0]
    high = low + tab[count]
    finish = high + tab[2 * count]
    for t in range(1, count):
        here = pos >= tab[t]
        top = tab[t] + tab[count + t]
        low = jnp.where(here, tab[t], low)
        high = jnp.where(here, top, high)
        finish = jnp.where(here, top + tab[2 * count + t], finish)
    return low, high, finish


def pack_body(qkv_ref, out_ref, up_ref, down_ref, *refs):
    vec_refs, (q_ref, m_ref, vec_scr) = refs[:-3], refs[-3:]
    part, width = out_ref.shape
    blocks = up_ref.shape[1] // width
    vec_scr[...] = jnp.zeros(vec_scr.shape, F32)
    for k, ref in enumerate(vec_refs[:-1]):
        vec_scr[k : k + 1, :part] = ref[...].astype(F32)
    for j in range(blocks):
        vec_scr[8 + j : 9 + j, :part] = vec_refs[-1][:, j * part : (j + 1) * part].astype(F32)
    for i in range(3):
        q_ref[i] = qkv_ref[:, i * width : (i + 1) * width]
    q_ref[3] = jnp.zeros((part, width), BF)
    q_ref[3, :, :HEAD_DIM] = jnp.transpose(vec_scr[...])[:part].astype(BF)
    m_ref[0] = out_ref[...]
    for j in range(blocks):
        m_ref[1 + j] = up_ref[:, j * width : (j + 1) * width]
        m_ref[1 + blocks + j] = down_ref[j * part : (j + 1) * part, :]


def sum_body(*refs, plan, count):
    for out_ref, terms in zip(refs[count:], plan, strict=True):
        total = None
        for which, spot in terms:
            term = refs[which][spot].astype(F32)
            total = term if total is None else total + term
        out_ref[...] = total.astype(out_ref.dtype)


def join_body(*refs, plan, count):
    out_ref, row = refs[count], 0
    for terms in plan:
        total = None
        for which, spot in terms:
            term = refs[which][spot].astype(F32)
            total = term if total is None else total + term
        out_ref[row : row + total.shape[0]] = total.astype(out_ref.dtype)
        row += total.shape[0]


def join_up(arrays, plan):
    shapes = [jax.eval_shape(lambda v: v[terms[0][1]], arrays[terms[0][0]]).shape for terms in plan]
    shape = (sum(v[0] for v in shapes),) + shapes[0][1:]
    moved = math.prod(shape) * 4
    return call(
        functools.partial(join_body, plan=plan, count=len(arrays)), [jax.ShapeDtypeStruct(shape, BF)], arrays,
        [VMEM] * len(arrays), [VMEM], flops=moved, moved=moved, vmem=16, name="join",
    )


def add_up(arrays, plan, dtype=BF):
    outs = []
    for terms in plan:
        which, spot = terms[0]
        outs.append(jax.ShapeDtypeStruct(jax.eval_shape(lambda v: v[spot], arrays[which]).shape, dtype))
    moved = sum(o.size for o in outs) * 4
    return call(
        functools.partial(sum_body, plan=plan, count=len(arrays)), outs, arrays,
        [VMEM] * len(arrays), [VMEM] * len(outs), flops=moved, moved=moved, vmem=16, name="add",
    )


def copy_body(*refs, plan, count):
    outs, sem = refs[count:-1], refs[-1]
    copies = []
    for k, (which, source, out, spot) in enumerate(plan):
        copies.append(pltpu.make_async_copy(refs[which].at[source], outs[out].at[spot], sem.at[k]))
        copies[-1].start()
    for copy in copies:
        copy.wait()


def copy_out(arrays, shapes, plan):
    moved = sum(math.prod(shape) for shape in shapes) * 4
    return call(
        functools.partial(copy_body, plan=plan, count=len(arrays)),
        [jax.ShapeDtypeStruct(shape, arrays[0].dtype) for shape in shapes], arrays,
        [HBM] * len(arrays), [VMEM] * len(shapes),
        scratch=[pltpu.SemaphoreType.DMA((len(plan),))], moved=moved, vmem=4, name="copy",
    )


def stack(arrays):
    shape = (len(arrays),) + arrays[0].shape
    every = (slice(None),)
    (out,) = copy_out(arrays, [shape], [(i, every, 0, (i,)) for i in range(len(arrays))])
    return out


def assemble_body(idx, *refs, rows, count):
    pieces, (w_ref, row_ref, col_ref, low_scr, sem) = refs[:count], refs[count:]
    k = 0
    for piece in pieces:
        for j in range(piece.shape[0]):
            at = pl.ds(pl.multiple_of(idx[k] * rows, rows), rows)
            pltpu.make_async_copy(piece.at[j, pl.ds(0, 3)], w_ref.at[:, at, :], sem.at[0]).start()
            pltpu.make_async_copy(piece.at[j, 3, :, pl.ds(0, HEAD_DIM)], low_scr.at[at, :], sem.at[1]).start()
            k += 1
    pltpu.make_async_copy(low_scr, low_scr, sem.at[1]).wait()
    columns = low_scr[...].astype(F32)
    col_ref[...] = columns
    row_ref[...] = jnp.transpose(columns)[: row_ref.shape[0]]
    pltpu.make_async_copy(w_ref, w_ref, sem.at[0]).wait()


def project_body(*refs, with_q, spots, count):
    pieces, (w_ref, row_ref), outs = refs[:count], refs[count : count + 2], refs[count + 2 :]
    kv_ref, n_ref = outs[:2]
    gain, shift = row_ref[0:1, :], row_ref[1:2, :]
    for i, (which, lead) in enumerate(spots):
        plain, unused_inverse = normalize(pieces[which][lead].astype(F32))
        n_ref[i] = plain.astype(BF)
        normed = (plain * gain + shift).astype(BF)
        keys = mm(normed, w_ref[1])
        values = mm(normed, w_ref[2]) + row_ref[3:4, :]
        for h in range(HEADS):
            lanes = slice(h * HEAD_DIM, (h + 1) * HEAD_DIM)
            kv_ref[i, h] = keys[:, lanes].astype(BF)
            kv_ref[i, HEADS + h] = values[:, lanes].astype(BF)
        if with_q and i == 0:
            queries = (mm(normed, w_ref[0]) + row_ref[2:3, :]) * SCALE2
            for h in range(HEADS):
                outs[2][h] = queries[:, h * HEAD_DIM : (h + 1) * HEAD_DIM].astype(BF)


def ready_body(idx, *refs, rows, count, part):
    pieces, (own_ref, own_x_ref, tok_ref) = refs[:count], refs[count : count + 3]
    w_ref, row_ref, col_ref, up_ref, kv_own, n_own, q_ref, kv_z, n_z, n_first, low_scr, sem = refs[count + 3 :]
    assemble_body(idx, *pieces, w_ref, row_ref, col_ref, low_scr, sem, rows=rows, count=count)
    width = up_ref.shape[1]
    blocks = up_ref.shape[0]
    per = width // blocks
    source = lax.broadcasted_iota(I32, (per, width), 0)
    target = lax.broadcasted_iota(I32, (per, width), 1)
    total = jnp.zeros((blocks, width), F32)
    for k in range(blocks):
        spread = jnp.where(
            target == (source // part) * (blocks * part) + k * part + lax.rem(source, part), 1.0, 0.0
        ).astype(BF)
        mine = [row_ref[8 + k : 9 + k, j * per : (j + 1) * per] for j in range(blocks)]
        total += mm(jnp.concatenate(mine, axis=0).astype(BF), spread)
    up_ref[...] = total
    every = slice(None)
    project_body(
        own_ref, own_x_ref, w_ref, row_ref, kv_own, n_own, q_ref, with_q=True, spots=[(0, every), (1, every)], count=2
    )
    n_first[0] = n_own[0]
    spots = [(0, i) for i in range(tok_ref.shape[0])]
    project_body(tok_ref, w_ref, row_ref, kv_z, n_z, with_q=False, spots=spots, count=1)


def reach(sc, tab, rows):
    count = tab.shape[0] // 3
    min_low, min_high, unused = table_of(tab, count, sc[1])
    max_low, max_high, unused = table_of(tab, count, sc[1] + 2 * rows - 1)
    return min_low, max_high, max_low, min_high


def chip_rows(sc, rows, shape, dim):
    spot = lax.broadcasted_iota(I32, shape, dim) + sc[0] * rows
    return sc[1] + jnp.where(spot >= 2 * rows, spot - 2 * rows, spot)


def attend_body(sc, tab, q_own, q_other, *refs, kv_units):
    kv_refs, (keep_ref, send_ref, q_scr, s_scr, m_scr, acc_scr, kv_ref, sem) = refs[:-8], refs[-8:]
    count = tab.shape[0] // 3
    units, unused, rows, unused = kv_ref.shape
    k = 0
    for ref in kv_refs:
        for i in range(ref.shape[0]):
            pltpu.make_async_copy(ref.at[i], kv_ref.at[kv_units[k]], sem.at[kv_units[k]]).start()
            k += 1
    min_low, max_high, max_low, min_high = reach(sc, tab, rows)
    q_pos = chip_rows(sc, rows, (2 * rows, 1), 0)
    low, high, unused = table_of(tab, count, q_pos)
    ones = jnp.ones((rows, HEAD_DIM), BF)
    q_scr[:, :rows] = q_own[...]
    q_scr[:, rows:] = q_other[...]
    m_scr[...] = jnp.full(m_scr.shape, NEG, F32)
    acc_scr[...] = jnp.zeros(acc_scr.shape, F32)

    def keep_scores(u, allowed):
        for h in range(HEADS):
            scores = mm_nt(q_scr[h], kv_ref[u, h])
            if allowed is not None:
                scores = jnp.where(allowed, scores, NEG)
            s_scr[u, h] = scores
            top = m_scr[h]
            for j in range(rows // HEAD_DIM):
                top = jnp.maximum(top, scores[:, j * HEAD_DIM : (j + 1) * HEAD_DIM])
            m_scr[h] = top

    def score_step(u, carry):
        start = sc[2 + u]

        pltpu.make_async_copy(kv_refs[0].at[0], kv_ref.at[u], sem.at[u]).wait()
        needed = (start < max_high) & (start + rows > min_low)
        whole = (start >= max_low) & (start + rows <= min_high)

        @pl.when(needed & whole)
        def _():
            keep_scores(u, None)

        @pl.when(needed & jnp.logical_not(whole))
        def _():
            k_pos = start + lax.broadcasted_iota(I32, (1, rows), 1)
            keep_scores(u, (k_pos >= low) & (k_pos < high))

        return carry

    lax.fori_loop(0, units, score_step, 0)
    for h in range(HEADS):
        top = jnp.max(m_scr[h], axis=-1, keepdims=True)
        m_scr[h] = jnp.broadcast_to(jnp.where(top > 0.5 * NEG, top, 0.0), m_scr.shape[1:])

    def value_step(u, carry):
        start = sc[2 + u]
        needed = (start < max_high) & (start + rows > min_low)

        @pl.when(needed)
        def _():
            for h in range(HEADS):
                soft = jnp.exp2(s_scr[u, h] - m_scr[h][:, :1]).astype(BF)
                wide = jnp.concatenate([kv_ref[u, HEADS + h], ones], axis=1)
                acc_scr[h] += mm(soft, wide)

        return carry

    lax.fori_loop(0, units, value_step, 0)
    lane = lax.broadcasted_iota(I32, (1, HEAD_DIM), 1)
    width = HEADS * HEAD_DIM
    mine = jnp.zeros((rows, HEAD_DIM), F32)
    theirs = mine
    for h in range(HEADS):
        lanes = slice(h * HEAD_DIM, (h + 1) * HEAD_DIM)
        total = acc_scr[h, :, HEAD_DIM:]
        some = total > 0.0
        mixed = acc_scr[h, :, :HEAD_DIM] / jnp.where(some, total, 1.0)
        log_total = jnp.where(some, m_scr[h] + jnp.log2(jnp.where(some, total, 1.0)), NEG)
        keep_ref[:, lanes] = mixed[:rows]
        send_ref[:, lanes] = mixed[rows:]
        mine = jnp.where(lane == h, log_total[:rows], jnp.where(lane == HEADS + h, log_total[rows:], mine))
        theirs = jnp.where(lane == h, log_total[rows:], jnp.where(lane == HEADS + h, log_total[:rows], theirs))
    keep_ref[:, width:] = mine
    send_ref[:, width:] = theirs


def middle_body(idx, sc, tab, *refs, rows, m_count, grad_count):
    m_refs, (tok_ref, own_ref, other_ref, cot_ref, row_ref, up_row_ref) = refs[:m_count], refs[m_count : m_count + 6]
    outs = refs[m_count + 6 :]
    out_ref, dmid_ref, d_ref, lse_ref, vec_ref = outs[:5]
    g_refs = outs[5 : 5 + grad_count]
    (w_out, w_up, w_down, g_out, g_up, g_down, dh_scr, sem, g_sem) = outs[5 + grad_count :]
    blocks, width = w_up.shape[0], w_up.shape[2]
    pieces = w_down.shape[0] // blocks
    count = tab.shape[0] // 3
    local = tok_ref.shape[0]
    spots = []
    for m_ref in m_refs:
        for spot in range(m_ref.shape[0]):
            owner = idx[len(spots)]
            spots.append(
                (m_ref, spot, pl.ds(pl.multiple_of(owner * rows, rows), rows), pl.ds(owner * blocks, blocks))
            )
    for m_ref, spot, at, unused in spots:
        pltpu.make_async_copy(m_ref.at[spot, 0], w_out.at[at, :], sem.at[0]).start()
    for m_ref, spot, unused, at in spots:
        pltpu.make_async_copy(m_ref.at[spot, pl.ds(1 + blocks, blocks)], w_down.at[at], sem.at[2]).start()
    for m_ref, spot, at, unused in spots:
        pltpu.make_async_copy(m_ref.at[spot, pl.ds(1, blocks)], w_up.at[:, at, :], sem.at[1]).start()

    pos = sc[1] + sc[0] * local + lax.broadcasted_iota(I32, (local, 1), 0)
    unused_low, unused_high, finish = table_of(tab, count, pos)
    live = (pos < finish).astype(F32)
    gain, shift = row_ref[5:6, :], row_ref[6:7, :]
    lane = lax.broadcasted_iota(I32, (1, HEAD_DIM), 1)
    lse_own, lse_other = own_ref[:, width:], other_ref[:, width:]
    top = jnp.maximum(lse_own, lse_other)
    share_own, share_other = jnp.exp2(lse_own - top), jnp.exp2(lse_other - top)
    share = share_own + share_other
    log_total = jnp.transpose(top + jnp.log2(share))
    lse_ref[...] = jnp.concatenate([log_total[:HEADS], log_total[HEADS : 2 * HEADS]], axis=1)
    share_own, share_other = share_own / share, share_other / share
    mixed = []
    for h in range(HEADS):
        lanes = slice(h * HEAD_DIM, (h + 1) * HEAD_DIM)
        mixed.append(own_ref[:, lanes] * share_own[:, h : h + 1] + other_ref[:, lanes] * share_other[:, h : h + 1])
    mixed = jnp.concatenate(mixed, axis=1)
    attended = (mixed * live).astype(BF)
    cot = cot_ref[...]
    pltpu.make_async_copy(w_out, w_out, sem.at[0]).wait()
    middle = tok_ref[...].astype(F32) + mm(attended, w_out[...]) + row_ref[4:5, :]
    pltpu.make_async_copy(w_down, w_down, sem.at[2]).wait()
    for j in range(blocks):
        dh_scr[j] = mm_nt(cot, w_down[j * pieces : (j + 1) * pieces].reshape(width, width))
    plain, inverse = normalize(middle)
    normed = (plain * gain + shift).astype(BF)
    pltpu.make_async_copy(w_up, w_up, sem.at[1]).wait()
    total = middle + row_ref[7:8, :]
    d_norm = jnp.zeros(middle.shape, F32)
    ones = jnp.ones((8, local), BF)
    up_sums = []
    for j in range(blocks):
        up = w_up[j]
        down = w_down[j * pieces : (j + 1) * pieces].reshape(width, width)
        pre = mm(normed, up) + up_row_ref[j : j + 1, :]
        square = pre * pre
        t = jnp.tanh(GELU_A * pre * (1.0 + GELU_B * square))
        half = 0.5 * (1.0 + t)
        hidden = (pre * half).astype(BF)
        slope = half + 0.5 * pre * (1.0 - t * t) * (GELU_A * (1.0 + 3.0 * GELU_B * square))
        total = total + mm(hidden, down)
        d_pre = (dh_scr[j] * slope).astype(BF)
        d_norm = d_norm + mm_nt(d_pre, up)
        g_down[j * pieces : (j + 1) * pieces] = mm_tn(hidden, cot).astype(BF).reshape(pieces, rows, width)
        g_up[j] = mm_tn(normed, d_pre).astype(BF)
        up_sums.append(mm(ones, d_pre)[0:1])
    g_pieces = g_refs[0].shape[0]
    spots = []
    for i in range(pieces):
        g_ref, spot, where = g_refs[i // g_pieces], i % g_pieces, idx[pieces + i]
        spots.append((g_ref, spot, pl.ds(pl.multiple_of(where * rows, rows), rows)))
        at = pl.ds(where * blocks, blocks)
        pltpu.make_async_copy(g_down.at[at], g_ref.at[spot, pl.ds(1 + blocks, blocks)], g_sem).start()
    for g_ref, spot, at in spots:
        pltpu.make_async_copy(g_up.at[:, at, :], g_ref.at[spot, pl.ds(1, blocks)], g_sem).start()
    out_ref[...] = total.astype(BF)
    cot_f = cot.astype(F32)
    d_middle = cot_f + norm_back(d_norm, plain, inverse, gain)
    dmid_ref[...] = d_middle
    d_branch = d_middle.astype(BF)
    g_out[...] = mm_tn(attended, d_branch).astype(BF)
    for g_ref, spot, at in spots:
        pltpu.make_async_copy(g_out.at[at, :], g_ref.at[spot, 0], g_sem).start()
    d_att = mm_nt(d_branch, w_out[...]).astype(BF) * live.astype(BF)
    d_ref[:, :width] = d_att
    product = d_att.astype(F32) * mixed
    tail = jnp.zeros((local, HEAD_DIM), F32)
    for h in range(HEADS):
        delta = jnp.sum(product[:, h * HEAD_DIM : (h + 1) * HEAD_DIM], axis=-1, keepdims=True)
        high = delta.astype(BF).astype(F32)
        tail = jnp.where(lane == h, high, jnp.where(lane == HEADS + h, delta - high, tail))
    d_ref[:, width:] = tail.astype(BF)

    sums = [jnp.sum(v, axis=0, keepdims=True) for v in (d_middle, d_norm * plain, d_norm, cot_f)]
    sums = jnp.concatenate(sums + up_sums + [jnp.zeros((HEAD_DIM - 4 - blocks, width), F32)], axis=0)
    columns = jnp.transpose(sums)
    if pieces > 1:
        per = pieces // blocks
        vec_ref[...] = jnp.where(lane < 4, columns, 0.0)
        for j in range(blocks):
            column = jnp.broadcast_to(columns[:, 4 + j : 5 + j], (width, HEAD_DIM)).reshape(
                per, blocks, rows, HEAD_DIM
            )
            wide_lane = lane.reshape(1, 1, HEAD_DIM)
            placed = sum(jnp.where(wide_lane == 4 + i, column[:, i], 0.0) for i in range(blocks))
            vec_ref[j * per * rows : (j + 1) * per * rows, :] += placed.reshape(per * rows, HEAD_DIM)
    else:
        vec_ref[...] = jnp.where(lane < 4 + blocks, columns, 0.0)
    for g_ref in g_refs:
        pltpu.make_async_copy(g_ref, g_ref, g_sem).wait()


def back_body(
    sc, tab, q_ref, do_ref, delta_ref, lse_ref, kv_near, kv_far, n_near, n_far, w_ref, own_in, other_in, nk_in, sum_in,
    keep_ref, send_ref, own_ref, other_ref, nk_ref, sum_ref, dkv_scr, *, plane, spots,
):
    count = tab.shape[0] // 3
    unused, unused, rows, unused = kv_near.shape
    width = w_ref.shape[1]
    min_low, max_high, max_low, min_high = reach(sc, tab, rows)
    q_pos = chip_rows(sc, rows, (1, 2 * rows), 1)
    low, high, unused = table_of(tab, count, q_pos)
    if own_in is None:
        own_ref[...] = jnp.zeros(own_ref.shape, F32)
        other_ref[...] = jnp.zeros(other_ref.shape, F32)
    else:
        own_ref[...] = own_in[...]
        other_ref[...] = other_in[...]

    def unit(u, allowed):
        for h in range(HEADS):
            lanes = slice(h * HEAD_DIM, (h + 1) * HEAD_DIM)
            v_lanes = slice(width + h * HEAD_DIM, width + (h + 1) * HEAD_DIM)
            kv_ref, spot = (kv_near, kv_far)[u], spots[u]
            q, do, key = q_ref[h], do_ref[h], kv_ref[spot, h]
            soft = jnp.exp2(mm_nt(key, q) - lse_ref[h : h + 1, :])
            if allowed is not None:
                soft = jnp.where(allowed, soft, 0.0)
            d_soft = mm_nt(kv_ref[spot, HEADS + h], do)
            d_scores = (soft * (d_soft - delta_ref[h : h + 1, :])).astype(BF)
            dkv_scr[u, :, v_lanes] = mm(soft.astype(BF), do).astype(BF)
            dkv_scr[u, :, lanes] = (mm(d_scores, q) * (SCALE / SCALE2)).astype(BF)
            d_query = mm_tn(key, d_scores)
            own_ref[h] += d_query[:, :rows]
            other_ref[h] += d_query[:, rows:]

    for u in range(2):
        start = sc[2 + 2 * plane + u]
        needed = (start < max_high) & (start + rows > min_low)
        whole = (start >= max_low) & (start + rows <= min_high)

        @pl.when(needed & whole)
        def _(u=u):
            unit(u, None)

        @pl.when(needed & jnp.logical_not(whole))
        def _(u=u, start=start):
            k_pos = start + lax.broadcasted_iota(I32, (rows, 1), 0)
            unit(u, (k_pos >= low) & (k_pos < high))

        @pl.when(jnp.logical_not(needed))
        def _(u=u):
            dkv_scr[u] = jnp.zeros(dkv_scr.shape[1:], BF)

    ones = jnp.ones((8, rows), BF)
    for u, ref in enumerate((keep_ref, send_ref)):
        ref[...] = (mm_nt(dkv_scr[u, :, :width], w_ref[1]) + mm_nt(dkv_scr[u, :, width:], w_ref[2])).astype(BF)
    product = mm_tn(n_near[spots[0]], dkv_scr[0]) + mm_tn(n_far[spots[1]], dkv_scr[1])
    sums = mm(ones, dkv_scr[0]) + mm(ones, dkv_scr[1])
    nk_ref[...] = product if nk_in is None else nk_in[...] + product
    sum_ref[...] = sums if sum_in is None else sum_in[...] + sums


def first_back_body(sc, tab, q_ref, d_own, d_other, *refs, **options):
    ins, outs, do_ref, delta_ref, dkv_scr = refs[:6], refs[6:-3], refs[-3], refs[-2], refs[-1]
    rows, width = d_own.shape[0], HEADS * HEAD_DIM
    for i, ref in enumerate((d_own, d_other)):
        for h in range(HEADS):
            do_ref[h, i * rows : (i + 1) * rows] = ref[:, h * HEAD_DIM : (h + 1) * HEAD_DIM]
        tail = jnp.transpose(ref[:, width:].astype(F32))
        delta_ref[:, i * rows : (i + 1) * rows] = tail[:HEADS] + tail[HEADS : 2 * HEADS]
    nothing = [None] * 4
    back_body(sc, tab, q_ref, do_ref, delta_ref, *ins, *nothing, *outs, dkv_scr, **options)


def message_body(idx, n_own, n_other, dq_own, dq_other, nk_ref, sum_ref, w_ref, col_ref, vec_ref, *refs, rows):
    msg_refs, (full, vec) = refs[:-2], refs[-2:]
    local = n_own.shape[1]
    width = w_ref.shape[1]
    q_product = jnp.zeros((width, width), F32)
    q_sums = jnp.zeros((8, width), F32)
    ones = jnp.ones((8, local), BF)
    for n_ref, dq_ref in ((n_own, dq_own), (n_other, dq_other)):
        d_query = jnp.concatenate([dq_ref[h] * SCALE for h in range(HEADS)], axis=0).astype(BF)
        q_product += lax.dot_general(n_ref[0], d_query, (((0,), (1,)), ((), ())), preferred_element_type=F32)
        q_sums += mm_nt(ones, d_query)
    gain, shift = col_ref[:, 0:1], col_ref[:, 1:2]
    lane = lax.broadcasted_iota(I32, (1, HEAD_DIM), 1)
    gain_grad = jnp.zeros((width, 1), F32)
    shift_grad = jnp.zeros((width, 1), F32)
    columns = []
    for i in range(3):
        lanes = slice(i * width, (i + 1) * width)
        if i == 0:
            product, sums = q_product, q_sums[0:1]
        else:
            at = slice((i - 1) * width, i * width)
            product, sums = nk_ref[:, at], sum_ref[0:1, at]
        weight = w_ref[i].astype(F32)
        full[:, lanes] = (product * gain + shift * sums).astype(BF)
        gain_grad += jnp.sum(product * weight, axis=-1, keepdims=True)
        shift_grad += jnp.sum(weight * sums, axis=-1, keepdims=True)
        if i != 1:
            columns.append(jnp.transpose(jnp.broadcast_to(sums, (HEAD_DIM, width))))
    vec[...] = vec_ref[...]
    for at, column in ((8, gain_grad), (9, shift_grad), (10, columns[0]), (11, columns[1])):
        vec[...] += jnp.where(lane == at, column, 0.0)
    full[:, 3 * width :] = vec[...].astype(BF)
    k = 0
    for msg_ref in msg_refs:
        for i in range(msg_ref.shape[0]):
            msg_ref[i] = full[pl.ds(pl.multiple_of(idx[k] * rows, rows), rows), :]
            k += 1


def query_body(dq_own, dq_other, w_ref, keep_ref, send_ref):
    for dq_ref, out_ref in ((dq_own, keep_ref), (dq_other, send_ref)):
        d_query = jnp.concatenate([dq_ref[h] * SCALE for h in range(HEADS)], axis=0).astype(BF)
        out = lax.dot_general(d_query, w_ref[0], (((0,), (1,)), ((), ())), preferred_element_type=F32)
        out_ref[...] = out.astype(BF)


def finish_body(tok_ref, dmid_ref, row_ref, *refs):
    plain, inverse = normalize(tok_ref[...].astype(F32))
    total = refs[0][...].astype(F32)
    for ref in refs[1:-1]:
        total = total + ref[...].astype(F32)
    refs[-1][...] = (dmid_ref[...] + norm_back(total, plain, inverse, row_ref[0:1, :])).astype(BF)


def matrices_body(*refs):
    terms, (out_ref, up_ref, down_ref) = refs[:-3], refs[-3:]
    width = out_ref.shape[1]
    part = out_ref.shape[0]
    blocks = up_ref.shape[1] // width

    def block(i):
        total = terms[0][i].astype(F32)
        for term in terms[1:]:
            total = total + term[i].astype(F32)
        return total

    out_ref[...] = block(0)
    for j in range(blocks):
        up_ref[:, j * width : (j + 1) * width] = block(1 + j)
        down_ref[j * part : (j + 1) * part, :] = block(1 + blocks + j)


def unpack_body(*refs):
    terms, (qkv_ref, *vec_refs, up_ref, pad_ref) = refs[:-11], refs[-11:]
    total = terms[0][...]
    for term in terms[1:]:
        total = total + term[...].astype(F32)
    width = qkv_ref.shape[1]
    part = qkv_ref.shape[0]
    qkv_ref[...] = total[:, :width]
    pad_ref[...] = jnp.zeros(pad_ref.shape, F32)
    pad_ref[:part] = total[:, width:]
    rows = jnp.transpose(pad_ref[...])
    for ref, row in zip(vec_refs, (8, 9, 10, 11, 0, 1, 2, 3), strict=True):
        ref[...] = rows[row : row + 1, :part]
    up_ref[...] = rows[4 : 4 + up_ref.shape[0], :part]


def shards(
    tokens, w_qkv, w_out, w_up, w_down,
    norm1_gain, norm1_bias, query_bias, value_bias, out_bias, norm2_gain, norm2_bias, up_bias, down_bias,
    cotangent, table_start, support_count, query_count, *, R, F,
):
    A = R // PLANE
    count = R * F
    local, width = tokens.shape[1], tokens.shape[2]
    part = w_qkv.shape[0]
    hidden = w_up.shape[1]
    blocks = hidden // width
    aligned = part % 16 == 0
    rows = part if aligned else width
    pieces = count if aligned else 1
    sds = jax.ShapeDtypeStruct

    r, f = lax.axis_index("rows"), lax.axis_index("fsdp")
    a, x, c = r // PLANE, (r // 2) % 2, r % 2

    def swap_c(v):
        return lax.ppermute(v, "rows", [(i, i ^ 1) for i in range(R)])

    def swap_x(v):
        return lax.ppermute(v, "rows", [(i, i ^ 2) for i in range(R)])

    def turn_a(v, s):
        return lax.ppermute(
            v, "rows", [(i, ((i // PLANE + s) % A) * PLANE + i % PLANE) for i in range(R)]
        )

    def turn_f(v, t):
        return lax.ppermute(v, "fsdp", [(i, (i + t) % F) for i in range(F)])

    def turn_xf(v, t):
        return lax.ppermute(
            v, ("rows", "fsdp"),
            [(i * F + j, (i ^ 2) * F + (j + t) % F) for i in range(R) for j in range(F)],
        )

    def owners(order):
        cr, t, xr, s = (np.array(list(z), np.int32) for z in zip(*order, strict=True))
        plane = lax.rem(a - s + A, A)
        return (((plane * 2 + (x ^ xr)) * 2 + (c ^ cr)) * F + lax.rem(f - t + F, F)).astype(I32)

    unit_s = np.repeat(np.arange(A), 2).astype(np.int32)
    unit_x = np.tile(np.arange(2), A).astype(np.int32)
    unit_start = (lax.rem(a - unit_s + A, A) * 2 + (x ^ unit_x)) * (2 * local) + c * local
    sc = jnp.concatenate([jnp.stack([c, (a * 2 + x) * 2 * local]), unit_start]).astype(I32)
    tab = jnp.concatenate([table_start[0], support_count[0], query_count[0]])
    q_order = [(cr, t, xr, s) for cr in range(2) for t in range(F) for xr in range(2) for s in range(A)]
    parts = [slice(0, A // 2), slice(A // 2, A)]
    m_order = [(cr, 0, xr, s) for xr in range(2) for cr in range(2) for s in range(A)]
    m_order += [(cr, t, 0, s) for cr in range(2) for t in range(1, F) for s in range(A)]
    m_order += [
        (cr, t, 1, s) for cr in range(2) for half in parts for t in range(1, F) for s in list(range(A))[half]
    ]
    every_owner = owners(q_order + m_order)
    q_owner, m_owner = every_owner[:count], every_owner[count:]
    if aligned:
        q_idx, idx = q_owner, jnp.concatenate([m_owner, q_owner])
    else:
        q_idx, idx = jnp.zeros((1,), I32), jnp.zeros((2,), I32)

    near = list(range(1, A))
    early, late = near[:2], near[2:]
    own = tokens[0]
    vectors = [
        v.reshape(1, -1)
        for v in (
            norm1_gain, norm1_bias, query_bias, value_bias, out_bias, norm2_gain, norm2_bias, down_bias, up_bias
        )
    ]
    wide = 3 * width + HEAD_DIM
    pack_in = [w_qkv, w_out, w_up, w_down, *vectors]
    q_own, m_own = pl.pallas_call(
        pack_body,
        grid=(1,),
        out_shape=[sds((4, part, width), BF), sds((1 + 2 * blocks, part, width), BF)],
        in_specs=[pl.BlockSpec(v.shape, lambda i: (0, 0)) for v in pack_in],
        out_specs=[VMEM] * 2,
        scratch_shapes=[pltpu.VMEM((HEAD_DIM, HEAD_DIM), F32)],
        compiler_params=pltpu.CompilerParams(vmem_limit_bytes=56 * MIB),
        cost_estimate=pl.CostEstimate(flops=0, bytes_accessed=16 * part * width, transcendentals=0),
        name="pack",
    )(*pack_in)
    *q_z, own_x, tok_first, sc, tab, q_idx, idx = together(
        *(turn_a(q_own, s) for s in range(1, A)), swap_x(own), turn_a(own, 1), sc, tab, q_idx, idx
    )
    q_z = jnp.stack([q_own] + q_z)
    tok_z, m_z = {1: tok_first}, {0: m_own}
    moved = [swap_x(q_z)] + [v for t in range(1, F) for v in (turn_f(q_z, t), turn_xf(q_z, t))]
    *q_far, tok_z[2], m_z[1] = together(*moved, turn_a(tok_z[1], 1), turn_a(after(m_own, tok_first), 1))
    tok_early = jnp.stack([tok_z[s] for s in early])
    x_early = swap_x(tok_early)
    tok_z[3], m_z[2] = turn_a(tok_z[2], 1), turn_a(m_z[1], 1)
    q_four = jnp.stack([q_z] + q_far)
    q_other = swap_c(q_four)
    q_pieces = [q_four.reshape(count // 2, 4, part, width), q_other.reshape(count // 2, 4, part, width)]
    if not aligned:
        stacked = jnp.concatenate(q_pieces)
        by_owner = jnp.zeros_like(stacked).at[q_owner].set(stacked)
        q_pieces = [by_owner.transpose(1, 0, 2, 3).reshape(1, 4, width, width)]
    key_shape = (2 * HEADS, local, HEAD_DIM)
    w_all, row_vec, col_vec, up_row, kv_own, n_own, q, kv_z, n_z, n_first = call(
        functools.partial(ready_body, rows=rows, count=len(q_pieces), part=part),
        [
            sds((3, width, width), BF), sds((16, width), F32), sds((width, HEAD_DIM), F32), sds((blocks, width), F32),
            sds((2,) + key_shape, BF), sds((2, local, width), BF), sds((HEADS, local, HEAD_DIM), BF),
            sds((2,) + key_shape, BF), sds((2, local, width), BF), sds((1, local, width), BF),
        ],
        [q_idx, *q_pieces, own, own_x, tok_early], [SMEM] + [HBM] * len(q_pieces) + [VMEM] * 3, [VMEM] * 10,
        scratch=[pltpu.VMEM((width, HEAD_DIM), BF), pltpu.SemaphoreType.DMA((2,))],
        flops=4 * (A + 1) * local * width * width, moved=4 * width * wide, vmem=12, name="ready",
    )

    q_other, n_other = swap_c(q), swap_c(n_first)
    tok_z[3], m_z[2], x_early, kv_z = together(tok_z[3], m_z[2], x_early, kv_z)
    for s in range(4, A):
        tok_z[s], m_z[s - 1] = together(turn_a(tok_z[s - 1], 1), turn_a(m_z[s - 2], 1))
    tok_late = tok_z[3][None] if A == 4 else jnp.stack([tok_z[s] for s in late])
    x_late, m_z[A - 1] = together(swap_x(tok_late), turn_a(m_z[A - 2], 1))
    m_z = stack([m_z[s] for s in range(A)])
    m_x, m_f = swap_x(m_z), [turn_f(m_z, t) for t in range(1, F)]
    m_c = swap_c(m_z)
    spots = [(0, i) for i in range(A - 3)] + [(1, i) for i in range(2)] + [(2, i) for i in range(A - 3)]
    kv_x, n_x = call(
        functools.partial(project_body, with_q=False, spots=spots, count=3),
        [sds((len(spots),) + key_shape, BF), sds((len(spots), local, width), BF)],
        [tok_late, x_early, after(x_late, m_z), w_all, row_vec], [VMEM] * 5, [VMEM] * 2,
        flops=4 * len(spots) * local * width * width, moved=8 * len(spots) * local * width, vmem=8, name="project",
    )
    where = {0: ((kv_own, kv_own, 0, 1), (n_own, n_own, 0, 1))}
    for i, s in enumerate(early):
        where[s] = ((kv_z, kv_x, i, A - 3 + i), (n_z, n_x, i, A - 3 + i))
    for i, s in enumerate(late):
        where[s] = ((kv_x, kv_x, i, A - 1 + i), (n_x, n_x, i, A - 1 + i))
    kv_pieces = [kv_own, kv_z, kv_x]
    kv_units = [0, 1] + [2 * s for s in near] + [2 * s + 1 for s in near]

    unit = 2 * local
    work = 4 * unit * A * unit * width
    packet = width + HEAD_DIM
    att_keep, att_send, q_chip = call(
        functools.partial(attend_body, kv_units=kv_units),
        [sds((local, packet), F32)] * 2 + [sds((HEADS, unit, HEAD_DIM), BF)],
        [sc, tab, q, q_other, *kv_pieces], [SMEM, SMEM, VMEM, VMEM] + [ANY] * 3, [VMEM] * 3,
        scratch=[
            pltpu.VMEM((2 * A, HEADS, unit, local), F32),
            pltpu.VMEM((HEADS, unit, HEAD_DIM), F32), pltpu.VMEM((HEADS, unit, 2 * HEAD_DIM), F32),
            pltpu.VMEM((2 * A, 2 * HEADS, local, HEAD_DIM), BF), pltpu.SemaphoreType.DMA((2 * A,)),
        ],
        flops=work, moved=8 * A * unit * width, trans=HEADS * unit * A * unit, vmem=4 + 6 * A, name="attend",
    )
    att_keep, att_send, m_x, m_c, *m_f = together(att_keep, att_send, m_x, m_c, *m_f)
    half_shape = (A // 2,) + m_z.shape[1:]
    halves = copy_out(
        [m_x, *m_f], [half_shape] * F, [(0, (parts[0],), 0, ())] + [(t, (parts[1],), t, ()) for t in range(1, F)]
    )
    crossed = [turn_f(halves[0], t) for t in range(1, F)] + [swap_x(v) for v in halves[1:]]
    att_other, *crossed = together(swap_c(att_send), *crossed)
    m_arrays = [m_z, m_c, m_x, swap_c(m_x), *m_f, *(swap_c(v) for v in m_f), *crossed, *(swap_c(v) for v in crossed)]
    if not aligned:
        stacked = jnp.concatenate(m_arrays)
        by_owner = jnp.zeros_like(stacked).at[m_owner].set(stacked)
        m_arrays = [
            jnp.concatenate(
                [
                    by_owner[:, 0].reshape(1, width, width),
                    by_owner[:, 1 : 1 + blocks].transpose(1, 0, 2, 3).reshape(blocks, width, width),
                    by_owner[:, 1 + blocks :].reshape(blocks, width, width),
                ]
            )[None]
        ]

    spots = [(t, xr) for t in range(F) for xr in range(2)]
    grad_count = 4 * F if aligned else 1
    g_shape = sds((pieces // grad_count, 1 + 2 * blocks, rows, width), BF)
    got = call(
        functools.partial(middle_body, rows=rows, m_count=len(m_arrays), grad_count=grad_count),
        [
            sds((local, width), BF), sds((local, width), F32), sds((local, packet), BF), sds((HEADS, unit), F32),
            sds((width, HEAD_DIM), F32),
        ] + [g_shape] * grad_count,
        [idx, sc, tab, *m_arrays, own, att_keep, att_other, cotangent[0], row_vec, up_row],
        [SMEM] * 3 + [HBM] * len(m_arrays) + [VMEM] * 6,
        [VMEM] * 5 + [HBM] * grad_count,
        scratch=[
            pltpu.VMEM((width, width), BF), pltpu.VMEM((blocks, width, width), BF),
            pltpu.VMEM((pieces * blocks, rows, width), BF),
            pltpu.VMEM((width, width), BF), pltpu.VMEM((blocks, width, width), BF),
            pltpu.VMEM((pieces * blocks, rows, width), BF), pltpu.VMEM((blocks, local, width), F32),
            pltpu.SemaphoreType.DMA((3,)), pltpu.SemaphoreType.DMA,
        ],
        flops=6 * local * width * width * (1 + 2 * blocks), moved=4 * width * width * (1 + 2 * blocks),
        trans=local * hidden, vmem=50, name="middle",
    )
    outputs, d_middle, d_own, lse, vec = got[:5]
    grads = got[5:]
    d_other = swap_c(d_own)

    lead = (A, 1 + 2 * blocks, part, width)
    if aligned:
        relative = [g.reshape(lead) for g in grads]
    else:
        whole = grads[0][0]
        by_owner = jnp.concatenate(
            [
                whole[0].reshape(count, 1, part, width),
                whole[1 : 1 + blocks].reshape(blocks, count, part, width).transpose(1, 0, 2, 3),
                whole[1 + blocks :].reshape(count, blocks, part, width),
            ],
            axis=1,
        )
        by_owner = by_owner[q_owner].reshape((4 * F,) + lead)
        relative = [by_owner[i] for i in range(4 * F)]
    g_near = {spot: relative[i] for i, spot in enumerate(spots)}
    g_far = {spot: swap_c(after(relative[2 * F + i], d_other)) for i, spot in reversed(list(enumerate(spots)))}

    def through_f(xr, half):
        return [
            turn_f(add_up([g_near[t, xr], g_far[t, xr]], [[(0, (half,)), (1, (half,))]])[0], F - t)
            for t in range(1, F)
        ]

    def g_kept(xr, half):
        arrays = [g_near[0, xr], g_far[0, xr], *g_y[xr, half]]
        return arrays, [(0, (half,)), (1, (half,))] + [(2 + i, ()) for i in range(F - 1)]

    carried, d_all = [], []
    d_x, d_z, d_keep, d_send = {}, {}, {}, {}
    g_y, g_x = {}, {}
    back_order = near + [0]
    q_now = q_chip
    steps = len(back_order)
    y_parts = [(xr, half) for xr in (1, 0) for half in parts]
    for step, s in enumerate(back_order):
        kv_at, n_at = where[s]
        if step:
            ins = [sc, tab, q_now, *d_all, lse, *kv_at[:2], *n_at[:2], w_all, *carried]
            body = back_body
        else:
            ins = [sc, tab, q_now, d_own, d_other, lse, *kv_at[:2], *n_at[:2], w_all]
            body = first_back_body
        dq_shape = sds((HEADS, HEAD_DIM, local), F32)
        shapes = [
            sds((local, width), BF), sds((local, width), BF), dq_shape, dq_shape,
            sds((width, 2 * width), F32), sds((8, 2 * width), F32),
        ]
        if not step:
            shapes += [sds((HEADS, unit, HEAD_DIM), BF), sds((HEADS, unit), F32)]
        outs = call(
            functools.partial(body, plane=s, spots=kv_at[2:]), shapes, ins,
            [SMEM, SMEM] + [VMEM] * (len(ins) - 2), [VMEM] * len(shapes),
            scratch=[pltpu.VMEM((2, local, 2 * width), BF)],
            flops=work // A * 5 // 2 + 8 * unit * width * width, moved=16 * unit * width,
            trans=HEADS * unit * unit, name="back",
        )
        if step == 0:
            keys = list(g_far)
            got = together(*outs, *(g_far[k] for k in keys))
            outs, d_all = got[:6], got[6:8]
            g_far = dict(zip(keys, got[8:], strict=True))
        else:
            prev = back_order[step - 1]
            beside = {("x", prev): swap_x(d_send[prev])}
            if step >= 2:
                beside["z", step] = turn_a(d_sum, 1)
            if step - 1 < len(y_parts):
                for i, v in enumerate(through_f(y_parts[step - 1][0], y_parts[step - 1][1])):
                    beside["y", step - 1, i] = v
            keys = list(beside)
            got = together(*outs, *beside.values())
            outs = got[:6]
            beside = dict(zip(keys, got[6:], strict=True))
            for key, v in beside.items():
                if key[0] == "x":
                    d_x[key[1]] = v
                elif key[0] == "z":
                    d_z[key[1]] = v
                else:
                    g_y[y_parts[key[1]]] = g_y.get(y_parts[key[1]], []) + [v]
            arrived = [d_keep[prev], d_x[prev]] + ([d_z[step]] if step in d_z else [])
            (d_sum,) = add_up(arrived, [[(i, ()) for i in range(len(arrived))]])
        d_keep[s], d_send[s], *carried = outs
        q_now = after(q_chip, outs[2])
        if step:
            q_now = after(q_now, d_sum)

    for k in range(steps - 1, len(y_parts)):
        g_y[y_parts[k]] = through_f(*y_parts[k])
    d_last = turn_a(d_sum, 1)
    dq_own, dq_other, n_product, sums = carried

    half_count = 2 * F
    msg_lead = (A, part, wide)
    msg_shape = [sds((pieces // 2, rows, wide), BF)] * 2 if aligned else [sds((1, rows, wide), BF)]
    message = call(
        functools.partial(message_body, rows=rows),
        msg_shape,
        [q_idx, n_own, n_other, dq_own, dq_other, n_product, sums, w_all, col_vec, vec],
        [SMEM] + [VMEM] * 9, [VMEM] * len(msg_shape),
        scratch=[pltpu.VMEM((width, wide), BF), pltpu.VMEM((width, HEAD_DIM), F32)],
        flops=2 * local * width * width, moved=8 * width * wide, vmem=8, name="message",
    )
    if not aligned:
        flat = message[0][0]
        at = slice(3 * width + 4, 3 * width + 4 + blocks)
        up_part = flat[:, at].T.reshape(count, blocks, part)
        by_owner = flat.reshape(count, part, wide)
        by_owner = by_owner.at[:, :, at].set(up_part.transpose(0, 2, 1))
        by_owner = by_owner[q_owner]
        message = [by_owner[: count // 2], by_owner[count // 2 :]]
    w_far = swap_c(message[1])
    arrays = [g_near[0, 1], g_far[0, 1], *g_y[1, parts[0]], *g_y[1, parts[1]]]
    lows = [(0, (parts[0],)), (1, (parts[0],))] + [(2 + i, ()) for i in range(F - 1)]
    highs = [(0, (parts[1],)), (1, (parts[1],))] + [(1 + F + i, ()) for i in range(F - 1)]
    (g_x_send,) = join_up(arrays, [lows, highs])
    g_x_all = swap_x(g_x_send)
    w_far = w_far.reshape((half_count,) + msg_lead)
    w_near = message[0].reshape((half_count,) + msg_lead)
    w_both = add_up([w_near, w_far], [[(0, (i,)), (1, (i,))] for i in range(half_count)])
    got = []
    for (t, xr), sent in zip(spots, w_both, strict=True):
        if xr:
            sent = turn_xf(sent, F - t) if t else swap_x(sent)
        elif t:
            sent = turn_f(sent, F - t)
        got.append(sent)
    got[0], d_last = together(got[0], d_last)
    d_x[0] = swap_x(after(d_send[0], got[0]))
    w_z = add_up(got, [[(i, (s,)) for i in range(len(got))] for s in near])
    (w_own,) = add_up(got, [[(i, (0,)) for i in range(len(got))]], F32)
    w_z = [turn_a(v, A - s) for s, v in zip(near, w_z, strict=True)]
    grad_qkv, *vector_grads, up_grad = call(
        unpack_body, [sds((part, 3 * width), F32)] + [sds((1, part), F32)] * 8 + [sds((blocks, part), F32)],
        [w_own, *w_z], [VMEM] * A, [VMEM] * 10, scratch=[pltpu.VMEM((HEAD_DIM, HEAD_DIM), F32)], moved=16 * part * width, vmem=8, name="unpack",
    )

    g_z_send, g_mine = {}, None
    for half in parts:
        arrays, terms = g_kept(0, half)
        arrays.append(g_x_all)
        planes = list(range(A))[half]

        def one(s, terms=terms, start=half.start, last=len(arrays) - 1):
            out = [(i, (start + s,) if spot else (s,)) for i, spot in terms]
            return out + [(last, (start + s,))]

        for s, v in zip(planes, add_up(arrays, [one(s - half.start) for s in planes]), strict=True):
            if s:
                g_z_send[s] = v
            else:
                g_mine = v
    g_z_send = [g_z_send[s] for s in near]
    g_z = [turn_a(v, A - s) for s, v in zip(near, g_z_send, strict=True)]
    grad_out, grad_up, grad_down = call(
        matrices_body,
        [sds((part, width), F32), sds((part, hidden), F32), sds((blocks * part, width), F32)],
        [g_mine, *g_z], [VMEM] * A, [VMEM] * 3, moved=6 * A * g_mine.size, vmem=8, name="matrices",
    )
    query_keep, query_send = call(
        query_body, [sds((local, width), BF)] * 2, [after(dq_own, got[0]), dq_other, w_all], [VMEM] * 3, [VMEM] * 2,
        flops=4 * local * width * width, moved=4 * local * width, vmem=8, name="query",
    )
    grad_tokens = call(
        finish_body, sds((local, width), BF),
        [own, d_middle, row_vec, query_keep, swap_c(query_send), d_keep[0], d_x[0], d_last],
        [VMEM] * 8, VMEM, flops=20 * local * width, moved=16 * local * width, vmem=8, name="finish",
    )
    return (
        outputs[None],
        grad_tokens[None],
        grad_qkv,
        grad_out,
        grad_up,
        grad_down,
        *(v.reshape(part) for v in vector_grads[:7]),
        up_grad.reshape(blocks * part),
        vector_grads[7].reshape(part),
    )


def solution(mesh):
    both = ("rows", "fsdp")
    matrix, vector, act, table = P(both, None), P(both), P("fsdp", "rows", None), P("fsdp", None)
    return jax.shard_map(
        functools.partial(shards, R=mesh.shape["rows"], F=mesh.shape["fsdp"]),
        mesh=mesh,
        in_specs=(act,) + (matrix,) * 4 + (vector,) * 9 + (act,) + (table,) * 3,
        out_specs=(act, act) + (matrix,) * 4 + (vector,) * 9,
        check_vma=False,
    )
```

profile of v0, /device:TPU:0, one launch (start us, length us, event | category | flops | bytes accessed | tf_op | source)
XLA Modules:
  0.0 183.0 jit_solution(18119389857464727060)
XLA Ops:
  0.7 1.8 pack.1
  2.5 3.0 %collective-permute-start = (bf16[4,16,512]{2,1,0:T(8,128)(2,1)}, bf16[4,16,512]{2,1,0:T(8,128)(2,1)S(1)}, u32[]{:S(2)}, u32[]{:S(2)}) collective-permute-start(bf16[4,16,512]{2,1,0:T(8,128)(2,1)} %get-tuple-element.182), channel_id=1, source_target_pairs={{0,8},{2,10},{4,12},{6,14},{8,16},{10,18},{12,20},{14,22},{16,24},... | collective-permute-start | bytes 196616 | tf_op jit(solution)/shard_map/ppermute | solution.py:646
  5.5 2.6 %collective-permute-start.1 = (bf16[4,16,512]{2,1,0:T(8,128)(2,1)}, bf16[4,16,512]{2,1,0:T(8,128)(2,1)S(1)}, u32[]{:S(2)}, u32[]{:S(2)}) collective-permute-start(bf16[4,16,512]{2,1,0:T(8,128)(2,1)} %get-tuple-element.182), channel_id=1, source_target_pairs={{0,16},{2,18},{4,20},{6,22},{8,24},{10,26},{12,28},{14,30},{16,0},... | collective-permute-start | bytes 196616 | tf_op jit(solution)/shard_map/ppermute | solution.py:646
  8.1 1.3 collective-permute-start.2
  9.4 1.5 collective-permute-start.3
  11.6 0.7 fusion.7
  13.2 0.8 pad_add_fusion.1.tab
  14.0 2.8 %collective-permute-done.3.refs_3_ = bf16[256,512]{1,0:T(8,128)(2,1)S(1)} collective-permute-done((bf16[256,512]{1,0:T(8,128)(2,1)}, bf16[256,512]{1,0:T(8,128)(2,1)S(1)}, u32[]{:S(2)}, u32[]{:S(2)}) %collective-permute-start.3) | collective-permute-done | bytes 262176 | tf_op jit(solution)/shard_map/ppermute | solution.py:643
  16.9 3.0 %collective-permute-done.4 = bf16[256,512]{1,0:T(8,128)(2,1)S(1)} collective-permute-done((bf16[256,512]{1,0:T(8,128)(2,1)}, bf16[256,512]{1,0:T(8,128)(2,1)S(1)}, u32[]{:S(2)}, u32[]{:S(2)}) %collective-permute-start.4) | collective-permute-done | bytes 262176 | tf_op jit(solution)/shard_map/ppermute | solution.py:646
  19.9 0.9 fusion.12
  21.5 1.5 collective-permute-start.6
  23.0 1.3 collective-permute-start.7
  24.3 1.5 collective-permute-start.9
  25.8 8.7 %collective-permute-done.9.refs_1_ = bf16[9,16,512]{2,1,0:T(8,128)(2,1)S(1)} collective-permute-done((bf16[9,16,512]{2,1,0:T(8,128)(2,1)}, bf16[9,16,512]{2,1,0:T(8,128)(2,1)S(1)}, u32[]{:S(2)}, u32[]{:S(2)}) %collective-permute-start.9) | collective-permute-done | bytes 147488 | tf_op jit(solution)/shard_map/ppermute | solution.py:646
  34.7 0.9 collective-permute-start.12
  35.7 1.8 collective-permute-start.10
  37.5 0.8 collective-permute-start.11
  38.3 3.3 %ready.1 = (bf16[3,512,512]{2,1,0:T(8,128)(2,1)S(1)}, f32[16,512]{1,0:T(8,128)S(1)}, f32[512,128]{1,0:T(8,128)S(1)}, f32[4,512]{1,0:T(4,128)S(1)}, bf16[2,8,256,...) custom-call(s32[32]{0:T(128)S(1)} %get-tuple-element.194.idx, ...), custom_call_target="tpu_custom_call" | custom-call | flops 1342177280 | bytes 3407872 | tf_op jit(solution)/shard_map/ready/pallas_call | solution.py:53
  41.6 7.4 %collective-permute-done.11.refs_2_ = bf16[9,16,512]{2,1,0:T(8,128)(2,1)S(1)} collective-permute-done((bf16[9,16,512]{2,1,0:T(8,128)(2,1)S(1)}, bf16[9,16,512]{2,1,0:T(8,128)(2,1)S(1)}, u32[]{:S(2)}, u32[]{:S(2)}) %collective-permute-start.11) | collective-permute-done | bytes 147488 | tf_op jit(solution)/shard_map/ppermute | solution.py:646
  49.1 1.1 collective-permute-start.14
  50.2 2.0 %collective-permute-start.15 = (bf16[9,16,512]{2,1,0:T(8,128)(2,1)S(1)}, bf16[9,16,512]{2,1,0:T(8,128)(2,1)S(1)}, u32[]{:S(2)}, u32[]{:S(2)}) collective-permute-start(bf16[9,16,512]{2,1,0:T(8,128)(2,1)S(1)} %collective-permute-done.11.refs_2_), channel_id=1, source_target_pairs={{0,8},{2,10},{4,12},{6,14},{8,16},{10,18},{12,20},{14,22},{16,24},... | collective-permute-start | bytes 442376 | tf_op jit(solution)/shard_map/ppermute | solution.py:646
  52.2 5.3 %collective-permute-done.15.refs_3_ = bf16[9,16,512]{2,1,0:T(8,128)(2,1)S(1)} collective-permute-done((bf16[9,16,512]{2,1,0:T(8,128)(2,1)S(1)}, bf16[9,16,512]{2,1,0:T(8,128)(2,1)S(1)}, u32[]{:S(2)}, u32[]{:S(2)}) %collective-permute-start.15) | collective-permute-done | bytes 147488 | tf_op jit(solution)/shard_map/ppermute | solution.py:646
  57.6 0.8 copy.41.refs_0_
  58.4 1.0 collective-permute-start.17
  59.4 1.5 collective-permute-start.19
  61.2 1.7 project.1
  62.9 8.6 %attend.1 = (f32[256,640]{1,0:T(8,128)S(1)}, f32[256,640]{1,0:T(8,128)S(1)}, bf16[4,512,128]{2,1,0:T(8,128)(2,1)S(1)}) custom-call(s32[10]{0:T(128)S(1)} %pad_add_fusion.sc, s32[24]{0:T(128)S(1)} %pad_add_fusion.1.tab, bf16[4,256,128]{2,1,0:T(8,128)(2,1)S(1)} %get-tuple-element.203.q_own, bf16[4,256,128]{2,1,0:T(8,128)(2,1)S(1)} %collective-permute-done.16.q_other, ...), custom_call_target="tpu_custom_call" | custom-call | flops 2147483648 | bytes 8388608 | tf_op jit(solution)/shard_map/attend/pallas_call | solution.py:53
  71.5 0.8 copy-done.10
  72.4 2.8 %collective-permute-done.19.refs_1_.refs_4_ = bf16[4,9,16,512]{3,2,1,0:T(8,128)(2,1)S(1)} collective-permute-done((bf16[4,9,16,512]{3,2,1,0:T(8,128)(2,1)S(1)}, bf16[4,9,16,512]{3,2,1,0:T(8,128)(2,1)S(1)}, u32[]{:S(2)}, u32[]{:S(2)}) %collective-permute-start.19) | collective-permute-done | bytes 589856 | tf_op jit(solution)/shard_map/ppermute | solution.py:651
  75.3 1.6 collective-permute-start.23
  76.9 1.1 collective-permute-start.24
  78.5 6.3 %collective-permute-done.23.refs_6_ = bf16[2,9,16,512]{3,2,1,0:T(8,128)(2,1)S(1)} collective-permute-done((bf16[2,9,16,512]{3,2,1,0:T(8,128)(2,1)S(1)}, bf16[2,9,16,512]{3,2,1,0:T(8,128)(2,1)S(1)}, u32[]{:S(2)}, u32[]{:S(2)}) %collective-permute-start.23) | collective-permute-done | bytes 294944 | tf_op jit(solution)/shard_map/ppermute | solution.py:651
  84.8 1.2 collective-permute-done.24.refs_7_
  86.6 1.1 collective-permute-done.25.refs_8_
  88.1 12.7 %middle.1 = (bf16[256,512]{1,0:T(8,128)(2,1)}, f32[256,512]{1,0:T(8,128)S(1)}, bf16[256,640]{1,0:T(8,128)(2,1)S(1)}, f32[4,512]{1,0:T(4,128)S(1)}, f32[512,128]{...) custom-call(s32[64]{0:T(128)S(1)} %pad_add_fusion.2.idx, ...), custom_call_target="tpu_custom_call" | custom-call | flops 3623878656 | bytes 9437184 | tf_op jit(solution)/shard_map/middle/pallas_call | solution.py:53
  101.1 1.5 collective-permute-done.27.d_other
  103.6 2.2 %back.4 = (bf16[256,512]{1,0:T(8,128)(2,1)S(1)}, bf16[256,512]{1,0:T(8,128)(2,1)S(1)}, f32[4,128,256]{2,1,0:T(8,128)S(1)}, f32[4,128,256]{2,1,0:T(8,128)S(1)}, f...) custom-call(s32[10]{0:T(128)S(1)} %pad_add_fusion.sc, ...), custom_call_target="tpu_custom_call" | custom-call | flops 2415919104 | bytes 4194304 | tf_op jit(solution)/shard_map/back/pallas_call | solution.py:53
  106.5 0.8 collective-permute-done.28.refs_1_
  108.0 1.0 collective-permute-start.32
  109.1 1.6 collective-permute-start.36
  110.7 5.3 %back.5 = (bf16[256,512]{1,0:T(8,128)(2,1)S(1)}, bf16[256,512]{1,0:T(8,128)(2,1)S(1)}, f32[4,128,256]{2,1,0:T(8,128)S(1)}, f32[4,128,256]{2,1,0:T(8,128)S(1)}, f...) custom-call(s32[10]{0:T(128)S(1)} %pad_add_fusion.sc, s32[24]{0:T(128)S(1)} %pad_add_fusion.1.tab, ...), custom_call_target="tpu_custom_call" | custom-call | flops 2415919104 | bytes 4194304 | tf_op jit(solution)/shard_map/back/pallas_call | solution.py:53
  116.0 1.3 collective-permute-done.33.refs_2_
  117.4 1.9 %collective-permute-start.35 = (bf16[256,512]{1,0:T(8,128)(2,1)S(1)}, bf16[256,512]{1,0:T(8,128)(2,1)S(1)}, u32[]{:S(2)}, u32[]{:S(2)}) collective-permute-start(bf16[256,512]{1,0:T(8,128)(2,1)S(1)} %add.133), channel_id=1, source_target_pairs={{0,8},{2,10},{4,12},{6,14},{8,16},{10,18},{12,20},{14,22},{16,24},... | collective-permute-start | bytes 786440 | tf_op jit(solution)/shard_map/ppermute | solution.py:646
  119.2 1.5 collective-permute-start.34
  121.4 5.1 %back.6 = (bf16[256,512]{1,0:T(8,128)(2,1)S(1)}, bf16[256,512]{1,0:T(8,128)(2,1)S(1)}, f32[4,128,256]{2,1,0:T(8,128)S(1)}, f32[4,128,256]{2,1,0:T(8,128)S(1)}, f...) custom-call(s32[10]{0:T(128)S(1)} %pad_add_fusion.sc, s32[24]{0:T(128)S(1)} %pad_add_fusion.1.tab, ...), custom_call_target="tpu_custom_call" | custom-call | flops 2415919104 | bytes 4194304 | tf_op jit(solution)/shard_map/back/pallas_call | solution.py:53
  127.1 1.2 collective-permute-start.37
  128.3 5.3 %back.7 = (bf16[256,512]{1,0:T(8,128)(2,1)S(1)}, bf16[256,512]{1,0:T(8,128)(2,1)S(1)}, f32[4,128,256]{2,1,0:T(8,128)S(1)}, f32[4,128,256]{2,1,0:T(8,128)S(1)}, f...) custom-call(s32[10]{0:T(128)S(1)} %pad_add_fusion.sc, s32[24]{0:T(128)S(1)} %pad_add_fusion.1.tab, ...), custom_call_target="tpu_custom_call" | custom-call | flops 2415919104 | bytes 4194304 | tf_op jit(solution)/shard_map/back/pallas_call | solution.py:53
  133.7 1.2 collective-permute-done.38.refs_2_
  134.9 2.5 %message.1 = (bf16[16,16,1664]{2,1,0:T(8,128)(2,1)S(1)}, bf16[16,16,1664]{2,1,0:T(8,128)(2,1)S(1)}) custom-call(s32[32]{0:T(128)S(1)} %get-tuple-element.194.idx, bf16[2,256,512]{2,1,0:T(8,128)(2,1)S(1)} %get-tuple-element.285.n_near.n_far.n_own, bf16[1,256,512]{2,1,0:T(8,128)(2,1)S(1)} %collective-permute-done.40.n_other, ...), custom_call_target="tpu_custom_call" | custom-call | flops 134217728 | bytes 6815744 | tf_op jit(solution)/shard_map/message/pallas_call | solution.py:53
  137.7 1.1 collective-permute-start.51
  139.0 0.8 collective-permute-start.53
  140.0 1.9 %collective-permute-start.45 = (bf16[4,16,1664]{2,1,0:T(8,128)(2,1)S(1)}, bf16[4,16,1664]{2,1,0:T(8,128)(2,1)S(1)}, u32[]{:S(2)}, u32[]{:S(2)}) collective-permute-start(bf16[4,16,1664]{2,1,0:T(8,128)(2,1)S(1)} %get-tuple-element.319), channel_id=1, source_target_pairs={{0,4},{2,6},{4,0},{6,2},{8,12},{10,14},{12,8},{14,10},{16,20},{18,... | collective-permute-start | bytes 638984 | tf_op jit(solution)/shard_map/ppermute | solution.py:643
  142.4 6.7 %collective-permute-done.42.refs_4_ = bf16[256,512]{1,0:T(8,128)(2,1)S(1)} collective-permute-done((bf16[256,512]{1,0:T(8,128)(2,1)S(1)}, bf16[256,512]{1,0:T(8,128)(2,1)S(1)}, u32[]{:S(2)}, u32[]{:S(2)}) %collective-permute-start.42) | collective-permute-done | bytes 262176 | tf_op jit(solution)/shard_map/ppermute | solution.py:646
  149.1 2.0 %collective-permute-start.47 = (bf16[4,16,1664]{2,1,0:T(8,128)(2,1)S(1)}, bf16[4,16,1664]{2,1,0:T(8,128)(2,1)S(1)}, u32[]{:S(2)}, u32[]{:S(2)}) collective-permute-start(bf16[4,16,1664]{2,1,0:T(8,128)(2,1)S(1)} %get-tuple-element.321), channel_id=1, source_target_pairs={{0,5},{1,4},{2,7},{3,6},{4,1},{5,0},{6,3},{7,2},{8,13},{9,12},{10,... | collective-permute-start | bytes 638984 | tf_op jit(solution)/shard_map/ppermute | solution.py:654
  152.0 1.9 %collective-permute-done.51.refs_3_ = bf16[4,9,16,512]{3,2,1,0:T(8,128)(2,1)S(1)} collective-permute-done((bf16[4,9,16,512]{3,2,1,0:T(8,128)(2,1)S(1)}, bf16[4,9,16,512]{3,2,1,0:T(8,128)(2,1)S(1)}, u32[]{:S(2)}, u32[]{:S(2)}) %collective-permute-start.51) | collective-permute-done | bytes 589856 | tf_op jit(solution)/shard_map/ppermute | solution.py:643
  154.2 4.2 %collective-permute-done.45.refs_1_ = bf16[4,16,1664]{2,1,0:T(8,128)(2,1)S(1)} collective-permute-done((bf16[4,16,1664]{2,1,0:T(8,128)(2,1)S(1)}, bf16[4,16,1664]{2,1,0:T(8,128)(2,1)S(1)}, u32[]{:S(2)}, u32[]{:S(2)}) %collective-permute-start.45) | collective-permute-done | bytes 213024 | tf_op jit(solution)/shard_map/ppermute | solution.py:643
  159.1 1.9 %collective-permute-start.55 = (bf16[9,16,512]{2,1,0:T(8,128)(2,1)S(1)}, bf16[9,16,512]{2,1,0:T(8,128)(2,1)S(1)}, u32[]{:S(2)}, u32[]{:S(2)}) collective-permute-start(bf16[9,16,512]{2,1,0:T(8,128)(2,1)S(1)} %get-tuple-element.336), channel_id=1, source_target_pairs={{0,8},{2,10},{4,12},{6,14},{8,16},{10,18},{12,20},{14,22},{16,24},... | collective-permute-start | bytes 442376 | tf_op jit(solution)/shard_map/ppermute | solution.py:646
  161.0 2.9 %collective-permute-done.47.refs_3_ = bf16[4,16,1664]{2,1,0:T(8,128)(2,1)S(1)} collective-permute-done((bf16[4,16,1664]{2,1,0:T(8,128)(2,1)S(1)}, bf16[4,16,1664]{2,1,0:T(8,128)(2,1)S(1)}, u32[]{:S(2)}, u32[]{:S(2)}) %collective-permute-start.47) | collective-permute-done | bytes 213024 | tf_op jit(solution)/shard_map/ppermute | solution.py:654
  163.9 2.0 %collective-permute-start.52 = (bf16[9,16,512]{2,1,0:T(8,128)(2,1)S(1)}, bf16[9,16,512]{2,1,0:T(8,128)(2,1)S(1)}, u32[]{:S(2)}, u32[]{:S(2)}) collective-permute-start(bf16[9,16,512]{2,1,0:T(8,128)(2,1)S(1)} %get-tuple-element.334), channel_id=1, source_target_pairs={{0,24},{2,26},{4,28},{6,30},{8,0},{10,2},{12,4},{14,6},{16,8},{18,... | collective-permute-start | bytes 442376 | tf_op jit(solution)/shard_map/ppermute | solution.py:646
  166.0 4.2 %collective-permute-done.54.refs_2_ = bf16[9,16,512]{2,1,0:T(8,128)(2,1)S(1)} collective-permute-done((bf16[9,16,512]{2,1,0:T(8,128)(2,1)S(1)}, bf16[9,16,512]{2,1,0:T(8,128)(2,1)S(1)}, u32[]{:S(2)}, u32[]{:S(2)}) %collective-permute-start.54) | collective-permute-done | bytes 147488 | tf_op jit(solution)/shard_map/ppermute | solution.py:646
  170.2 5.2 %collective-permute-start.49 = (bf16[16,1664]{1,0:T(8,128)(2,1)S(1)}, bf16[16,1664]{1,0:T(8,128)(2,1)S(1)}, u32[]{:S(2)}, u32[]{:S(2)}) collective-permute-start(bf16[16,1664]{1,0:T(8,128)(2,1)S(1)} %get-tuple-element.323), channel_id=1, source_target_pairs={{0,16},{2,18},{4,20},{6,22},{8,24},{10,26},{12,28},{14,30},{16,0},... | collective-permute-start | bytes 159752 | tf_op jit(solution)/shard_map/ppermute | solution.py:646
  175.4 0.7 matrices.1
  176.2 1.2 finish.1
  177.5 3.8 %collective-permute-done.50.refs_3_ = bf16[16,1664]{1,0:T(8,128)(2,1)S(1)} collective-permute-done((bf16[16,1664]{1,0:T(8,128)(2,1)S(1)}, bf16[16,1664]{1,0:T(8,128)(2,1)S(1)}, u32[]{:S(2)}, u32[]{:S(2)}) %collective-permute-start.50) | collective-permute-done | bytes 53280 | tf_op jit(solution)/shard_map/ppermute | solution.py:646
  (117 shorter events, 13.0 us)
Async XLA Ops:
  0.7 37.6 %copy-start.5 = (bf16[1,256,512]{2,1,0:T(8,128)(2,1)S(1)}, bf16[1,256,512]{2,1,0:T(8,128)(2,1)}, u32[]{:S(2)}) copy-start(bf16[1,256,512]{2,1,0:T(8,128)(2,1)} %param.24) | copy-start | bytes 786436
  2.5 11.5 %collective-permute-start = (bf16[4,16,512]{2,1,0:T(8,128)(2,1)}, bf16[4,16,512]{2,1,0:T(8,128)(2,1)S(1)}, u32[]{:S(2)}, u32[]{:S(2)}) collective-permute-start(bf16[4,16,512]{2,1,0:T(8,128)(2,1)} %get-tuple-element.182), channel_id=1, source_target_pairs={{0,8},{2,10},{4,12},{6,14},{8,16},{10,18},{12,20},{14,22},{16,24},... | collective-permute-start | bytes 196616 | tf_op jit(solution)/shard_map/ppermute | solution.py:646
  5.5 8.5 %collective-permute-start.1 = (bf16[4,16,512]{2,1,0:T(8,128)(2,1)}, bf16[4,16,512]{2,1,0:T(8,128)(2,1)S(1)}, u32[]{:S(2)}, u32[]{:S(2)}) collective-permute-start(bf16[4,16,512]{2,1,0:T(8,128)(2,1)} %get-tuple-element.182), channel_id=1, source_target_pairs={{0,16},{2,18},{4,20},{6,22},{8,24},{10,26},{12,28},{14,30},{16,0},... | collective-permute-start | bytes 196616 | tf_op jit(solution)/shard_map/ppermute | solution.py:646
  8.1 5.9 %collective-permute-start.2 = (bf16[4,16,512]{2,1,0:T(8,128)(2,1)}, bf16[4,16,512]{2,1,0:T(8,128)(2,1)S(1)}, u32[]{:S(2)}, u32[]{:S(2)}) collective-permute-start(bf16[4,16,512]{2,1,0:T(8,128)(2,1)} %get-tuple-element.182), channel_id=1, source_target_pairs={{0,24},{2,26},{4,28},{6,30},{8,0},{10,2},{12,4},{14,6},{16,8},{18,... | collective-permute-start | bytes 196616 | tf_op jit(solution)/shard_map/ppermute | solution.py:646
  9.4 7.4 %collective-permute-start.3 = (bf16[256,512]{1,0:T(8,128)(2,1)}, bf16[256,512]{1,0:T(8,128)(2,1)S(1)}, u32[]{:S(2)}, u32[]{:S(2)}) collective-permute-start(bf16[256,512]{1,0:T(8,128)(2,1)} %bitcast.45), channel_id=1, source_target_pairs={{0,4},{2,6},{4,0},{6,2},{8,12},{10,14},{12,8},{14,10},{16,20},{18,... | collective-permute-start | bytes 786440 | tf_op jit(solution)/shard_map/ppermute | solution.py:643
  10.9 8.9 %collective-permute-start.4 = (bf16[256,512]{1,0:T(8,128)(2,1)}, bf16[256,512]{1,0:T(8,128)(2,1)S(1)}, u32[]{:S(2)}, u32[]{:S(2)}) collective-permute-start(bf16[256,512]{1,0:T(8,128)(2,1)} %bitcast.46), channel_id=1, source_target_pairs={{0,8},{2,10},{4,12},{6,14},{8,16},{10,18},{12,20},{14,22},{16,24},... | collective-permute-start | bytes 786440 | tf_op jit(solution)/shard_map/ppermute | solution.py:646
  20.7 13.7 %collective-permute-start.5 = (bf16[4,4,16,512]{3,2,1,0:T(8,128)(2,1)S(1)}, bf16[4,4,16,512]{3,2,1,0:T(8,128)(2,1)S(1)}, u32[]{:S(2)}, u32[]{:S(2)}) collective-permute-start(bf16[4,4,16,512]{3,2,1,0:T(8,128)(2,1)S(1)} %get-tuple-element.350), channel_id=1, source_target_pairs={{0,4},{2,6},{4,0},{6,2},{8,12},{10,14},{12,8},{14,10},{16,20},{18,... | collective-permute-start | bytes 786440 | tf_op jit(solution)/shard_map/ppermute | solution.py:643
  21.5 13.0 %collective-permute-start.6 = (bf16[4,4,16,512]{3,2,1,0:T(8,128)(2,1)S(1)}, bf16[4,4,16,512]{3,2,1,0:T(8,128)(2,1)S(1)}, u32[]{:S(2)}, u32[]{:S(2)}) collective-permute-start(bf16[4,4,16,512]{3,2,1,0:T(8,128)(2,1)S(1)} %get-tuple-element.350), channel_id=1, source_target_pairs={{0,1},{1,0},{2,3},{3,2},{4,5},{5,4},{6,7},{7,6},{8,9},{9,8},{10,11... | collective-permute-start | bytes 786440 | tf_op jit(solution)/shard_map/ppermute | solution.py:651
  23.0 11.5 %collective-permute-start.7 = (bf16[4,4,16,512]{3,2,1,0:T(8,128)(2,1)S(1)}, bf16[4,4,16,512]{3,2,1,0:T(8,128)(2,1)S(1)}, u32[]{:S(2)}, u32[]{:S(2)}) collective-permute-start(bf16[4,4,16,512]{3,2,1,0:T(8,128)(2,1)S(1)} %get-tuple-element.350), channel_id=1, source_target_pairs={{0,5},{1,4},{2,7},{3,6},{4,1},{5,0},{6,3},{7,2},{8,13},{9,12},{10,... | collective-permute-start | bytes 786440 | tf_op jit(solution)/shard_map/ppermute | solution.py:654
  24.3 10.1 %collective-permute-start.8 = (bf16[256,512]{1,0:T(8,128)(2,1)S(1)}, bf16[256,512]{1,0:T(8,128)(2,1)S(1)}, u32[]{:S(2)}, u32[]{:S(2)}) collective-permute-start(bf16[256,512]{1,0:T(8,128)(2,1)S(1)} %collective-permute-done.4), channel_id=1, source_target_pairs={{0,8},{2,10},{4,12},{6,14},{8,16},{10,18},{12,20},{14,22},{16,24},... | collective-permute-start | bytes 786440 | tf_op jit(solution)/shard_map/ppermute | solution.py:646
  24.3 10.1 %collective-permute-start.9 = (bf16[9,16,512]{2,1,0:T(8,128)(2,1)}, bf16[9,16,512]{2,1,0:T(8,128)(2,1)S(1)}, u32[]{:S(2)}, u32[]{:S(2)}) collective-permute-start(bf16[9,16,512]{2,1,0:T(8,128)(2,1)} %get-tuple-element.191.refs_0_), channel_id=1, source_target_pairs={{0,8},{2,10},{4,12},{6,14},{8,16},{10,18},{12,20},{14,22},{16,24},... | collective-permute-start | bytes 442376 | tf_op jit(solution)/shard_map/ppermute | solution.py:646
  34.6 3.7 %collective-permute-start.13 = (bf16[4,4,4,16,512]{4,3,2,1,0:T(8,128)(2,1)S(1)}, bf16[4,4,4,16,512]{4,3,2,1,0:T(8,128)(2,1)S(1)}, u32[]{:S(2)}, u32[]{:S(2)}) collective-permute-start(bf16[4,4,4,16,512]{4,3,2,1,0:T(8,128)(2,1)S(1)} %pad_maximum_fusion), channel_id=1, source_target_pairs={{0,2},{2,0},{4,6},{6,4},{8,10},{10,8},{12,14},{14,12},{16,18},{18,... | collective-permute-start | bytes 3145736 | tf_op jit(solution)/shard_map/ppermute | solution.py:640
  34.7 14.4 %collective-permute-start.12 = (bf16[2,256,512]{2,1,0:T(8,128)(2,1)S(1)}, bf16[2,256,512]{2,1,0:T(8,128)(2,1)S(1)}, u32[]{:S(2)}, u32[]{:S(2)}) collective-permute-start(bf16[2,256,512]{2,1,0:T(8,128)(2,1)S(1)} %pad_maximum_fusion.1.refs_4_), channel_id=1, source_target_pairs={{0,4},{2,6},{4,0},{6,2},{8,12},{10,14},{12,8},{14,10},{16,20},{18,... | collective-permute-start | bytes 1572872 | tf_op jit(solution)/shard_map/ppermute | solution.py:643
  35.7 13.4 %collective-permute-start.10 = (bf16[256,512]{1,0:T(8,128)(2,1)S(1)}, bf16[256,512]{1,0:T(8,128)(2,1)S(1)}, u32[]{:S(2)}, u32[]{:S(2)}) collective-permute-start(bf16[256,512]{1,0:T(8,128)(2,1)S(1)} %collective-permute-done.8), channel_id=1, source_target_pairs={{0,8},{2,10},{4,12},{6,14},{8,16},{10,18},{12,20},{14,22},{16,24},... | collective-permute-start | bytes 786440 | tf_op jit(solution)/shard_map/ppermute | solution.py:646
  37.5 11.6 %collective-permute-start.11 = (bf16[9,16,512]{2,1,0:T(8,128)(2,1)S(1)}, bf16[9,16,512]{2,1,0:T(8,128)(2,1)S(1)}, u32[]{:S(2)}, u32[]{:S(2)}) collective-permute-start(bf16[9,16,512]{2,1,0:T(8,128)(2,1)S(1)} %collective-permute-done.9.refs_1_), channel_id=1, source_target_pairs={{0,8},{2,10},{4,12},{6,14},{8,16},{10,18},{12,20},{14,22},{16,24},... | collective-permute-start | bytes 442376 | tf_op jit(solution)/shard_map/ppermute | solution.py:646
  38.3 19.3 %copy-start.8 = (bf16[9,16,512]{2,1,0:T(8,128)(2,1)S(1)}, bf16[9,16,512]{2,1,0:T(8,128)(2,1)}, u32[]{:S(2)}) copy-start(bf16[9,16,512]{2,1,0:T(8,128)(2,1)} %get-tuple-element.191.refs_0_) | copy-start | bytes 442372
  49.1 8.5 %collective-permute-start.14 = (bf16[1,256,512]{2,1,0:T(8,128)(2,1)S(1)}, bf16[1,256,512]{2,1,0:T(8,128)(2,1)S(1)}, u32[]{:S(2)}, u32[]{:S(2)}) collective-permute-start(bf16[1,256,512]{2,1,0:T(8,128)(2,1)S(1)} %bitcast.52), channel_id=1, source_target_pairs={{0,4},{2,6},{4,0},{6,2},{8,12},{10,14},{12,8},{14,10},{16,20},{18,... | collective-permute-start | bytes 786440 | tf_op jit(solution)/shard_map/ppermute | solution.py:643
  50.2 7.4 %collective-permute-start.15 = (bf16[9,16,512]{2,1,0:T(8,128)(2,1)S(1)}, bf16[9,16,512]{2,1,0:T(8,128)(2,1)S(1)}, u32[]{:S(2)}, u32[]{:S(2)}) collective-permute-start(bf16[9,16,512]{2,1,0:T(8,128)(2,1)S(1)} %collective-permute-done.11.refs_2_), channel_id=1, source_target_pairs={{0,8},{2,10},{4,12},{6,14},{8,16},{10,18},{12,20},{14,22},{16,24},... | collective-permute-start | bytes 442376 | tf_op jit(solution)/shard_map/ppermute | solution.py:646
  58.4 13.1 %copy-start.2 = (bf16[4,9,16,512]{3,2,1,0:T(8,128)(2,1)}, bf16[4,9,16,512]{3,2,1,0:T(8,128)(2,1)S(1)}, u32[]{:S(2)}) copy-start(bf16[4,9,16,512]{3,2,1,0:T(8,128)(2,1)S(1)} %copy.41.refs_0_) | copy-start | bytes 1769476
  58.4 13.9 %collective-permute-start.17 = (bf16[4,9,16,512]{3,2,1,0:T(8,128)(2,1)S(1)}, bf16[4,9,16,512]{3,2,1,0:T(8,128)(2,1)S(1)}, u32[]{:S(2)}, u32[]{:S(2)}) collective-permute-start(bf16[4,9,16,512]{3,2,1,0:T(8,128)(2,1)S(1)} %copy.41.refs_0_), channel_id=1, source_target_pairs={{0,4},{2,6},{4,0},{6,2},{8,12},{10,14},{12,8},{14,10},{16,20},{18,... | collective-permute-start | bytes 1769480 | tf_op jit(solution)/shard_map/ppermute | solution.py:643
  59.4 12.9 %collective-permute-start.18 = (bf16[4,9,16,512]{3,2,1,0:T(8,128)(2,1)S(1)}, bf16[4,9,16,512]{3,2,1,0:T(8,128)(2,1)S(1)}, u32[]{:S(2)}, u32[]{:S(2)}) collective-permute-start(bf16[4,9,16,512]{3,2,1,0:T(8,128)(2,1)S(1)} %copy.41.refs_0_), channel_id=1, source_target_pairs={{0,2},{2,0},{4,6},{6,4},{8,10},{10,8},{12,14},{14,12},{16,18},{18,... | collective-permute-start | bytes 1769480 | tf_op jit(solution)/shard_map/ppermute | solution.py:640
  59.4 15.7 %collective-permute-start.19 = (bf16[4,9,16,512]{3,2,1,0:T(8,128)(2,1)S(1)}, bf16[4,9,16,512]{3,2,1,0:T(8,128)(2,1)S(1)}, u32[]{:S(2)}, u32[]{:S(2)}) collective-permute-start(bf16[4,9,16,512]{3,2,1,0:T(8,128)(2,1)S(1)} %copy.41.refs_0_), channel_id=1, source_target_pairs={{0,1},{1,0},{2,3},{3,2},{4,5},{5,4},{6,7},{7,6},{8,9},{9,8},{10,11... | collective-permute-start | bytes 1769480 | tf_op jit(solution)/shard_map/ppermute | solution.py:651
  61.0 1.9 %collective-permute-start.16 = (bf16[4,256,128]{2,1,0:T(8,128)(2,1)S(1)}, bf16[4,256,128]{2,1,0:T(8,128)(2,1)S(1)}, u32[]{:S(2)}, u32[]{:S(2)}) collective-permute-start(bf16[4,256,128]{2,1,0:T(8,128)(2,1)S(1)} %get-tuple-element.203.q_own), channel_id=1, source_target_pairs={{0,2},{2,0},{4,6},{6,4},{8,10},{10,8},{12,14},{14,12},{16,18},{18,... | collective-permute-start | bytes 786440 | tf_op jit(solution)/shard_map/ppermute | solution.py:640
  62.9 25.2 %copy-start.9 = (bf16[1,256,512]{2,1,0:T(8,128)(2,1)S(1)}, bf16[1,256,512]{2,1,0:T(8,128)(2,1)}, u32[]{:S(2)}) copy-start(bf16[1,256,512]{2,1,0:T(8,128)(2,1)} %param.38) | copy-start | bytes 786436
  72.3 15.7 %copy-start.3 = (bf16[4,9,16,512]{3,2,1,0:T(8,128)(2,1)}, bf16[4,9,16,512]{3,2,1,0:T(8,128)(2,1)S(1)}, u32[]{:S(2)}) copy-start(bf16[4,9,16,512]{3,2,1,0:T(8,128)(2,1)S(1)} %collective-permute-done.17.refs_0_.refs_2_) | copy-start | bytes 1769476
  75.2 12.9 %copy-start.4 = (bf16[4,9,16,512]{3,2,1,0:T(8,128)(2,1)}, bf16[4,9,16,512]{3,2,1,0:T(8,128)(2,1)S(1)}, u32[]{:S(2)}) copy-start(bf16[4,9,16,512]{3,2,1,0:T(8,128)(2,1)S(1)} %collective-permute-done.19.refs_1_.refs_4_) | copy-start | bytes 1769476
  75.2 10.9 %collective-permute-start.22 = (f32[256,640]{1,0:T(8,128)S(1)}, f32[256,640]{1,0:T(8,128)S(1)}, u32[]{:S(2)}, u32[]{:S(2)}) collective-permute-start(f32[256,640]{1,0:T(8,128)S(1)} %get-tuple-element.217), channel_id=1, source_target_pairs={{0,2},{2,0},{4,6},{6,4},{8,10},{10,8},{12,14},{14,12},{16,18},{18,... | collective-permute-start | bytes 1966088 | tf_op jit(solution)/shard_map/ppermute | solution.py:640
  75.3 9.5 %collective-permute-start.23 = (bf16[2,9,16,512]{3,2,1,0:T(8,128)(2,1)S(1)}, bf16[2,9,16,512]{3,2,1,0:T(8,128)(2,1)S(1)}, u32[]{:S(2)}, u32[]{:S(2)}) collective-permute-start(bf16[2,9,16,512]{3,2,1,0:T(8,128)(2,1)S(1)} %get-tuple-element.218), channel_id=1, source_target_pairs={{0,1},{1,0},{2,3},{3,2},{4,5},{5,4},{6,7},{7,6},{8,9},{9,8},{10,11... | collective-permute-start | bytes 884744 | tf_op jit(solution)/shard_map/ppermute | solution.py:651
  76.9 9.1 %collective-permute-start.24 = (bf16[2,9,16,512]{3,2,1,0:T(8,128)(2,1)S(1)}, bf16[2,9,16,512]{3,2,1,0:T(8,128)(2,1)S(1)}, u32[]{:S(2)}, u32[]{:S(2)}) collective-permute-start(bf16[2,9,16,512]{3,2,1,0:T(8,128)(2,1)S(1)} %get-tuple-element.219), channel_id=1, source_target_pairs={{0,4},{2,6},{4,0},{6,2},{8,12},{10,14},{12,8},{14,10},{16,20},{18,... | collective-permute-start | bytes 884744 | tf_op jit(solution)/shard_map/ppermute | solution.py:643
  78.0 8.6 %collective-permute-start.20 = (bf16[4,9,16,512]{3,2,1,0:T(8,128)(2,1)S(1)}, bf16[4,9,16,512]{3,2,1,0:T(8,128)(2,1)S(1)}, u32[]{:S(2)}, u32[]{:S(2)}) collective-permute-start(bf16[4,9,16,512]{3,2,1,0:T(8,128)(2,1)S(1)} %collective-permute-done.17.refs_0_.refs_2_), channel_id=1, source_target_pairs={{0,2},{2,0},{4,6},{6,4},{8,10},{10,8},{12,14},{14,12},{16,18},{18,... | collective-permute-start | bytes 1769480 | tf_op jit(solution)/shard_map/ppermute | solution.py:640
  78.0 8.6 %collective-permute-start.21 = (bf16[4,9,16,512]{3,2,1,0:T(8,128)(2,1)S(1)}, bf16[4,9,16,512]{3,2,1,0:T(8,128)(2,1)S(1)}, u32[]{:S(2)}, u32[]{:S(2)}) collective-permute-start(bf16[4,9,16,512]{3,2,1,0:T(8,128)(2,1)S(1)} %collective-permute-done.19.refs_1_.refs_4_), channel_id=1, source_target_pairs={{0,2},{2,0},{4,6},{6,4},{8,10},{10,8},{12,14},{14,12},{16,18},{18,... | collective-permute-start | bytes 1769480 | tf_op jit(solution)/shard_map/ppermute | solution.py:640
  86.1 1.6 collective-permute-start.25
  86.1 2.0 %collective-permute-start.26 = (bf16[2,9,16,512]{3,2,1,0:T(8,128)(2,1)S(1)}, bf16[2,9,16,512]{3,2,1,0:T(8,128)(2,1)S(1)}, u32[]{:S(2)}, u32[]{:S(2)}) collective-permute-start(bf16[2,9,16,512]{3,2,1,0:T(8,128)(2,1)S(1)} %collective-permute-done.24.refs_7_), channel_id=1, source_target_pairs={{0,2},{2,0},{4,6},{6,4},{8,10},{10,8},{12,14},{14,12},{16,18},{18,... | collective-permute-start | bytes 884744 | tf_op jit(solution)/shard_map/ppermute | solution.py:640
  100.9 1.7 collective-permute-start.27
  102.6 3.2 %collective-permute-start.31 = (bf16[4,9,16,512]{3,2,1,0:T(8,128)(2,1)}, bf16[4,9,16,512]{3,2,1,0:T(8,128)(2,1)S(1)}, u32[]{:S(2)}, u32[]{:S(2)}) collective-permute-start(bf16[4,9,16,512]{3,2,1,0:T(8,128)(2,1)} %get-tuple-element.247), channel_id=1, source_target_pairs={{0,2},{2,0},{4,6},{6,4},{8,10},{10,8},{12,14},{14,12},{16,18},{18,... | collective-permute-start | bytes 1769480 | tf_op jit(solution)/shard_map/ppermute | solution.py:640
  102.7 3.1 %collective-permute-start.30 = (bf16[4,9,16,512]{3,2,1,0:T(8,128)(2,1)}, bf16[4,9,16,512]{3,2,1,0:T(8,128)(2,1)S(1)}, u32[]{:S(2)}, u32[]{:S(2)}) collective-permute-start(bf16[4,9,16,512]{3,2,1,0:T(8,128)(2,1)} %get-tuple-element.245), channel_id=1, source_target_pairs={{0,2},{2,0},{4,6},{6,4},{8,10},{10,8},{12,14},{14,12},{16,18},{18,... | collective-permute-start | bytes 1769480 | tf_op jit(solution)/shard_map/ppermute | solution.py:640
  103.1 3.4 %collective-permute-start.29 = (bf16[4,9,16,512]{3,2,1,0:T(8,128)(2,1)}, bf16[4,9,16,512]{3,2,1,0:T(8,128)(2,1)S(1)}, u32[]{:S(2)}, u32[]{:S(2)}) collective-permute-start(bf16[4,9,16,512]{3,2,1,0:T(8,128)(2,1)} %get-tuple-element.243), channel_id=1, source_target_pairs={{0,2},{2,0},{4,6},{6,4},{8,10},{10,8},{12,14},{14,12},{16,18},{18,... | collective-permute-start | bytes 1769480 | tf_op jit(solution)/shard_map/ppermute | solution.py:640
  103.2 4.1 %collective-permute-start.28 = (bf16[4,9,16,512]{3,2,1,0:T(8,128)(2,1)}, bf16[4,9,16,512]{3,2,1,0:T(8,128)(2,1)S(1)}, u32[]{:S(2)}, u32[]{:S(2)}) collective-permute-start(bf16[4,9,16,512]{3,2,1,0:T(8,128)(2,1)} %get-tuple-element.241), channel_id=1, source_target_pairs={{0,2},{2,0},{4,6},{6,4},{8,10},{10,8},{12,14},{14,12},{16,18},{18,... | collective-permute-start | bytes 1769480 | tf_op jit(solution)/shard_map/ppermute | solution.py:640
  107.4 9.9 %collective-permute-start.33 = (bf16[2,9,16,512]{3,2,1,0:T(8,128)(2,1)S(1)}, bf16[2,9,16,512]{3,2,1,0:T(8,128)(2,1)S(1)}, u32[]{:S(2)}, u32[]{:S(2)}) collective-permute-start(bf16[2,9,16,512]{3,2,1,0:T(8,128)(2,1)S(1)} %add.132), channel_id=1, source_target_pairs={{0,1},{1,0},{2,3},{3,2},{4,5},{5,4},{6,7},{7,6},{8,9},{9,8},{10,11... | collective-permute-start | bytes 884744 | tf_op jit(solution)/shard_map/ppermute | solution.py:651
  108.0 8.1 %collective-permute-start.32 = (bf16[256,512]{1,0:T(8,128)(2,1)S(1)}, bf16[256,512]{1,0:T(8,128)(2,1)S(1)}, u32[]{:S(2)}, u32[]{:S(2)}) collective-permute-start(bf16[256,512]{1,0:T(8,128)(2,1)S(1)} %get-tuple-element.261), channel_id=1, source_target_pairs={{0,4},{2,6},{4,0},{6,2},{8,12},{10,14},{12,8},{14,10},{16,20},{18,... | collective-permute-start | bytes 786440 | tf_op jit(solution)/shard_map/ppermute | solution.py:643
  109.1 11.7 %copy-start = (bf16[4,9,16,512]{3,2,1,0:T(8,128)(2,1)S(1)}, bf16[4,9,16,512]{3,2,1,0:T(8,128)(2,1)}, u32[]{:S(2)}) copy-start(bf16[4,9,16,512]{3,2,1,0:T(8,128)(2,1)} %get-tuple-element.296.refs_0_) | copy-start | bytes 1769476
  109.1 17.4 %collective-permute-start.36 = (bf16[2,9,16,512]{3,2,1,0:T(8,128)(2,1)S(1)}, bf16[2,9,16,512]{3,2,1,0:T(8,128)(2,1)S(1)}, u32[]{:S(2)}, u32[]{:S(2)}) collective-permute-start(bf16[2,9,16,512]{3,2,1,0:T(8,128)(2,1)S(1)} %add.134), channel_id=1, source_target_pairs={{0,1},{1,0},{2,3},{3,2},{4,5},{5,4},{6,7},{7,6},{8,9},{9,8},{10,11... | collective-permute-start | bytes 884744 | tf_op jit(solution)/shard_map/ppermute | solution.py:651
  117.4 9.2 %collective-permute-start.35 = (bf16[256,512]{1,0:T(8,128)(2,1)S(1)}, bf16[256,512]{1,0:T(8,128)(2,1)S(1)}, u32[]{:S(2)}, u32[]{:S(2)}) collective-permute-start(bf16[256,512]{1,0:T(8,128)(2,1)S(1)} %add.133), channel_id=1, source_target_pairs={{0,8},{2,10},{4,12},{6,14},{8,16},{10,18},{12,20},{14,22},{16,24},... | collective-permute-start | bytes 786440 | tf_op jit(solution)/shard_map/ppermute | solution.py:646
  119.2 7.3 %collective-permute-start.34 = (bf16[256,512]{1,0:T(8,128)(2,1)S(1)}, bf16[256,512]{1,0:T(8,128)(2,1)S(1)}, u32[]{:S(2)}, u32[]{:S(2)}) collective-permute-start(bf16[256,512]{1,0:T(8,128)(2,1)S(1)} %get-tuple-element.278), channel_id=1, source_target_pairs={{0,4},{2,6},{4,0},{6,2},{8,12},{10,14},{12,8},{14,10},{16,20},{18,... | collective-permute-start | bytes 786440 | tf_op jit(solution)/shard_map/ppermute | solution.py:643
  120.8 12.8 %collective-permute-start.39 = (bf16[2,9,16,512]{3,2,1,0:T(8,128)(2,1)S(1)}, bf16[2,9,16,512]{3,2,1,0:T(8,128)(2,1)S(1)}, u32[]{:S(2)}, u32[]{:S(2)}) collective-permute-start(bf16[2,9,16,512]{3,2,1,0:T(8,128)(2,1)S(1)} %add.136), channel_id=1, source_target_pairs={{0,1},{1,0},{2,3},{3,2},{4,5},{5,4},{6,7},{7,6},{8,9},{9,8},{10,11... | collective-permute-start | bytes 884744 | tf_op jit(solution)/shard_map/ppermute | solution.py:651
  126.7 8.2 %collective-permute-start.38 = (bf16[256,512]{1,0:T(8,128)(2,1)S(1)}, bf16[256,512]{1,0:T(8,128)(2,1)S(1)}, u32[]{:S(2)}, u32[]{:S(2)}) collective-permute-start(bf16[256,512]{1,0:T(8,128)(2,1)S(1)} %add.135), channel_id=1, source_target_pairs={{0,8},{2,10},{4,12},{6,14},{8,16},{10,18},{12,20},{14,22},{16,24},... | collective-permute-start | bytes 786440 | tf_op jit(solution)/shard_map/ppermute | solution.py:646
  127.1 7.8 %collective-permute-start.37 = (bf16[256,512]{1,0:T(8,128)(2,1)S(1)}, bf16[256,512]{1,0:T(8,128)(2,1)S(1)}, u32[]{:S(2)}, u32[]{:S(2)}) collective-permute-start(bf16[256,512]{1,0:T(8,128)(2,1)S(1)} %get-tuple-element.295), channel_id=1, source_target_pairs={{0,4},{2,6},{4,0},{6,2},{8,12},{10,14},{12,8},{14,10},{16,20},{18,... | collective-permute-start | bytes 786440 | tf_op jit(solution)/shard_map/ppermute | solution.py:643
  128.3 6.5 %collective-permute-start.40 = (bf16[1,256,512]{2,1,0:T(8,128)(2,1)S(1)}, bf16[1,256,512]{2,1,0:T(8,128)(2,1)S(1)}, u32[]{:S(2)}, u32[]{:S(2)}) collective-permute-start(bf16[1,256,512]{2,1,0:T(8,128)(2,1)S(1)} %get-tuple-element.299), channel_id=1, source_target_pairs={{0,2},{2,0},{4,6},{6,4},{8,10},{10,8},{12,14},{14,12},{16,18},{18,... | collective-permute-start | bytes 786440 | tf_op jit(solution)/shard_map/ppermute | solution.py:640
  128.3 6.5 %copy-start.7 = (f32[512,128]{1,0:T(8,128)S(1)}, f32[512,128]{1,0:T(8,128)}, u32[]{:S(2)}) copy-start(f32[512,128]{1,0:T(8,128)} %copy-done.6) | copy-start | bytes 786436
  137.3 2.4 %collective-permute-start.41 = (bf16[16,16,1664]{2,1,0:T(8,128)(2,1)S(1)}, bf16[16,16,1664]{2,1,0:T(8,128)(2,1)S(1)}, u32[]{:S(2)}, u32[]{:S(2)}) collective-permute-start(bf16[16,16,1664]{2,1,0:T(8,128)(2,1)S(1)} %get-tuple-element.306), channel_id=1, source_target_pairs={{0,2},{2,0},{4,6},{6,4},{8,10},{10,8},{12,14},{14,12},{16,18},{18,... | collective-permute-start | bytes 2555912 | tf_op jit(solution)/shard_map/ppermute | solution.py:640
  137.7 16.2 %collective-permute-start.51 = (bf16[4,9,16,512]{3,2,1,0:T(8,128)(2,1)S(1)}, bf16[4,9,16,512]{3,2,1,0:T(8,128)(2,1)S(1)}, u32[]{:S(2)}, u32[]{:S(2)}) collective-permute-start(bf16[4,9,16,512]{3,2,1,0:T(8,128)(2,1)S(1)} %join.1), channel_id=1, source_target_pairs={{0,4},{2,6},{4,0},{6,2},{8,12},{10,14},{12,8},{14,10},{16,20},{18,... | collective-permute-start | bytes 1769480 | tf_op jit(solution)/shard_map/ppermute | solution.py:643
  138.8 10.3 %collective-permute-start.42 = (bf16[256,512]{1,0:T(8,128)(2,1)S(1)}, bf16[256,512]{1,0:T(8,128)(2,1)S(1)}, u32[]{:S(2)}, u32[]{:S(2)}) collective-permute-start(bf16[256,512]{1,0:T(8,128)(2,1)S(1)} %add.138), channel_id=1, source_target_pairs={{0,8},{2,10},{4,12},{6,14},{8,16},{10,18},{12,20},{14,22},{16,24},... | collective-permute-start | bytes 786440 | tf_op jit(solution)/shard_map/ppermute | solution.py:646
  139.0 12.6 %collective-permute-start.53 = (bf16[2,9,16,512]{3,2,1,0:T(8,128)(2,1)S(1)}, bf16[2,9,16,512]{3,2,1,0:T(8,128)(2,1)S(1)}, u32[]{:S(2)}, u32[]{:S(2)}) collective-permute-start(bf16[2,9,16,512]{3,2,1,0:T(8,128)(2,1)S(1)} %add.142), channel_id=1, source_target_pairs={{0,1},{1,0},{2,3},{3,2},{4,5},{5,4},{6,7},{7,6},{8,9},{9,8},{10,11... | collective-permute-start | bytes 884744 | tf_op jit(solution)/shard_map/ppermute | solution.py:651
  140.0 18.4 %collective-permute-start.45 = (bf16[4,16,1664]{2,1,0:T(8,128)(2,1)S(1)}, bf16[4,16,1664]{2,1,0:T(8,128)(2,1)S(1)}, u32[]{:S(2)}, u32[]{:S(2)}) collective-permute-start(bf16[4,16,1664]{2,1,0:T(8,128)(2,1)S(1)} %get-tuple-element.319), channel_id=1, source_target_pairs={{0,4},{2,6},{4,0},{6,2},{8,12},{10,14},{12,8},{14,10},{16,20},{18,... | collective-permute-start | bytes 638984 | tf_op jit(solution)/shard_map/ppermute | solution.py:643
  141.9 17.3 %collective-permute-start.46 = (bf16[4,16,1664]{2,1,0:T(8,128)(2,1)S(1)}, bf16[4,16,1664]{2,1,0:T(8,128)(2,1)S(1)}, u32[]{:S(2)}, u32[]{:S(2)}) collective-permute-start(bf16[4,16,1664]{2,1,0:T(8,128)(2,1)S(1)} %get-tuple-element.320), channel_id=1, source_target_pairs={{0,1},{1,0},{2,3},{3,2},{4,5},{5,4},{6,7},{7,6},{8,9},{9,8},{10,11... | collective-permute-start | bytes 638984 | tf_op jit(solution)/shard_map/ppermute | solution.py:651
  149.1 14.8 %collective-permute-start.47 = (bf16[4,16,1664]{2,1,0:T(8,128)(2,1)S(1)}, bf16[4,16,1664]{2,1,0:T(8,128)(2,1)S(1)}, u32[]{:S(2)}, u32[]{:S(2)}) collective-permute-start(bf16[4,16,1664]{2,1,0:T(8,128)(2,1)S(1)} %get-tuple-element.321), channel_id=1, source_target_pairs={{0,5},{1,4},{2,7},{3,6},{4,1},{5,0},{6,3},{7,2},{8,13},{9,12},{10,... | collective-permute-start | bytes 638984 | tf_op jit(solution)/shard_map/ppermute | solution.py:654
  151.6 24.6 %collective-permute-start.44 = (bf16[256,512]{1,0:T(8,128)(2,1)S(1)}, bf16[256,512]{1,0:T(8,128)(2,1)S(1)}, u32[]{:S(2)}, u32[]{:S(2)}) collective-permute-start(bf16[256,512]{1,0:T(8,128)(2,1)S(1)} %get-tuple-element.317), channel_id=1, source_target_pairs={{0,4},{2,6},{4,0},{6,2},{8,12},{10,14},{12,8},{14,10},{16,20},{18,... | collective-permute-start | bytes 786440 | tf_op jit(solution)/shard_map/ppermute | solution.py:643
  153.8 22.3 %collective-permute-start.43 = (bf16[256,512]{1,0:T(8,128)(2,1)S(1)}, bf16[256,512]{1,0:T(8,128)(2,1)S(1)}, u32[]{:S(2)}, u32[]{:S(2)}) collective-permute-start(bf16[256,512]{1,0:T(8,128)(2,1)S(1)} %get-tuple-element.314), channel_id=1, source_target_pairs={{0,2},{2,0},{4,6},{6,4},{8,10},{10,8},{12,14},{14,12},{16,18},{18,... | collective-permute-start | bytes 786440 | tf_op jit(solution)/shard_map/ppermute | solution.py:640
  158.4 11.8 %collective-permute-start.54 = (bf16[9,16,512]{2,1,0:T(8,128)(2,1)S(1)}, bf16[9,16,512]{2,1,0:T(8,128)(2,1)S(1)}, u32[]{:S(2)}, u32[]{:S(2)}) collective-permute-start(bf16[9,16,512]{2,1,0:T(8,128)(2,1)S(1)} %get-tuple-element.335), channel_id=1, source_target_pairs={{0,16},{2,18},{4,20},{6,22},{8,24},{10,26},{12,28},{14,30},{16,0},... | collective-permute-start | bytes 442376 | tf_op jit(solution)/shard_map/ppermute | solution.py:646
  159.1 11.1 %collective-permute-start.55 = (bf16[9,16,512]{2,1,0:T(8,128)(2,1)S(1)}, bf16[9,16,512]{2,1,0:T(8,128)(2,1)S(1)}, u32[]{:S(2)}, u32[]{:S(2)}) collective-permute-start(bf16[9,16,512]{2,1,0:T(8,128)(2,1)S(1)} %get-tuple-element.336), channel_id=1, source_target_pairs={{0,8},{2,10},{4,12},{6,14},{8,16},{10,18},{12,20},{14,22},{16,24},... | collective-permute-start | bytes 442376 | tf_op jit(solution)/shard_map/ppermute | solution.py:646
  163.9 11.4 %collective-permute-start.52 = (bf16[9,16,512]{2,1,0:T(8,128)(2,1)S(1)}, bf16[9,16,512]{2,1,0:T(8,128)(2,1)S(1)}, u32[]{:S(2)}, u32[]{:S(2)}) collective-permute-start(bf16[9,16,512]{2,1,0:T(8,128)(2,1)S(1)} %get-tuple-element.334), channel_id=1, source_target_pairs={{0,24},{2,26},{4,28},{6,30},{8,0},{10,2},{12,4},{14,6},{16,8},{18,... | collective-permute-start | bytes 442376 | tf_op jit(solution)/shard_map/ppermute | solution.py:646
  170.2 7.2 %collective-permute-start.48 = (bf16[16,1664]{1,0:T(8,128)(2,1)S(1)}, bf16[16,1664]{1,0:T(8,128)(2,1)S(1)}, u32[]{:S(2)}, u32[]{:S(2)}) collective-permute-start(bf16[16,1664]{1,0:T(8,128)(2,1)S(1)} %get-tuple-element.322), channel_id=1, source_target_pairs={{0,24},{2,26},{4,28},{6,30},{8,0},{10,2},{12,4},{14,6},{16,8},{18,... | collective-permute-start | bytes 159752 | tf_op jit(solution)/shard_map/ppermute | solution.py:646
  170.2 7.3 %collective-permute-start.49 = (bf16[16,1664]{1,0:T(8,128)(2,1)S(1)}, bf16[16,1664]{1,0:T(8,128)(2,1)S(1)}, u32[]{:S(2)}, u32[]{:S(2)}) collective-permute-start(bf16[16,1664]{1,0:T(8,128)(2,1)S(1)} %get-tuple-element.323), channel_id=1, source_target_pairs={{0,16},{2,18},{4,20},{6,22},{8,24},{10,26},{12,28},{14,30},{16,0},... | collective-permute-start | bytes 159752 | tf_op jit(solution)/shard_map/ppermute | solution.py:646
  175.4 5.9 %collective-permute-start.50 = (bf16[16,1664]{1,0:T(8,128)(2,1)S(1)}, bf16[16,1664]{1,0:T(8,128)(2,1)S(1)}, u32[]{:S(2)}, u32[]{:S(2)}) collective-permute-start(bf16[16,1664]{1,0:T(8,128)(2,1)S(1)} %get-tuple-element.324), channel_id=1, source_target_pairs={{0,8},{2,10},{4,12},{6,14},{8,16},{10,18},{12,20},{14,22},{16,24},... | collective-permute-start | bytes 159752 | tf_op jit(solution)/shard_map/ppermute | solution.py:646
  (7 other events, 19.1 us)
where the time goes:
time: 186 us; the launch traced here: 183 us
  waiting for transfers between devices  68.7 us (37%)
  Pallas kernels  53.9 us (29%)
  starting transfers between devices  53.9 us (29%)
  other arithmetic  3.39 us (2%)
    pallas_call x28, Pallas kernels, call(): pl.pallas_call(body, out_shape=outs, in_specs=in_specs, out_specs=out_spe...  52.1 us
    ppermute x18, waiting for transfers between devices, turn_a(): lax.ppermute(v, 'rows', [(i, (i // PLANE + s) % A * PLANE + i % PLANE) fo...  40.5 us
    ppermute x18, starting transfers between devices, turn_a(): lax.ppermute(v, 'rows', [(i, (i // PLANE + s) % A * PLANE + i % PLANE) fo...  25.8 us
    ppermute x12, starting transfers between devices, swap_x(): return lax.ppermute(v, 'rows', [(i, i ^ 2) for i in range(R)])  13.4 us
    ppermute x8, waiting for transfers between devices, turn_f(): return lax.ppermute(v, 'fsdp', [(i, (i + t) % F) for i in range(F)])  10.4 us
    ppermute x12, waiting for transfers between devices, swap_x(): return lax.ppermute(v, 'rows', [(i, i ^ 2) for i in range(R)])  10.3 us
    ppermute x8, starting transfers between devices, turn_f(): return lax.ppermute(v, 'fsdp', [(i, (i + t) % F) for i in range(F)])  8.69 us
    ppermute x16, waiting for transfers between devices, swap_c(): return lax.ppermute(v, 'rows', [(i, i ^ 1) for i in range(R)])  4.49 us
  transfers between devices with their start and end apart: 56, of which 23 were waited for; matrix products, arithmetic and copies ran while one was open for 1% of the time, Pallas kernels for 19%

commit v1 on v0

v1 whole, which is shorter than its diff:
```python
import functools
import math

import jax
import jax.numpy as jnp
import numpy as np
from jax import lax
from jax.experimental import pallas as pl
from jax.experimental.pallas import tpu as pltpu
from jax.sharding import PartitionSpec as P

HEADS = 4
HEAD_DIM = 128
EPS = 1e-05
NEG = -1e30
PLANE = 4
MIB = 1024 * 1024
BF = jnp.bfloat16
F32 = jnp.float32
I32 = jnp.int32
SCALE = 1.0 / math.sqrt(HEAD_DIM)
SCALE2 = SCALE * math.log2(math.e)
GELU_A = math.sqrt(2.0 / math.pi)
GELU_B = 0.044715

VMEM = pl.BlockSpec(memory_space=pltpu.VMEM)
SMEM = pl.BlockSpec(memory_space=pltpu.SMEM)
HBM = pl.BlockSpec(memory_space=pltpu.HBM)
ANY = pl.BlockSpec(memory_space=pl.ANY)


def after(value, *others):
    return lax.optimization_barrier((value, *others))[0]


def together(*values):
    return lax.optimization_barrier(values)


def mm(left, right):
    return jnp.dot(left, right, preferred_element_type=F32)


def mm_nt(left, right):
    return lax.dot_general(left, right, (((1,), (1,)), ((), ())), preferred_element_type=F32)


def mm_tn(left, right):
    return lax.dot_general(left, right, (((0,), (0,)), ((), ())), preferred_element_type=F32)


def call(body, outs, ins, in_specs, out_specs, scratch=(), flops=0, moved=0, trans=0, vmem=16, name=None):
    return pl.pallas_call(
        body,
        out_shape=outs,
        in_specs=in_specs,
        out_specs=out_specs,
        scratch_shapes=scratch,
        compiler_params=pltpu.CompilerParams(vmem_limit_bytes=vmem * MIB),
        cost_estimate=pl.CostEstimate(
            flops=int(flops), bytes_accessed=int(moved), transcendentals=int(trans)
        ),
        name=name,
    )(*ins)


def normalize(values):
    centre = values - jnp.mean(values, axis=-1, keepdims=True)
    spread = jnp.mean(centre * centre, axis=-1, keepdims=True)
    inverse = lax.rsqrt(spread + EPS)
    return centre * inverse, inverse


def norm_back(grad_out, plain, inverse, gain):
    scaled = grad_out * gain
    return inverse * (
        scaled
        - jnp.mean(scaled, axis=-1, keepdims=True)
        - plain * jnp.mean(scaled * plain, axis=-1, keepdims=True)
    )


def table_of(tab, count, pos):
    low = jnp.zeros_like(pos) + tab[0]
    high = low + tab[count]
    finish = high + tab[2 * count]
    for t in range(1, count):
        here = pos >= tab[t]
        top = tab[t] + tab[count + t]
        low = jnp.where(here, tab[t], low)
        high = jnp.where(here, top, high)
        finish = jnp.where(here, top + tab[2 * count + t], finish)
    return low, high, finish


def pack_body(qkv_ref, out_ref, up_ref, down_ref, *refs):
    vec_refs, (q_ref, m_ref, vec_scr) = refs[:-3], refs[-3:]
    part, width = out_ref.shape
    blocks = up_ref.shape[1] // width
    vec_scr[...] = jnp.zeros(vec_scr.shape, F32)
    for k, ref in enumerate(vec_refs[:-1]):
        vec_scr[k : k + 1, :part] = ref[...].astype(F32)
    for j in range(blocks):
        vec_scr[8 + j : 9 + j, :part] = vec_refs[-1][:, j * part : (j + 1) * part].astype(F32)
    for i in range(3):
        q_ref[i] = qkv_ref[:, i * width : (i + 1) * width]
    q_ref[3] = jnp.zeros((part, width), BF)
    q_ref[3, :, :HEAD_DIM] = jnp.transpose(vec_scr[...])[:part].astype(BF)
    m_ref[0] = out_ref[...]
    for j in range(blocks):
        m_ref[1 + j] = up_ref[:, j * width : (j + 1) * width]
        m_ref[1 + blocks + j] = down_ref[j * part : (j + 1) * part, :]


def sum_body(*refs, plan, count):
    for out_ref, terms in zip(refs[count:], plan, strict=True):
        total = None
        for which, spot in terms:
            term = refs[which][spot].astype(F32)
            total = term if total is None else total + term
        out_ref[...] = total.astype(out_ref.dtype)


def join_body(*refs, plan, count):
    out_ref, row = refs[count], 0
    for terms in plan:
        total = None
        for which, spot in terms:
            term = refs[which][spot].astype(F32)
            total = term if total is None else total + term
        out_ref[row : row + total.shape[0]] = total.astype(out_ref.dtype)
        row += total.shape[0]


def join_up(arrays, plan):
    shapes = [jax.eval_shape(lambda v: v[terms[0][1]], arrays[terms[0][0]]).shape for terms in plan]
    shape = (sum(v[0] for v in shapes),) + shapes[0][1:]
    moved = math.prod(shape) * 4
    return call(
        functools.partial(join_body, plan=plan, count=len(arrays)), [jax.ShapeDtypeStruct(shape, BF)], arrays,
        [VMEM] * len(arrays), [VMEM], flops=moved, moved=moved, vmem=16, name="join",
    )


def lay_body(*refs, plan, count):
    out_ref, row = refs[count], 0
    width = out_ref.shape[2]
    for wide, terms in plan:
        total = None
        for which, spot in terms:
            term = refs[which][spot].astype(F32)
            total = term if total is None else total + term
        total = total.astype(out_ref.dtype)
        if wide:
            for j in range(-(-total.shape[1] // width)):
                piece = total[:, j * width : (j + 1) * width]
                if piece.shape[1] < width:
                    out_ref[row] = jnp.zeros(out_ref.shape[1:], out_ref.dtype)
                out_ref[row, :, : piece.shape[1]] = piece
                row += 1
        else:
            out_ref[row : row + total.shape[0]] = total
            row += total.shape[0]


def lay_out(arrays, plan, part, width):
    blocks = 0
    for wide, terms in plan:
        shape = jax.eval_shape(lambda v: v[terms[0][1]], arrays[terms[0][0]]).shape
        blocks += -(-shape[1] // width) if wide else shape[0]
    moved = blocks * part * width * 4
    return call(
        functools.partial(lay_body, plan=plan, count=len(arrays)), [jax.ShapeDtypeStruct((blocks, part, width), BF)],
        arrays, [VMEM] * len(arrays), [VMEM], flops=moved, moved=moved, vmem=8, name="lay",
    )[0]


def add_up(arrays, plan, dtype=BF):
    outs = []
    for terms in plan:
        which, spot = terms[0]
        outs.append(jax.ShapeDtypeStruct(jax.eval_shape(lambda v: v[spot], arrays[which]).shape, dtype))
    moved = sum(o.size for o in outs) * 4
    return call(
        functools.partial(sum_body, plan=plan, count=len(arrays)), outs, arrays,
        [VMEM] * len(arrays), [VMEM] * len(outs), flops=moved, moved=moved, vmem=16, name="add",
    )


def copy_body(*refs, plan, count):
    outs, sem = refs[count:-1], refs[-1]
    copies = []
    for k, (which, source, out, spot) in enumerate(plan):
        copies.append(pltpu.make_async_copy(refs[which].at[source], outs[out].at[spot], sem.at[k]))
        copies[-1].start()
    for copy in copies:
        copy.wait()


def copy_out(arrays, shapes, plan):
    moved = sum(math.prod(shape) for shape in shapes) * 4
    return call(
        functools.partial(copy_body, plan=plan, count=len(arrays)),
        [jax.ShapeDtypeStruct(shape, arrays[0].dtype) for shape in shapes], arrays,
        [HBM] * len(arrays), [VMEM] * len(shapes),
        scratch=[pltpu.SemaphoreType.DMA((len(plan),))], moved=moved, vmem=4, name="copy",
    )


def stack(arrays):
    shape = (len(arrays),) + arrays[0].shape
    every = (slice(None),)
    (out,) = copy_out(arrays, [shape], [(i, every, 0, (i,)) for i in range(len(arrays))])
    return out


def assemble_body(idx, *refs, rows, count):
    pieces, (w_ref, row_ref, col_ref, low_scr, sem) = refs[:count], refs[count:]
    k = 0
    for piece in pieces:
        for j in range(piece.shape[0]):
            at = pl.ds(pl.multiple_of(idx[k] * rows, rows), rows)
            pltpu.make_async_copy(piece.at[j, pl.ds(0, 3)], w_ref.at[:, at, :], sem.at[0]).start()
            pltpu.make_async_copy(piece.at[j, 3, :, pl.ds(0, HEAD_DIM)], low_scr.at[at, :], sem.at[1]).start()
            k += 1
    pltpu.make_async_copy(low_scr, low_scr, sem.at[1]).wait()
    columns = low_scr[...].astype(F32)
    col_ref[...] = columns
    row_ref[...] = jnp.transpose(columns)[: row_ref.shape[0]]
    pltpu.make_async_copy(w_ref, w_ref, sem.at[0]).wait()


def project_body(*refs, with_q, spots, count):
    pieces, (w_ref, row_ref), outs = refs[:count], refs[count : count + 2], refs[count + 2 :]
    kv_ref, n_ref = outs[:2]
    gain, shift = row_ref[0:1, :], row_ref[1:2, :]
    for i, (which, lead) in enumerate(spots):
        plain, unused_inverse = normalize(pieces[which][lead].astype(F32))
        n_ref[i] = plain.astype(BF)
        normed = (plain * gain + shift).astype(BF)
        keys = mm(normed, w_ref[1])
        values = mm(normed, w_ref[2]) + row_ref[3:4, :]
        for h in range(HEADS):
            lanes = slice(h * HEAD_DIM, (h + 1) * HEAD_DIM)
            kv_ref[i, h] = keys[:, lanes].astype(BF)
            kv_ref[i, HEADS + h] = values[:, lanes].astype(BF)
        if with_q and i == 0:
            queries = (mm(normed, w_ref[0]) + row_ref[2:3, :]) * SCALE2
            for h in range(HEADS):
                outs[2][h] = queries[:, h * HEAD_DIM : (h + 1) * HEAD_DIM].astype(BF)


def ready_body(idx, *refs, rows, count, part):
    pieces, (own_ref, tok_ref) = refs[:count], refs[count : count + 2]
    w_ref, row_ref, col_ref, up_ref, kv_ref, n_ref, q_ref, n_first, low_scr, sem = refs[count + 2 :]
    assemble_body(idx, *pieces, w_ref, row_ref, col_ref, low_scr, sem, rows=rows, count=count)
    width = up_ref.shape[1]
    blocks = up_ref.shape[0]
    per = width // blocks
    source = lax.broadcasted_iota(I32, (per, width), 0)
    target = lax.broadcasted_iota(I32, (per, width), 1)
    total = jnp.zeros((blocks, width), F32)
    for k in range(blocks):
        spread = jnp.where(
            target == (source // part) * (blocks * part) + k * part + lax.rem(source, part), 1.0, 0.0
        ).astype(BF)
        mine = [row_ref[8 + k : 9 + k, j * per : (j + 1) * per] for j in range(blocks)]
        total += mm(jnp.concatenate(mine, axis=0).astype(BF), spread)
    up_ref[...] = total
    spots = [(0, slice(None))] + [(1, i) for i in range(tok_ref.shape[0])]
    project_body(own_ref, tok_ref, w_ref, row_ref, kv_ref, n_ref, q_ref, with_q=True, spots=spots, count=2)
    n_first[0] = n_ref[0]


def reach(sc, tab, rows):
    count = tab.shape[0] // 3
    min_low, min_high, unused = table_of(tab, count, sc[0])
    max_low, max_high, unused = table_of(tab, count, sc[0] + PLANE * rows - 1)
    return min_low, max_high, max_low, min_high


def plane_rows(sc, rows, shape, dim):
    spot = lax.broadcasted_iota(I32, shape, dim)
    place = spot + sc[1]
    for b in range(1, PLANE):
        place = jnp.where(spot >= b * rows, spot + (sc[1 + b] - b * rows), place)
    return place


def attend_body(sc, tab, *refs, kv_units):
    q_refs, kv_refs = refs[:PLANE], refs[PLANE:-8]
    keep_ref, send_ref, q_scr, s_scr, m_scr, acc_scr, kv_ref, sem = refs[-8:]
    count = tab.shape[0] // 3
    units, unused, rows, unused = kv_ref.shape
    k = 0
    for ref in kv_refs:
        for i in range(ref.shape[0]):
            pltpu.make_async_copy(ref.at[i], kv_ref.at[kv_units[k]], sem.at[kv_units[k]]).start()
            k += 1
    min_low, max_high, max_low, min_high = reach(sc, tab, rows)
    q_pos = plane_rows(sc, rows, (PLANE * rows, 1), 0)
    low, high, unused = table_of(tab, count, q_pos)
    ones = jnp.ones((rows, HEAD_DIM), BF)
    for b, ref in enumerate(q_refs):
        q_scr[:, b * rows : (b + 1) * rows] = ref[...]
    m_scr[...] = jnp.full(m_scr.shape, NEG, F32)
    acc_scr[...] = jnp.zeros(acc_scr.shape, F32)

    def keep_scores(u, allowed):
        for h in range(HEADS):
            scores = mm_nt(q_scr[h], kv_ref[u, h])
            if allowed is not None:
                scores = jnp.where(allowed, scores, NEG)
            s_scr[u, h] = scores
            top = m_scr[h]
            for j in range(rows // HEAD_DIM):
                top = jnp.maximum(top, scores[:, j * HEAD_DIM : (j + 1) * HEAD_DIM])
            m_scr[h] = top

    def score_step(u, carry):
        start = sc[1 + PLANE + u]
        pltpu.make_async_copy(kv_refs[0].at[0], kv_ref.at[u], sem.at[u]).wait()
        needed = (start < max_high) & (start + rows > min_low)
        whole = (start >= max_low) & (start + rows <= min_high)

        @pl.when(needed & whole)
        def _():
            keep_scores(u, None)

        @pl.when(needed & jnp.logical_not(whole))
        def _():
            k_pos = start + lax.broadcasted_iota(I32, (1, rows), 1)
            keep_scores(u, (k_pos >= low) & (k_pos < high))

        return carry

    lax.fori_loop(0, units, score_step, 0)
    for h in range(HEADS):
        top = jnp.max(m_scr[h], axis=-1, keepdims=True)
        m_scr[h] = jnp.broadcast_to(jnp.where(top > 0.5 * NEG, top, 0.0), m_scr.shape[1:])

    def value_step(u, carry):
        start = sc[1 + PLANE + u]
        needed = (start < max_high) & (start + rows > min_low)

        @pl.when(needed)
        def _():
            for h in range(HEADS):
                soft = jnp.exp2(s_scr[u, h] - m_scr[h][:, :1]).astype(BF)
                wide = jnp.concatenate([kv_ref[u, HEADS + h], ones], axis=1)
                acc_scr[h] += mm(soft, wide)

        return carry

    lax.fori_loop(0, units, value_step, 0)
    lane = lax.broadcasted_iota(I32, (1, HEAD_DIM), 1)
    width = HEADS * HEAD_DIM
    for b in range(PLANE):
        ref, spot = (keep_ref, send_ref)[b % 2], b // 2
        at = slice(b * rows, (b + 1) * rows)
        logs = jnp.zeros((rows, HEAD_DIM), F32)
        for h in range(HEADS):
            total = acc_scr[h, at, HEAD_DIM:]
            some = total > 0.0
            safe = jnp.where(some, total, 1.0)
            ref[spot, :, h * HEAD_DIM : (h + 1) * HEAD_DIM] = acc_scr[h, at, :HEAD_DIM] / safe
            logs = jnp.where(lane == h, jnp.where(some, m_scr[h, at] + jnp.log2(safe), NEG), logs)
        ref[spot, :, width:] = logs


def in_parts(value, lane, first):
    out = jnp.zeros((value[0].shape[0], HEAD_DIM), F32)
    for h, column in enumerate(value):
        high = column.astype(BF).astype(F32)
        rest = column - high
        middle = rest.astype(BF).astype(F32)
        for i, part in enumerate((high, middle, rest - middle)):
            out = jnp.where(lane == first + i * HEADS + h, part, out)
    return out


def merge_body(mine_ref, other_ref, own_ref, far_ref):
    width = HEADS * HEAD_DIM
    lane = lax.broadcasted_iota(I32, (1, HEAD_DIM), 1)
    for b in range(2):
        lse_mine, lse_other = mine_ref[b, :, width:], other_ref[b, :, width:]
        top = jnp.maximum(lse_mine, lse_other)
        share_mine, share_other = jnp.exp2(lse_mine - top), jnp.exp2(lse_other - top)
        share = share_mine + share_other
        log_total = top + jnp.log2(share)
        share_mine, share_other = share_mine / share, share_other / share
        for h in range(HEADS):
            lanes = slice(h * HEAD_DIM, (h + 1) * HEAD_DIM)
            mixed = mine_ref[b, :, lanes] * share_mine[:, h : h + 1] + other_ref[b, :, lanes] * share_other[:, h : h + 1]
            if b == 0:
                own_ref[:, lanes] = mixed
            else:
                far_ref[:, lanes] = mixed.astype(BF)
        if b == 0:
            own_ref[:, width:] = log_total
        else:
            columns = [log_total[:, h : h + 1] for h in range(HEADS)]
            far_ref[:, width:] = in_parts(columns, lane, 0).astype(BF)


def middle_body(idx, sc, tab, *refs, rows, m_count, grad_count):
    m_refs, (tok_ref, own_ref, other_ref, cot_ref, row_ref, up_row_ref) = refs[:m_count], refs[m_count : m_count + 6]
    outs = refs[m_count + 6 :]
    out_ref, dmid_ref, d_ref, vec_ref = outs[:4]
    g_refs = outs[4 : 4 + grad_count]
    (w_out, w_up, w_down, g_out, g_up, g_down, dh_scr, sem, g_sem) = outs[4 + grad_count :]
    blocks, width = w_up.shape[0], w_up.shape[2]
    pieces = w_down.shape[0] // blocks
    count = tab.shape[0] // 3
    local = tok_ref.shape[0]
    spots = []
    for m_ref in m_refs:
        for spot in range(m_ref.shape[0]):
            owner = idx[len(spots)]
            spots.append(
                (m_ref, spot, pl.ds(pl.multiple_of(owner * rows, rows), rows), pl.ds(owner * blocks, blocks))
            )
    for m_ref, spot, at, unused in spots:
        pltpu.make_async_copy(m_ref.at[spot, 0], w_out.at[at, :], sem.at[0]).start()
    for m_ref, spot, unused, at in spots:
        pltpu.make_async_copy(m_ref.at[spot, pl.ds(1 + blocks, blocks)], w_down.at[at], sem.at[2]).start()
    for m_ref, spot, at, unused in spots:
        pltpu.make_async_copy(m_ref.at[spot, pl.ds(1, blocks)], w_up.at[:, at, :], sem.at[1]).start()

    pos = sc[1] + lax.broadcasted_iota(I32, (local, 1), 0)
    unused_low, unused_high, finish = table_of(tab, count, pos)
    live = (pos < finish).astype(F32)
    gain, shift = row_ref[5:6, :], row_ref[6:7, :]
    lane = lax.broadcasted_iota(I32, (1, HEAD_DIM), 1)
    logs, mixed = [], []
    for h in range(HEADS):
        lanes = slice(h * HEAD_DIM, (h + 1) * HEAD_DIM)
        lse_own = own_ref[:, width + h : width + h + 1]
        lse_other = sum(
            other_ref[:, width + i * HEADS + h : width + i * HEADS + h + 1].astype(F32) for i in range(3)
        )
        top = jnp.maximum(lse_own, lse_other)
        share_own, share_other = jnp.exp2(lse_own - top), jnp.exp2(lse_other - top)
        share = share_own + share_other
        logs.append(top + jnp.log2(share))
        mixed.append(
            own_ref[:, lanes] * (share_own / share) + other_ref[:, lanes].astype(F32) * (share_other / share)
        )
    mixed = jnp.concatenate(mixed, axis=1)
    attended = (mixed * live).astype(BF)
    cot = cot_ref[...]
    pltpu.make_async_copy(w_out, w_out, sem.at[0]).wait()
    middle = tok_ref[...].astype(F32) + mm(attended, w_out[...]) + row_ref[4:5, :]
    pltpu.make_async_copy(w_down, w_down, sem.at[2]).wait()
    for j in range(blocks):
        dh_scr[j] = mm_nt(cot, w_down[j * pieces : (j + 1) * pieces].reshape(width, width))
    plain, inverse = normalize(middle)
    normed = (plain * gain + shift).astype(BF)
    pltpu.make_async_copy(w_up, w_up, sem.at[1]).wait()
    total = middle + row_ref[7:8, :]
    d_norm = jnp.zeros(middle.shape, F32)
    ones = jnp.ones((8, local), BF)
    up_sums = []
    for j in range(blocks):
        up = w_up[j]
        down = w_down[j * pieces : (j + 1) * pieces].reshape(width, width)
        pre = mm(normed, up) + up_row_ref[j : j + 1, :]
        square = pre * pre
        t = jnp.tanh(GELU_A * pre * (1.0 + GELU_B * square))
        half = 0.5 * (1.0 + t)
        hidden = (pre * half).astype(BF)
        slope = half + 0.5 * pre * (1.0 - t * t) * (GELU_A * (1.0 + 3.0 * GELU_B * square))
        total = total + mm(hidden, down)
        d_pre = (dh_scr[j] * slope).astype(BF)
        d_norm = d_norm + mm_nt(d_pre, up)
        g_down[j * pieces : (j + 1) * pieces] = mm_tn(hidden, cot).astype(BF).reshape(pieces, rows, width)
        g_up[j] = mm_tn(normed, d_pre).astype(BF)
        up_sums.append(mm(ones, d_pre)[0:1])
    g_pieces = g_refs[0].shape[0]
    spots = []
    for i in range(pieces):
        g_ref, spot, where = g_refs[i // g_pieces], i % g_pieces, idx[pieces + i]
        spots.append((g_ref, spot, pl.ds(pl.multiple_of(where * rows, rows), rows)))
        at = pl.ds(where * blocks, blocks)
        pltpu.make_async_copy(g_down.at[at], g_ref.at[spot, pl.ds(1 + blocks, blocks)], g_sem).start()
    for g_ref, spot, at in spots:
        pltpu.make_async_copy(g_up.at[:, at, :], g_ref.at[spot, pl.ds(1, blocks)], g_sem).start()
    out_ref[...] = total.astype(BF)
    cot_f = cot.astype(F32)
    d_middle = cot_f + norm_back(d_norm, plain, inverse, gain)
    dmid_ref[...] = d_middle
    d_branch = d_middle.astype(BF)
    g_out[...] = mm_tn(attended, d_branch).astype(BF)
    for g_ref, spot, at in spots:
        pltpu.make_async_copy(g_out.at[at, :], g_ref.at[spot, 0], g_sem).start()
    d_att = mm_nt(d_branch, w_out[...]).astype(BF) * live.astype(BF)
    d_ref[:, :width] = d_att
    product = d_att.astype(F32) * mixed
    deltas = [
        jnp.sum(product[:, h * HEAD_DIM : (h + 1) * HEAD_DIM], axis=-1, keepdims=True) for h in range(HEADS)
    ]
    d_ref[:, width:] = (in_parts(deltas, lane, 0) + in_parts(logs, lane, 3 * HEADS)).astype(BF)

    sums = [jnp.sum(v, axis=0, keepdims=True) for v in (d_middle, d_norm * plain, d_norm, cot_f)]
    sums = jnp.concatenate(sums + up_sums + [jnp.zeros((HEAD_DIM - 4 - blocks, width), F32)], axis=0)
    columns = jnp.transpose(sums)
    if pieces > 1:
        per = pieces // blocks
        vec_ref[...] = jnp.where(lane < 4, columns, 0.0)
        for j in range(blocks):
            column = jnp.broadcast_to(columns[:, 4 + j : 5 + j], (width, HEAD_DIM)).reshape(
                per, blocks, rows, HEAD_DIM
            )
            wide_lane = lane.reshape(1, 1, HEAD_DIM)
            placed = sum(jnp.where(wide_lane == 4 + i, column[:, i], 0.0) for i in range(blocks))
            vec_ref[j * per * rows : (j + 1) * per * rows, :] += placed.reshape(per * rows, HEAD_DIM)
    else:
        vec_ref[...] = jnp.where(lane < 4 + blocks, columns, 0.0)
    for g_ref in g_refs:
        pltpu.make_async_copy(g_ref, g_ref, g_sem).wait()


def back_unit(sc, tab, plane, kv_ref, spot, q_ref, do_refs, stat_refs, dq_refs, put, none):
    count = tab.shape[0] // 3
    rows = kv_ref.shape[2]
    min_low, max_high, max_low, min_high = reach(sc, tab, rows)
    low, high, unused = table_of(tab, count, plane_rows(sc, rows, (1, PLANE * rows), 1))
    start = sc[1 + PLANE + plane]
    needed = (start < max_high) & (start + rows > min_low)
    whole = (start >= max_low) & (start + rows <= min_high)

    def unit(masked):
        k_pos = start + lax.broadcasted_iota(I32, (rows, 1), 0)
        for h in range(HEADS):
            key, value = kv_ref[spot, h], kv_ref[spot, HEADS + h]
            d_key, d_value = 0.0, 0.0
            for half in do_refs:
                at = slice(2 * half * rows, 2 * (half + 1) * rows)
                q, do, stat_ref = q_ref[h, at], do_refs[half][h], stat_refs[half]
                soft = jnp.exp2(mm_nt(key, q) - stat_ref[HEADS + h : HEADS + h + 1, :])
                if masked:
                    soft = jnp.where((k_pos >= low[:, at]) & (k_pos < high[:, at]), soft, 0.0)
                d_soft = mm_nt(value, do)
                d_scores = (soft * (d_soft - stat_ref[h : h + 1, :])).astype(BF)
                d_value = d_value + mm(soft.astype(BF), do)
                d_key = d_key + mm(d_scores, q)
                dq_refs[half][h] += mm_tn(key, d_scores)
            put(slice(h * HEAD_DIM, (h + 1) * HEAD_DIM), d_key * (SCALE / SCALE2))
            put(slice((HEADS + h) * HEAD_DIM, (HEADS + h + 1) * HEAD_DIM), d_value)

    @pl.when(needed & whole)
    def _():
        unit(False)

    @pl.when(needed & jnp.logical_not(whole))
    def _():
        unit(True)

    @pl.when(jnp.logical_not(needed))
    def _():
        none()


def unpack_rows(packets, do_ref, stat_ref):
    rows, width = packets[0].shape[0], HEADS * HEAD_DIM
    for b, ref in enumerate(packets):
        at = slice(b * rows, (b + 1) * rows)
        for h in range(HEADS):
            do_ref[h, at] = ref[:, h * HEAD_DIM : (h + 1) * HEAD_DIM]
        tail = jnp.transpose(ref[:, width:].astype(F32))
        parts = [tail[i * HEADS : (i + 1) * HEADS] for i in range(6)]
        stat_ref[:, at] = jnp.concatenate([parts[0] + parts[1] + parts[2], parts[3] + parts[4] + parts[5]], axis=0)


def open_body(sc, tab, q_ref, d_own, d_c, kv_ref, do_ref, stat_ref, dq_ref, part_ref, *, units):
    unpack_rows((d_own, d_c), do_ref, stat_ref)
    dq_ref[...] = jnp.zeros(dq_ref.shape, F32)
    for j, (plane, spot) in enumerate(units):

        def put(lanes, value, j=j):
            part_ref[j, :, lanes] = value

        def none(j=j):
            part_ref[j] = jnp.zeros(part_ref.shape[1:], F32)

        back_unit(sc, tab, plane, kv_ref, spot, q_ref, {0: do_ref}, {0: stat_ref}, {0: dq_ref}, put, none)


def keep_planes(units, n_ref, w_ref, d_refs, nk_ref, sum_ref, nk_in, sum_in, dkv_scr):
    width = w_ref.shape[1]
    ones = jnp.ones((8, dkv_scr.shape[1]), BF)
    product = 0.0 if nk_in is None else nk_in[...]
    sums = 0.0 if sum_in is None else sum_in[...]
    for j, (unused, spot) in enumerate(units):
        d_refs[j][...] = (mm_nt(dkv_scr[j, :, :width], w_ref[1]) + mm_nt(dkv_scr[j, :, width:], w_ref[2])).astype(BF)
        product = product + mm_tn(n_ref[spot], dkv_scr[j])
        sums = sums + mm(ones, dkv_scr[j])
    nk_ref[...] = product
    sum_ref[...] = sums


def close_body(
    sc, tab, q_ref, d_x, d_xc, kv_ref, n_ref, w_ref, part_ref, do_ref, stat_ref, dq_ref, nk_ref, sum_ref, *refs, units
):
    d_refs, dkv_scr = refs[:-1], refs[-1]
    unpack_rows((d_x, d_xc), do_ref, stat_ref)
    dq_ref[...] = jnp.zeros(dq_ref.shape, F32)
    for j, (plane, spot) in enumerate(units):

        def put(lanes, value, j=j):
            dkv_scr[j, :, lanes] = (part_ref[j, :, lanes] + value).astype(BF)

        def none(j=j):
            dkv_scr[j] = jnp.zeros(dkv_scr.shape[1:], BF)

        back_unit(sc, tab, plane, kv_ref, spot, q_ref, {1: do_ref}, {1: stat_ref}, {1: dq_ref}, put, none)
    keep_planes(units, n_ref, w_ref, d_refs, nk_ref, sum_ref, None, None, dkv_scr)


def back_body(
    sc, tab, q_ref, do_one, do_two, stat_one, stat_two, kv_ref, n_ref, w_ref, one_in, two_in, nk_in, sum_in,
    d_ref, one_ref, two_ref, nk_ref, sum_ref, dkv_scr, *, unit,
):
    one_ref[...] = one_in[...]
    two_ref[...] = two_in[...]

    def put(lanes, value):
        dkv_scr[0, :, lanes] = value.astype(BF)

    def none():
        dkv_scr[0] = jnp.zeros(dkv_scr.shape[1:], BF)

    halves = {0: do_one, 1: do_two}, {0: stat_one, 1: stat_two}, {0: one_ref, 1: two_ref}
    back_unit(sc, tab, unit[0], kv_ref, unit[1], q_ref, *halves, put, none)
    keep_planes([unit], n_ref, w_ref, [d_ref], nk_ref, sum_ref, nk_in, sum_in, dkv_scr)


def query_block(dq_refs, b, rows):
    ref, at = dq_refs[b // 2], slice((b % 2) * rows, (b % 2 + 1) * rows)
    return jnp.concatenate([ref[h, :, at] * SCALE for h in range(HEADS)], axis=0).astype(BF)


def message_body(idx, *refs, rows):
    n_refs, dq_refs = refs[:PLANE], refs[PLANE : PLANE + 2]
    (nk_ref, sum_ref, w_ref, col_ref, vec_ref), (full, vec) = refs[PLANE + 2 : PLANE + 7], refs[-2:]
    msg_refs = refs[PLANE + 7 : -2]
    local = n_refs[0].shape[1]
    width = w_ref.shape[1]
    q_product = jnp.zeros((width, width), F32)
    q_sums = jnp.zeros((8, width), F32)
    ones = jnp.ones((8, local), BF)
    for b, n_ref in enumerate(n_refs):
        d_query = query_block(dq_refs, b, local)
        q_product += lax.dot_general(n_ref[0], d_query, (((0,), (1,)), ((), ())), preferred_element_type=F32)
        q_sums += mm_nt(ones, d_query)
    gain, shift = col_ref[:, 0:1], col_ref[:, 1:2]
    lane = lax.broadcasted_iota(I32, (1, HEAD_DIM), 1)
    gain_grad = jnp.zeros((width, 1), F32)
    shift_grad = jnp.zeros((width, 1), F32)
    columns = []
    for i in range(3):
        lanes = slice(i * width, (i + 1) * width)
        if i == 0:
            product, sums = q_product, q_sums[0:1]
        else:
            at = slice((i - 1) * width, i * width)
            product, sums = nk_ref[:, at], sum_ref[0:1, at]
        weight = w_ref[i].astype(F32)
        full[:, lanes] = (product * gain + shift * sums).astype(BF)
        gain_grad += jnp.sum(product * weight, axis=-1, keepdims=True)
        shift_grad += jnp.sum(weight * sums, axis=-1, keepdims=True)
        if i != 1:
            columns.append(jnp.transpose(jnp.broadcast_to(sums, (HEAD_DIM, width))))
    vec[...] = vec_ref[...]
    for at, column in ((8, gain_grad), (9, shift_grad), (10, columns[0]), (11, columns[1])):
        vec[...] += jnp.where(lane == at, column, 0.0)
    full[:, 3 * width :] = vec[...].astype(BF)
    k = 0
    for msg_ref in msg_refs:
        for i in range(msg_ref.shape[0]):
            msg_ref[i] = full[pl.ds(pl.multiple_of(idx[k] * rows, rows), rows), :]
            k += 1


def query_body(dq_one, dq_two, w_ref, keep_ref, send_ref):
    rows = keep_ref.shape[1]
    for b in range(PLANE):
        d_query = query_block((dq_one, dq_two), b, rows)
        out = lax.dot_general(d_query, w_ref[0], (((0,), (1,)), ((), ())), preferred_element_type=F32)
        (keep_ref, send_ref)[b % 2][b // 2] = out.astype(BF)


def finish_body(tok_ref, dmid_ref, row_ref, last_ref, *refs):
    plain, inverse = normalize(tok_ref[...].astype(F32))
    lines = 0 if len(last_ref.shape) == 2 else tok_ref.shape[0] // last_ref.shape[1]
    last = last_ref[:lines].reshape(tok_ref.shape) if lines else last_ref[...]
    total = last.astype(F32)
    for ref in refs[:-1]:
        total = total + ref[...].astype(F32)
    refs[-1][...] = (dmid_ref[...] + norm_back(total, plain, inverse, row_ref[0:1, :])).astype(BF)


def matrices_body(*refs, starts):
    terms, (out_ref, up_ref, down_ref) = refs[:-3], refs[-3:]
    width = out_ref.shape[1]
    part = out_ref.shape[0]
    blocks = up_ref.shape[1] // width

    def block(i):
        total = terms[0][starts[0] + i].astype(F32)
        for term, start in zip(terms[1:], starts[1:], strict=True):
            total = total + term[start + i].astype(F32)
        return total

    out_ref[...] = block(0)
    for j in range(blocks):
        up_ref[:, j * width : (j + 1) * width] = block(1 + j)
        down_ref[j * part : (j + 1) * part, :] = block(1 + blocks + j)


def unpack_body(*refs, w_blocks):
    terms, (qkv_ref, *vec_refs, up_ref, pad_ref) = refs[:-11], refs[-11:]
    total = terms[0][...]
    for term in terms[1:]:
        line = jnp.concatenate([term[j] for j in range(w_blocks)], axis=1)
        total = total + line[:, : total.shape[1]].astype(F32)
    width = qkv_ref.shape[1]
    part = qkv_ref.shape[0]
    qkv_ref[...] = total[:, :width]
    pad_ref[...] = jnp.zeros(pad_ref.shape, F32)
    pad_ref[:part] = total[:, width:]
    rows = jnp.transpose(pad_ref[...])
    for ref, row in zip(vec_refs, (8, 9, 10, 11, 0, 1, 2, 3), strict=True):
        ref[...] = rows[row : row + 1, :part]
    up_ref[...] = rows[4 : 4 + up_ref.shape[0], :part]


def shards(
    tokens, w_qkv, w_out, w_up, w_down,
    norm1_gain, norm1_bias, query_bias, value_bias, out_bias, norm2_gain, norm2_bias, up_bias, down_bias,
    cotangent, table_start, support_count, query_count, *, R, F,
):
    A = R // PLANE
    count = R * F
    local, width = tokens.shape[1], tokens.shape[2]
    part = w_qkv.shape[0]
    hidden = w_up.shape[1]
    blocks = hidden // width
    aligned = part % 16 == 0
    rows = part if aligned else width
    pieces = count if aligned else 1
    sds = jax.ShapeDtypeStruct

    r, f = lax.axis_index("rows"), lax.axis_index("fsdp")
    a, x, c = r // PLANE, (r // 2) % 2, r % 2

    def swap_c(v):
        return lax.ppermute(v, "rows", [(i, i ^ 1) for i in range(R)])

    def swap_x(v):
        return lax.ppermute(v, "rows", [(i, i ^ 2) for i in range(R)])

    def turn_a(v, s):
        return lax.ppermute(
            v, "rows", [(i, ((i // PLANE + s) % A) * PLANE + i % PLANE) for i in range(R)]
        )

    def turn_f(v, t):
        return lax.ppermute(v, "fsdp", [(i, (i + t) % F) for i in range(F)])

    def turn_xf(v, t):
        return lax.ppermute(
            v, ("rows", "fsdp"),
            [(i * F + j, (i ^ 2) * F + (j + t) % F) for i in range(R) for j in range(F)],
        )

    def owners(order):
        cr, t, xr, s = (np.array(list(z), np.int32) for z in zip(*order, strict=True))
        plane = lax.rem(a - s + A, A)
        return (((plane * 2 + (x ^ xr)) * 2 + (c ^ cr)) * F + lax.rem(f - t + F, F)).astype(I32)

    block_x, block_c = np.array([0, 0, 1, 1], np.int32), np.array([0, 1, 0, 1], np.int32)
    block_start = (a * 4 + (x ^ block_x) * 2 + (c ^ block_c)) * local
    unit_start = (lax.rem(a - np.arange(A, dtype=np.int32) + A, A) * 4 + 2 * x + c) * local
    sc = jnp.concatenate([(a * 4 * local)[None], block_start, unit_start]).astype(I32)
    tab = jnp.concatenate([table_start[0], support_count[0], query_count[0]])
    q_order = [(cr, t, xr, s) for cr in range(2) for t in range(F) for xr in range(2) for s in range(A)]
    parts = [slice(0, A // 2), slice(A // 2, A)]
    m_order = [
        (cr, t, xr, s)
        for cr in range(2)
        for planes in (range(2, A), range(2))
        for xr, t in [(0, 0), (1, 0)] + [(0, t) for t in range(1, F)] + [(1, t) for t in range(1, F)]
        for s in planes
    ]
    every_owner = owners(q_order + m_order)
    q_owner, m_owner = every_owner[:count], every_owner[count:]
    if aligned:
        q_idx, idx = q_owner, jnp.concatenate([m_owner, q_owner])
    else:
        q_idx, idx = jnp.zeros((1,), I32), jnp.zeros((2,), I32)

    near = list(range(1, A))
    early, late = near[:2], near[2:]
    own = tokens[0]
    vectors = [
        v.reshape(1, -1)
        for v in (
            norm1_gain, norm1_bias, query_bias, value_bias, out_bias, norm2_gain, norm2_bias, down_bias, up_bias
        )
    ]
    wide = 3 * width + HEAD_DIM
    pack_in = [w_qkv, w_out, w_up, w_down, *vectors]
    q_own, m_own = pl.pallas_call(
        pack_body,
        grid=(1,),
        out_shape=[sds((4, part, width), BF), sds((1 + 2 * blocks, part, width), BF)],
        in_specs=[pl.BlockSpec(v.shape, lambda i: (0, 0)) for v in pack_in],
        out_specs=[VMEM] * 2,
        scratch_shapes=[pltpu.VMEM((HEAD_DIM, HEAD_DIM), F32)],
        compiler_params=pltpu.CompilerParams(vmem_limit_bytes=56 * MIB),
        cost_estimate=pl.CostEstimate(flops=0, bytes_accessed=16 * part * width, transcendentals=0),
        name="pack",
    )(*pack_in)
    tok_z, m_z = {0: own}, {0: m_own}
    *q_z, tok_z[1], m_z[1], sc, tab, q_idx, idx = together(
        *(turn_a(q_own, s) for s in range(1, A)), turn_a(own, 1), turn_a(m_own, 1), sc, tab, q_idx, idx
    )
    q_z = jnp.stack([q_own] + q_z)
    moved = [swap_x(q_z)] + [v for t in range(1, F) for v in (turn_f(q_z, t), turn_xf(q_z, t))]
    *q_far, tok_z[2], m_z[2] = together(*moved, turn_a(tok_z[1], 1), turn_a(m_z[1], 1))
    tok_early, m_early = jnp.stack([tok_z[1], tok_z[2]]), jnp.stack([m_z[0], m_z[1]])
    early_x, early_f = swap_x(m_early), [turn_f(m_early, t) for t in range(1, F)]
    tok_z[3], m_z[3] = turn_a(tok_z[2], 1), turn_a(m_z[2], 1)
    q_four = jnp.stack([q_z] + q_far)
    q_other = swap_c(q_four)
    q_pieces = [q_four.reshape(count // 2, 4, part, width), q_other.reshape(count // 2, 4, part, width)]
    if not aligned:
        stacked = jnp.concatenate(q_pieces)
        by_owner = jnp.zeros_like(stacked).at[q_owner].set(stacked)
        q_pieces = [by_owner.transpose(1, 0, 2, 3).reshape(1, 4, width, width)]
    key_shape = (2 * HEADS, local, HEAD_DIM)
    w_all, row_vec, col_vec, up_row, kv_early, n_early, q, n_first = call(
        functools.partial(ready_body, rows=rows, count=len(q_pieces), part=part),
        [
            sds((3, width, width), BF), sds((16, width), F32), sds((width, HEAD_DIM), F32), sds((blocks, width), F32),
            sds((3,) + key_shape, BF), sds((3, local, width), BF), sds((HEADS, local, HEAD_DIM), BF),
            sds((1, local, width), BF),
        ],
        [q_idx, *q_pieces, own, tok_early], [SMEM] + [HBM] * len(q_pieces) + [VMEM] * 2, [VMEM] * 8,
        scratch=[pltpu.VMEM((width, HEAD_DIM), BF), pltpu.SemaphoreType.DMA((2,))],
        flops=4 * (A + 1) * local * width * width, moved=4 * width * wide, vmem=12, name="ready",
    )

    tok_z[3], m_z[3], early_x, q_x, *early_f = together(tok_z[3], m_z[3], early_x, swap_x(q), *early_f)
    for s in range(4, A):
        tok_z[s], m_z[s] = together(turn_a(tok_z[s - 1], 1), turn_a(m_z[s - 1], 1))
    q_blocks = [q, swap_c(q), q_x, swap_c(q_x)]
    late = list(range(3, A))
    tok_late = jnp.stack([tok_z[s] for s in late]) if A > 4 else tok_z[3][None]
    m_late = stack([m_z[s] for s in range(2, A)])
    late_x, late_f = swap_x(m_late), [turn_f(m_late, t) for t in range(1, F)]
    early_xf = [turn_f(early_x, t) for t in range(1, F)]
    kv_late, n_late = call(
        functools.partial(project_body, with_q=False, spots=[(0, i) for i in range(len(late))], count=1),
        [sds((len(late),) + key_shape, BF), sds((len(late), local, width), BF)],
        [after(tok_late, m_late), w_all, row_vec], [VMEM] * 3, [VMEM] * 2,
        flops=4 * len(late) * local * width * width, moved=8 * len(late) * local * width, vmem=8, name="project",
    )
    where = {s: (kv_early, n_early, s) if s < 3 else (kv_late, n_late, s - 3) for s in range(A)}

    unit = PLANE * local
    work = 4 * unit * A * local * width
    packet = width + HEAD_DIM
    att_keep, att_send, q_plane = call(
        functools.partial(attend_body, kv_units=list(range(A))),
        [sds((2, local, packet), F32)] * 2 + [sds((HEADS, unit, HEAD_DIM), BF)],
        [sc, tab, *q_blocks, kv_early, kv_late], [SMEM, SMEM] + [VMEM] * PLANE + [ANY] * 2, [VMEM] * 3,
        scratch=[
            pltpu.VMEM((A, HEADS, unit, local), F32),
            pltpu.VMEM((HEADS, unit, HEAD_DIM), F32), pltpu.VMEM((HEADS, unit, 2 * HEAD_DIM), F32),
            pltpu.VMEM((A, 2 * HEADS, local, HEAD_DIM), BF), pltpu.SemaphoreType.DMA((A,)),
        ],
        flops=work, moved=8 * A * local * width, trans=HEADS * unit * A * local, vmem=10 + 5 * A, name="attend",
    )
    early_side = [m_early, early_x, *early_f]
    att_keep, att_send, late_x, *more = together(
        att_keep, att_send, late_x, *late_f, *(swap_c(v) for v in early_side[:2])
    )
    late_f, early_c = list(more[: F - 1]), list(more[F - 1 :])
    att_recv = swap_c(att_send)
    late_xf = [turn_f(late_x, t) for t in range(1, F)]
    att_own, att_far = call(
        merge_body, [sds((local, packet), F32), sds((local, packet), BF)], [att_keep, att_recv], [VMEM] * 2,
        [VMEM] * 2, flops=32 * local * packet, moved=20 * local * packet, vmem=8, name="merge",
    )
    late_side = [m_late, late_x, *late_f]
    att_other, *more = together(
        swap_x(att_far), *late_xf, *(swap_c(v) for v in [*early_f, *early_xf, *late_side])
    )
    late_xf, more = list(more[: F - 1]), list(more[F - 1 :])
    early_c += more[: 2 * F - 2]
    late_c = more[2 * F - 2 :] + [swap_c(v) for v in late_xf]
    m_arrays = late_side + late_xf + early_side + early_xf + late_c + early_c
    if not aligned:
        stacked = jnp.concatenate(m_arrays)
        by_owner = jnp.zeros_like(stacked).at[m_owner].set(stacked)
        m_arrays = [
            jnp.concatenate(
                [
                    by_owner[:, 0].reshape(1, width, width),
                    by_owner[:, 1 : 1 + blocks].transpose(1, 0, 2, 3).reshape(blocks, width, width),
                    by_owner[:, 1 + blocks :].reshape(blocks, width, width),
                ]
            )[None]
        ]

    spots = [(t, xr) for t in range(F) for xr in range(2)]
    grad_count = 4 * F if aligned else 1
    g_shape = sds((pieces // grad_count, 1 + 2 * blocks, rows, width), BF)
    got = call(
        functools.partial(middle_body, rows=rows, m_count=len(m_arrays), grad_count=grad_count),
        [
            sds((local, width), BF), sds((local, width), F32), sds((local, packet), BF), sds((width, HEAD_DIM), F32),
        ] + [g_shape] * grad_count,
        [idx, sc, tab, *m_arrays, own, att_own, att_other, cotangent[0], row_vec, up_row],
        [SMEM] * 3 + [HBM] * len(m_arrays) + [VMEM] * 6,
        [VMEM] * 4 + [HBM] * grad_count,
        scratch=[
            pltpu.VMEM((width, width), BF), pltpu.VMEM((blocks, width, width), BF),
            pltpu.VMEM((pieces * blocks, rows, width), BF),
            pltpu.VMEM((width, width), BF), pltpu.VMEM((blocks, width, width), BF),
            pltpu.VMEM((pieces * blocks, rows, width), BF), pltpu.VMEM((blocks, local, width), F32),
            pltpu.SemaphoreType.DMA((3,)), pltpu.SemaphoreType.DMA,
        ],
        flops=6 * local * width * width * (1 + 2 * blocks), moved=4 * width * width * (1 + 2 * blocks),
        trans=local * hidden, vmem=52, name="middle",
    )
    *got, n_x = together(*got, swap_x(after(n_first, att_other)))
    outputs, d_middle, d_own, vec = got[:4]
    grads = got[4:]
    d_c = swap_c(d_own)

    lead = (A, 1 + 2 * blocks, part, width)
    if aligned:
        relative = [g.reshape(lead) for g in grads]
    else:
        whole = grads[0][0]
        by_owner = jnp.concatenate(
            [
                whole[0].reshape(count, 1, part, width),
                whole[1 : 1 + blocks].reshape(blocks, count, part, width).transpose(1, 0, 2, 3),
                whole[1 + blocks :].reshape(count, blocks, part, width),
            ],
            axis=1,
        )
        by_owner = by_owner[q_owner].reshape((4 * F,) + lead)
        relative = [by_owner[i] for i in range(4 * F)]
    g_near = {spot: relative[i] for i, spot in enumerate(spots)}
    g_far = {spot: swap_c(after(relative[2 * F + i], d_c)) for i, spot in reversed(list(enumerate(spots)))}

    def sums_of(keys, half, *others):
        arrays = [g_near[keys], g_far[keys], *others]
        return add_up(arrays, [[(0, (half,)), (1, (half,))] + [(2 + i, ()) for i in range(len(others))]])[0]

    first, second = parts
    half = A // 2
    ways = {}

    def joined(keys, planes):
        arrays = [v for key in keys for v in (g_near[key], g_far[key])]
        return join_up(arrays, [[(2 * i, (planes,)), (2 * i + 1, (planes,))] for i in range(len(keys))])[0]

    def start_ways(step):
        if step == 1:
            for t in range(1, F):
                ways["f", t] = turn_f(joined([(t, 1), (t, 0)], first), F - t)
            ways["x"] = swap_x(joined([(t, 1) for t in range(F)], second))
        if step == 2:
            return [("f", t) for t in range(1, F)] + ["x"]
        if step == 3:
            arrays = [g_near[0, 1], g_far[0, 1], *(ways["f", t] for t in range(1, F))]
            plan = [[(0, (first,)), (1, (first,))] + [(1 + t, (slice(0, half),)) for t in range(1, F)]]
            ways["x", F] = swap_x(add_up(arrays, plan)[0])
            for t in range(1, F):
                arrays = [g_near[t, 0], g_far[t, 0], ways["x"]]
                plan = [[(0, (second,)), (1, (second,)), (2, (slice(t * half, (t + 1) * half),))]]
                ways["f2", t] = turn_f(add_up(arrays, plan)[0], F - t)
            return [("x", F)] + [("f2", t) for t in range(1, F)]
        return []

    pair = [(s, where[s][2]) for s in (1, 2)]
    dq_shape = sds((HEADS, HEAD_DIM, 2 * local), F32)
    half_shapes = [sds((HEADS, 2 * local, HEAD_DIM), BF), sds((2 * HEADS, 2 * local), F32), dq_shape]
    keys = list(g_far)
    do_one, stat_one, dq_one, part_sums, d_x, *more = together(
        *call(
            functools.partial(open_body, units=pair), [*half_shapes, sds((2, local, 2 * width), F32)],
            [sc, tab, q_plane, d_own, d_c, kv_early], [SMEM] * 2 + [VMEM] * 4, [VMEM] * 4,
            flops=2 * work // A, moved=16 * unit * width, trans=HEADS * unit * local, vmem=16, name="open",
        ),
        swap_x(d_own), *(g_far[k] for k in keys),
    )
    g_far.update(zip(keys, more, strict=True))
    d_xc = swap_c(d_x)
    start_ways(1)
    got = together(
        *call(
            functools.partial(close_body, units=pair),
            [*half_shapes, sds((width, 2 * width), F32), sds((8, 2 * width), F32)] + [sds((local, width), BF)] * 2,
            [sc, tab, q_plane, d_x, d_xc, kv_early, n_early, w_all, part_sums],
            [SMEM] * 2 + [VMEM] * 7, [VMEM] * 7, scratch=[pltpu.VMEM((2, local, 2 * width), BF)],
            flops=3 * work // A, moved=16 * unit * width, trans=HEADS * unit * local, vmem=16, name="close",
        ),
    )
    do_two, stat_two, dq_two, n_product, sums, d_sum, d_next = got
    carried = [dq_one, dq_two, n_product, sums]
    q_now = q_plane
    for step, s in enumerate([*near[2:], 0], 1):
        kv_now, n_now, spot = where[s]
        outs = call(
            functools.partial(back_body, unit=(s, spot)),
            [sds((local, width), BF), dq_shape, dq_shape, sds((width, 2 * width), F32), sds((8, 2 * width), F32)],
            [sc, tab, q_now, do_one, do_two, stat_one, stat_two, kv_now, n_now, w_all, *carried],
            [SMEM] * 2 + [VMEM] * 12, [VMEM] * 5, scratch=[pltpu.VMEM((1, local, 2 * width), BF)],
            flops=work // A * 5 // 2 + 8 * local * width * width, moved=16 * unit * width,
            trans=HEADS * unit * local, name="back",
        )
        keys = start_ways(step + 1)
        got = together(*outs, turn_a(d_sum, 1), *(ways[k] for k in keys))
        outs, d_recv = got[:5], got[5]
        ways.update(zip(keys, got[6:], strict=True))
        (d_sum,) = add_up([d_next, d_recv], [[(0, ()), (1, ())]])
        d_next, *carried = outs
        q_now = after(q_plane, d_sum)

    dq_one, dq_two, n_product, sums = carried
    n_blocks = [n_first, swap_c(n_first), n_x, swap_c(n_x)]

    half_count = 2 * F
    msg_lead = (A, part, wide)
    msg_shape = [sds((pieces // 2, rows, wide), BF)] * 2 if aligned else [sds((1, rows, wide), BF)]
    message = call(
        functools.partial(message_body, rows=rows),
        msg_shape,
        [q_idx, *n_blocks, dq_one, dq_two, n_product, sums, w_all, col_vec, vec],
        [SMEM] + [VMEM] * (7 + PLANE), [VMEM] * len(msg_shape),
        scratch=[pltpu.VMEM((width, wide), BF), pltpu.VMEM((width, HEAD_DIM), F32)],
        flops=2 * local * width * width, moved=8 * width * wide, vmem=8, name="message",
    )
    g_sums = {}
    arrays = [g_near[0, 0], g_far[0, 0], ways["x", F], *(ways["f", t] for t in range(1, F))]
    plan = [
        [(0, (s,)), (1, (s,)), (2, (s,))] + [(2 + t, (half + s,)) for t in range(1, F)] for s in range(half)
    ]
    g_sums.update(zip(range(half), add_up(arrays, plan), strict=True))
    arrays = [g_near[0, 0], g_far[0, 0], ways["x"], *(ways["f2", t] for t in range(1, F))]
    plan = [
        [(0, (s,)), (1, (s,)), (2, (s - half,))] + [(2 + t, (s - half,)) for t in range(1, F)]
        for s in range(half, A)
    ]
    g_sums.update(zip(range(half, A), add_up(arrays, plan), strict=True))
    if not aligned:
        flat = message[0][0]
        at = slice(3 * width + 4, 3 * width + 4 + blocks)
        up_part = flat[:, at].T.reshape(count, blocks, part)
        by_owner = flat.reshape(count, part, wide)
        by_owner = by_owner.at[:, :, at].set(up_part.transpose(0, 2, 1))
        by_owner = by_owner[q_owner]
        message = [by_owner[: count // 2], by_owner[count // 2 :]]
    w_far = swap_c(message[1])
    w_far = w_far.reshape((half_count,) + msg_lead)
    w_near = message[0].reshape((half_count,) + msg_lead)
    w_both = add_up([w_near, w_far], [[(0, (i,)), (1, (i,))] for i in range(half_count)])
    got = []
    for (t, xr), sent in zip(spots, w_both, strict=True):
        if xr:
            sent = turn_xf(sent, F - t) if t else swap_x(sent)
        elif t:
            sent = turn_f(sent, F - t)
        got.append(sent)
    lines = local // part
    every = ()
    d_line = d_sum.reshape(lines, part, width)
    sent = lay_out([d_line, g_sums[A - 1]], [(False, [(0, every)]), (False, [(1, every)])], part, width)
    *got, arrived, g_two = together(*got, turn_a(sent, 1), turn_a(g_sums[2], A - 2))
    w_terms = {s: [(i, (s,)) for i in range(len(got))] for s in range(A)}
    w_blocks = -(-wide // width)
    packs = {}
    for s in near:
        arrays, plan = list(got), [(True, w_terms[s])]
        if s not in (2, A - 1):
            arrays.append(g_sums[s])
            plan.append((False, [(len(got), every)]))
        packs[s] = turn_a(lay_out(arrays, plan, part, width), A - s)
    (w_own,) = add_up(got, [w_terms[0]], F32)
    grad_qkv, *vector_grads, up_grad = call(
        functools.partial(unpack_body, w_blocks=w_blocks),
        [sds((part, 3 * width), F32)] + [sds((1, part), F32)] * 8 + [sds((blocks, part), F32)],
        [w_own, *packs.values()], [VMEM] * A, [VMEM] * 10, scratch=[pltpu.VMEM((HEAD_DIM, HEAD_DIM), F32)],
        moved=16 * part * width, vmem=8, name="unpack",
    )

    others = [s for s in near if s not in (2, A - 1)]
    starts = [0, lines, 0] + [w_blocks] * len(others)
    grad_out, grad_up, grad_down = call(
        functools.partial(matrices_body, starts=starts),
        [sds((part, width), F32), sds((part, hidden), F32), sds((blocks * part, width), F32)],
        [g_sums[0], arrived, g_two, *(packs[s] for s in others)], [VMEM] * A, [VMEM] * 3,
        moved=6 * A * g_sums[0].size, vmem=8, name="matrices",
    )
    d_last = arrived if aligned else arrived[:lines].reshape(local, width)
    query_keep, query_send = call(
        query_body, [sds((2, local, width), BF)] * 2, [after(dq_one, got[-1]), dq_two, w_all], [VMEM] * 3, [VMEM] * 2,
        flops=8 * local * width * width, moved=8 * local * width, vmem=8, name="query",
    )
    query_own, query_far = add_up([query_keep, swap_c(query_send)], [[(0, (b,)), (1, (b,))] for b in range(2)])
    grad_tokens = call(
        finish_body, sds((local, width), BF),
        [own, d_middle, row_vec, d_last, d_next, query_own, swap_x(query_far)],
        [VMEM] * 7, VMEM, flops=20 * local * width, moved=16 * local * width, vmem=8, name="finish",
    )
    return (
        outputs[None],
        grad_tokens[None],
        grad_qkv,
        grad_out,
        grad_up,
        grad_down,
        *(v.reshape(part) for v in vector_grads[:7]),
        up_grad.reshape(blocks * part),
        vector_grads[7].reshape(part),
    )


def solution(mesh):
    both = ("rows", "fsdp")
    matrix, vector, act, table = P(both, None), P(both), P("fsdp", "rows", None), P("fsdp", None)
    return jax.shard_map(
        functools.partial(shards, R=mesh.shape["rows"], F=mesh.shape["fsdp"]),
        mesh=mesh,
        in_specs=(act,) + (matrix,) * 4 + (vector,) * 9 + (act,) + (table,) * 3,
        out_specs=(act, act) + (matrix,) * 4 + (vector,) * 9,
        check_vma=False,
    )
```

time: 186 us -> 182 us (0.978)
  starting transfers between devices: 53.9 us -> 39.3 us
  waiting for transfers between devices: 68.7 us -> 74.4 us
  Pallas kernels: 53.9 us -> 56.2 us
    ppermute x18 -> x16, starting transfers between devices: 25.8 us -> 17.3 us  [turn_a(): lax.ppermute(v, 'rows', [(i, (i // PLANE + s) % A * PLANE + i % PLANE) fo...]
    ppermute x18 -> x16, waiting for transfers between devices: 40.5 us -> 46.6 us  [turn_a(): lax.ppermute(v, 'rows', [(i, (i // PLANE + s) % A * PLANE + i % PLANE) fo...]
    ppermute x16 -> x22, waiting for transfers between devices: 4.49 us -> 9.87 us  [swap_c(): return lax.ppermute(v, 'rows', [(i, i ^ 1) for i in range(R)])]
    ppermute x12 -> x11, starting transfers between devices: 13.4 us -> 9.08 us  [swap_x(): return lax.ppermute(v, 'rows', [(i, i ^ 2) for i in range(R)])]
    ppermute x12 -> x11, waiting for transfers between devices: 10.3 us -> 7.17 us  [swap_x(): return lax.ppermute(v, 'rows', [(i, i ^ 2) for i in range(R)])]
    ppermute x2, waiting for transfers between devices: 2.95 us -> 0.01 us  [turn_xf(): lax.ppermute(v, ('rows', 'fsdp'), [(i * F + j, (i ^ 2) * F + (j + t) % F)...]
    pallas_call x28 -> x30, Pallas kernels: 52.1 us -> 54.5 us  [call(): pl.pallas_call(body, out_shape=outs, in_specs=in_specs, out_specs=out_spe...]
    ppermute x16 -> x22, starting transfers between devices: 2.62 us -> 3.83 us  [swap_c(): return lax.ppermute(v, 'rows', [(i, i ^ 1) for i in range(R)])]
  transfers between devices with their start and end apart: 56 -> 59, of which waited for: 23 -> 22; matrix products, arithmetic and copies ran while one was open for 1% -> 2% of each run, Pallas kernels for 19% -> 28%
where the time goes in v1:
time: 182 us; the launch traced here: 178 us
  waiting for transfers between devices  74.4 us (41%)
  Pallas kernels  56.2 us (31%)
  starting transfers between devices  39.3 us (22%)
  other arithmetic  3.42 us (2%)
  local copies, waits for them, and re-layouts  3.23 us (2%)
    pallas_call x30, Pallas kernels, call(): pl.pallas_call(body, out_shape=outs, in_specs=in_specs, out_specs=out_spe...  54.5 us
    ppermute x16, waiting for transfers between devices, turn_a(): lax.ppermute(v, 'rows', [(i, (i // PLANE + s) % A * PLANE + i % PLANE) fo...  46.6 us
    ppermute x16, starting transfers between devices, turn_a(): lax.ppermute(v, 'rows', [(i, (i // PLANE + s) % A * PLANE + i % PLANE) fo...  17.3 us
    ppermute x8, waiting for transfers between devices, turn_f(): return lax.ppermute(v, 'fsdp', [(i, (i + t) % F) for i in range(F)])  10.8 us
    ppermute x22, waiting for transfers between devices, swap_c(): return lax.ppermute(v, 'rows', [(i, i ^ 1) for i in range(R)])  9.87 us
    ppermute x11, starting transfers between devices, swap_x(): return lax.ppermute(v, 'rows', [(i, i ^ 2) for i in range(R)])  9.08 us
    ppermute x8, starting transfers between devices, turn_f(): return lax.ppermute(v, 'fsdp', [(i, (i + t) % F) for i in range(F)])  7.36 us
    ppermute x11, waiting for transfers between devices, swap_x(): return lax.ppermute(v, 'rows', [(i, i ^ 2) for i in range(R)])  7.17 us
  transfers between devices with their start and end apart: 59, of which 22 were waited for; matrix products, arithmetic and copies ran while one was open for 2% of the time, Pallas kernels for 28%

profile of v1, /device:TPU:0, one launch (start us, length us, event | category | flops | bytes accessed | tf_op | source)
XLA Modules:
  0.0 178.2 jit_solution(12287353678876395799)
XLA Ops:
  0.7 1.8 pack.1
  2.4 3.0 %collective-permute-start = (bf16[4,16,512]{2,1,0:T(8,128)(2,1)}, bf16[4,16,512]{2,1,0:T(8,128)(2,1)S(1)}, u32[]{:S(2)}, u32[]{:S(2)}) collective-permute-start(bf16[4,16,512]{2,1,0:T(8,128)(2,1)} %get-tuple-element.176), channel_id=1, source_target_pairs={{0,8},{2,10},{4,12},{6,14},{8,16},{10,18},{12,20},{14,22},{16,24},... | collective-permute-start | bytes 196616 | tf_op jit(solution)/shard_map/ppermute | solution.py:764
  5.4 2.6 %collective-permute-start.1 = (bf16[4,16,512]{2,1,0:T(8,128)(2,1)}, bf16[4,16,512]{2,1,0:T(8,128)(2,1)S(1)}, u32[]{:S(2)}, u32[]{:S(2)}) collective-permute-start(bf16[4,16,512]{2,1,0:T(8,128)(2,1)} %get-tuple-element.176), channel_id=1, source_target_pairs={{0,16},{2,18},{4,20},{6,22},{8,24},{10,26},{12,28},{14,30},{16,0},... | collective-permute-start | bytes 196616 | tf_op jit(solution)/shard_map/ppermute | solution.py:764
  8.0 1.3 collective-permute-start.2
  9.4 0.7 collective-permute-start.3
  10.1 0.7 fusion.9
  10.9 0.7 fusion.4
  11.8 0.8 pad_add_fusion.1.tab
  13.0 8.9 %collective-permute-done.4 = bf16[9,16,512]{2,1,0:T(8,128)(2,1)S(1)} collective-permute-done((bf16[9,16,512]{2,1,0:T(8,128)(2,1)}, bf16[9,16,512]{2,1,0:T(8,128)(2,1)S(1)}, u32[]{:S(2)}, u32[]{:S(2)}) %collective-permute-start.4) | collective-permute-done | bytes 147488 | tf_op jit(solution)/shard_map/ppermute | solution.py:764
  21.9 0.9 fusion.12
  22.8 1.6 collective-permute-start.5
  24.3 1.5 collective-permute-start.6
  26.3 1.5 collective-permute-start.8
  27.8 1.1 collective-permute-start.9
  28.9 8.1 %collective-permute-done.9.refs_0_ = bf16[9,16,512]{2,1,0:T(8,128)(2,1)S(1)} collective-permute-done((bf16[9,16,512]{2,1,0:T(8,128)(2,1)S(1)}, bf16[9,16,512]{2,1,0:T(8,128)(2,1)S(1)}, u32[]{:S(2)}, u32[]{:S(2)}) %collective-permute-start.9) | collective-permute-done | bytes 147488 | tf_op jit(solution)/shard_map/ppermute | solution.py:764
  37.3 1.3 collective-permute-start.12
  38.6 1.5 collective-permute-start.15
  40.1 1.3 collective-permute-start.10
  41.5 3.0 %ready.1 = (bf16[3,512,512]{2,1,0:T(8,128)(2,1)S(1)}, f32[16,512]{1,0:T(8,128)S(1)}, f32[512,128]{1,0:T(8,128)S(1)}, f32[4,512]{1,0:T(4,128)S(1)}, bf16[3,8,256,...) custom-call(s32[32]{0:T(128)S(1)} %get-tuple-element.188.idx, ...), custom_call_target="tpu_custom_call" | custom-call | flops 1342177280 | bytes 3407872 | tf_op jit(solution)/shard_map/ready/pallas_call | solution.py:53
  44.5 1.6 collective-permute-start.14
  46.1 1.1 collective-permute-start.11
  47.7 5.6 %collective-permute-done.11.refs_1_ = bf16[9,16,512]{2,1,0:T(8,128)(2,1)S(1)} collective-permute-done((bf16[9,16,512]{2,1,0:T(8,128)(2,1)S(1)}, bf16[9,16,512]{2,1,0:T(8,128)(2,1)S(1)}, u32[]{:S(2)}, u32[]{:S(2)}) %collective-permute-start.11) | collective-permute-done | bytes 147488 | tf_op jit(solution)/shard_map/ppermute | solution.py:764
  54.2 0.7 collective-permute-start.18
  54.9 1.2 collective-permute-start.19
  56.1 0.7 project.1
  56.8 10.2 %attend.1 = (f32[2,256,640]{2,1,0:T(8,128)S(1)}, f32[2,256,640]{2,1,0:T(8,128)S(1)}, bf16[4,1024,128]{2,1,0:T(8,128)(2,1)S(1)}) custom-call(s32[9]{0:T(128)S(1)} %pad_add_fusion.sc, s32[24]{0:T(128)S(1)} %pad_add_fusion.1.tab, bf16[4,256,128]{2,1,0:T(8,128)(2,1)S(1)} %get-tuple-element.192.refs_0_, bf16[4,256,128]{2,1,0:T(8,128)(2,1)S(1)} %collective-permute-done.16.refs_1_, ...), custom_call_target="tpu_custom_call" | custom-call | flops 2147483648 | bytes 4194304 | tf_op jit(solution)/shard_map/attend/pallas_call | solution.py:53
  67.8 2.4 %collective-permute-done.22.other_ref = f32[2,256,640]{2,1,0:T(8,128)S(1)} collective-permute-done((f32[2,256,640]{2,1,0:T(8,128)S(1)}, f32[2,256,640]{2,1,0:T(8,128)S(1)}, u32[]{:S(2)}, u32[]{:S(2)}) %collective-permute-start.22) | collective-permute-done | bytes 1310752 | tf_op jit(solution)/shard_map/ppermute | solution.py:758
  70.2 0.9 merge.1
  71.1 0.8 copy-done.6
  71.9 0.6 collective-permute-start.24
  72.6 4.5 %collective-permute-done.26.refs_7_ = bf16[2,9,16,512]{3,2,1,0:T(8,128)(2,1)S(1)} collective-permute-done((bf16[2,9,16,512]{3,2,1,0:T(8,128)(2,1)S(1)}, bf16[2,9,16,512]{3,2,1,0:T(8,128)(2,1)S(1)}, u32[]{:S(2)}, u32[]{:S(2)}) %collective-permute-start.26) | collective-permute-done | bytes 294944 | tf_op jit(solution)/shard_map/ppermute | solution.py:769
  77.7 5.2 %collective-permute-done.24.refs_3_ = bf16[2,9,16,512]{3,2,1,0:T(8,128)(2,1)S(1)} collective-permute-done((bf16[2,9,16,512]{3,2,1,0:T(8,128)(2,1)S(1)}, bf16[2,9,16,512]{3,2,1,0:T(8,128)(2,1)S(1)}, u32[]{:S(2)}, u32[]{:S(2)}) %collective-permute-start.24) | collective-permute-done | bytes 294944 | tf_op jit(solution)/shard_map/ppermute | solution.py:769
  83.1 1.5 collective-permute-done.31.refs_11_
  84.7 0.6 copy-done.22
  85.3 12.2 %middle.1 = (bf16[256,512]{1,0:T(8,128)(2,1)}, f32[256,512]{1,0:T(8,128)}, bf16[256,640]{1,0:T(8,128)(2,1)}, f32[512,128]{1,0:T(8,128)S(1)}, bf16[4,9,16,512]{3,...) custom-call(s32[64]{0:T(128)S(1)} %pad_add_fusion.2.idx, ...), custom_call_target="tpu_custom_call" | custom-call | flops 3623878656 | bytes 9437184 | tf_op jit(solution)/shard_map/middle/pallas_call | solution.py:53
  97.8 1.7 collective-permute-done.35.d_c
  101.0 1.0 copy-done.7
  102.0 4.0 %open.1 = (bf16[4,512,128]{2,1,0:T(8,128)(2,1)S(1)}, f32[8,512]{1,0:T(8,128)S(1)}, f32[4,128,512]{2,1,0:T(8,128)S(1)}, f32[2,256,1024]{2,1,0:T(8,128)S(1)}) custom-call(s32[9]{0:T(128)S(1)} %pad_add_fusion.sc, s32[24]{0:T(128)S(1)} %pad_add_fusion.1.tab, bf16[4,1024,128]{2,1,0:T(8,128)(2,1)S(1)} %get-tuple-element.278.q_ref, bf16[256,640]{1,0:T(8,128)(2,1)S(1)} %copy-done.7, ...), custom_call_target="tpu_custom_call" | custom-call | flops 1073741824 | bytes 8388608 | tf_op jit(solution)/shard_map/open/pallas_call | solution.py:53
  106.0 4.5 %collective-permute-done.36.d_x = bf16[256,640]{1,0:T(8,128)(2,1)S(1)} collective-permute-done((bf16[256,640]{1,0:T(8,128)(2,1)}, bf16[256,640]{1,0:T(8,128)(2,1)S(1)}, u32[]{:S(2)}, u32[]{:S(2)}) %collective-permute-start.36) | collective-permute-done | bytes 327712 | tf_op jit(solution)/shard_map/ppermute | solution.py:761
  110.7 0.6 collective-permute-start.44
  112.2 5.2 %close.1 = (bf16[4,512,128]{2,1,0:T(8,128)(2,1)S(1)}, f32[8,512]{1,0:T(8,128)S(1)}, f32[4,128,512]{2,1,0:T(8,128)S(1)}, f32[512,1024]{1,0:T(8,128)S(1)}, f32[8,1...) custom-call(s32[9]{0:T(128)S(1)} %pad_add_fusion.sc, s32[24]{0:T(128)S(1)} %pad_add_fusion.1.tab, ...), custom_call_target="tpu_custom_call" | custom-call | flops 1610612736 | bytes 8388608 | tf_op jit(solution)/shard_map/close/pallas_call | solution.py:53
  117.4 1.2 collective-permute-start.42
  118.6 5.2 %back.2 = (bf16[256,512]{1,0:T(8,128)(2,1)S(1)}, f32[4,128,512]{2,1,0:T(8,128)S(1)}, f32[4,128,512]{2,1,0:T(8,128)S(1)}, f32[512,1024]{1,0:T(8,128)S(1)}, f32[8,1024]{1,0:T(8,128)S(1)}) custom-call(s32[9]{0:T(128)S(1)} %pad_add_fusion.sc, s32[24]{0:T(128)S(1)} %pad_add_fusion.1.tab, bf16[4,1024,128]{2,1,0:T(8,128)(2,1)S(1)} %get-tuple-element.278.q_ref, ...), custom_call_target="tpu_custom_call" | custom-call | flops 1879048192 | bytes 8388608 | tf_op jit(solution)/shard_map/back/pallas_call | solution.py:53
  123.8 2.7 %collective-permute-done.44.refs_2_ = bf16[4,9,16,512]{3,2,1,0:T(8,128)(2,1)S(1)} collective-permute-done((bf16[4,9,16,512]{3,2,1,0:T(8,128)(2,1)S(1)}, bf16[4,9,16,512]{3,2,1,0:T(8,128)(2,1)S(1)}, u32[]{:S(2)}, u32[]{:S(2)}) %collective-permute-start.44) | collective-permute-done | bytes 589856 | tf_op jit(solution)/shard_map/ppermute | solution.py:761
  127.6 1.5 collective-permute-start.46
  129.2 1.2 collective-permute-start.45
  130.9 5.3 %back.3 = (bf16[256,512]{1,0:T(8,128)(2,1)S(1)}, f32[4,128,512]{2,1,0:T(8,128)S(1)}, f32[4,128,512]{2,1,0:T(8,128)S(1)}, f32[512,1024]{1,0:T(8,128)S(1)}, f32[8,1024]{1,0:T(8,128)S(1)}) custom-call(s32[9]{0:T(128)S(1)} %pad_add_fusion.sc, s32[24]{0:T(128)S(1)} %pad_add_fusion.1.tab, bf16[4,1024,128]{2,1,0:T(8,128)(2,1)S(1)} %get-tuple-element.278.q_ref, ...), custom_call_target="tpu_custom_call" | custom-call | flops 1879048192 | bytes 8388608 | tf_op jit(solution)/shard_map/back/pallas_call | solution.py:53
  136.2 1.9 %collective-permute-done.45.refs_1_ = bf16[256,512]{1,0:T(8,128)(2,1)S(1)} collective-permute-done((bf16[256,512]{1,0:T(8,128)(2,1)S(1)}, bf16[256,512]{1,0:T(8,128)(2,1)S(1)}, u32[]{:S(2)}, u32[]{:S(2)}) %collective-permute-start.45) | collective-permute-done | bytes 262176 | tf_op jit(solution)/shard_map/ppermute | solution.py:764
  138.1 2.7 %message.1 = (bf16[16,16,1664]{2,1,0:T(8,128)(2,1)S(1)}, bf16[16,16,1664]{2,1,0:T(8,128)(2,1)S(1)}) custom-call(s32[32]{0:T(128)S(1)} %get-tuple-element.188.idx, bf16[1,256,512]{2,1,0:T(8,128)(2,1)S(1)} %get-tuple-element.234.refs_0_, bf16[1,256,512]{2,1,0:T(8,128)(2,1)S(1)} %collective-permute-done.33.refs_1_, ...), custom_call_target="tpu_custom_call" | custom-call | flops 134217728 | bytes 6815744 | tf_op jit(solution)/shard_map/message/pallas_call | solution.py:53
  141.2 2.0 %collective-permute-done.48 = bf16[16,16,1664]{2,1,0:T(8,128)(2,1)S(1)} collective-permute-done((bf16[16,16,1664]{2,1,0:T(8,128)(2,1)S(1)}, bf16[16,16,1664]{2,1,0:T(8,128)(2,1)S(1)}, u32[]{:S(2)}, u32[]{:S(2)}) %collective-permute-start.48) | collective-permute-done | bytes 852000 | tf_op jit(solution)/shard_map/ppermute | solution.py:758
  143.4 0.6 collective-permute-start.49
  144.0 1.7 collective-permute-start.50
  145.8 1.2 collective-permute-start.51
  147.0 14.2 %collective-permute-done.53.refs_2_ = bf16[9,16,512]{2,1,0:T(8,128)(2,1)S(1)} collective-permute-done((bf16[9,16,512]{2,1,0:T(8,128)(2,1)S(1)}, bf16[9,16,512]{2,1,0:T(8,128)(2,1)S(1)}, u32[]{:S(2)}, u32[]{:S(2)}) %collective-permute-start.53) | collective-permute-done | bytes 147488 | tf_op jit(solution)/shard_map/ppermute | solution.py:764
  161.2 0.8 query.1
  162.1 1.9 %collective-permute-done.54.refs_1_ = bf16[2,256,512]{2,1,0:T(8,128)(2,1)S(1)} collective-permute-done((bf16[2,256,512]{2,1,0:T(8,128)(2,1)S(1)}, bf16[2,256,512]{2,1,0:T(8,128)(2,1)S(1)}, u32[]{:S(2)}, u32[]{:S(2)}) %collective-permute-start.54) | collective-permute-done | bytes 524320 | tf_op jit(solution)/shard_map/ppermute | solution.py:758
  164.1 0.6 collective-permute-start.55
  165.0 2.1 %collective-permute-start.58 = (bf16[4,16,512]{2,1,0:T(8,128)(2,1)S(1)}, bf16[4,16,512]{2,1,0:T(8,128)(2,1)S(1)}, u32[]{:S(2)}, u32[]{:S(2)}) collective-permute-start(bf16[4,16,512]{2,1,0:T(8,128)(2,1)S(1)} %lay.7), channel_id=1, source_target_pairs={{0,8},{2,10},{4,12},{6,14},{8,16},{10,18},{12,20},{14,22},{16,24},... | collective-permute-start | bytes 196616 | tf_op jit(solution)/shard_map/ppermute | solution.py:764
  167.2 5.9 %collective-permute-done.58.refs_3_ = bf16[4,16,512]{2,1,0:T(8,128)(2,1)S(1)} collective-permute-done((bf16[4,16,512]{2,1,0:T(8,128)(2,1)S(1)}, bf16[4,16,512]{2,1,0:T(8,128)(2,1)S(1)}, u32[]{:S(2)}, u32[]{:S(2)}) %collective-permute-start.58) | collective-permute-done | bytes 65568 | tf_op jit(solution)/shard_map/ppermute | solution.py:764
  173.1 1.2 collective-permute-done.57.refs_2_
  174.8 0.7 unpack.1
  175.4 0.6 reshape.120
  176.0 0.7 matrices.1
  176.8 1.1 finish.1
  (142 shorter events, 10.6 us)
Async XLA Ops:
  2.4 34.8 %copy-start.10 = (bf16[9,16,512]{2,1,0:T(8,128)(2,1)S(1)}, bf16[9,16,512]{2,1,0:T(8,128)(2,1)}, u32[]{:S(2)}) copy-start(bf16[9,16,512]{2,1,0:T(8,128)(2,1)} %get-tuple-element.177) | copy-start | bytes 442372
  2.4 10.1 %collective-permute-start = (bf16[4,16,512]{2,1,0:T(8,128)(2,1)}, bf16[4,16,512]{2,1,0:T(8,128)(2,1)S(1)}, u32[]{:S(2)}, u32[]{:S(2)}) collective-permute-start(bf16[4,16,512]{2,1,0:T(8,128)(2,1)} %get-tuple-element.176), channel_id=1, source_target_pairs={{0,8},{2,10},{4,12},{6,14},{8,16},{10,18},{12,20},{14,22},{16,24},... | collective-permute-start | bytes 196616 | tf_op jit(solution)/shard_map/ppermute | solution.py:764
  5.4 7.3 %collective-permute-start.1 = (bf16[4,16,512]{2,1,0:T(8,128)(2,1)}, bf16[4,16,512]{2,1,0:T(8,128)(2,1)S(1)}, u32[]{:S(2)}, u32[]{:S(2)}) collective-permute-start(bf16[4,16,512]{2,1,0:T(8,128)(2,1)} %get-tuple-element.176), channel_id=1, source_target_pairs={{0,16},{2,18},{4,20},{6,22},{8,24},{10,26},{12,28},{14,30},{16,0},... | collective-permute-start | bytes 196616 | tf_op jit(solution)/shard_map/ppermute | solution.py:764
  8.0 4.9 %collective-permute-start.2 = (bf16[4,16,512]{2,1,0:T(8,128)(2,1)}, bf16[4,16,512]{2,1,0:T(8,128)(2,1)S(1)}, u32[]{:S(2)}, u32[]{:S(2)}) collective-permute-start(bf16[4,16,512]{2,1,0:T(8,128)(2,1)} %get-tuple-element.176), channel_id=1, source_target_pairs={{0,24},{2,26},{4,28},{6,30},{8,0},{10,2},{12,4},{14,6},{16,8},{18,... | collective-permute-start | bytes 196616 | tf_op jit(solution)/shard_map/ppermute | solution.py:764
  9.4 12.5 %collective-permute-start.3 = (bf16[256,512]{1,0:T(8,128)(2,1)}, bf16[256,512]{1,0:T(8,128)(2,1)S(1)}, u32[]{:S(2)}, u32[]{:S(2)}) collective-permute-start(bf16[256,512]{1,0:T(8,128)(2,1)} %bitcast.48), channel_id=1, source_target_pairs={{0,8},{2,10},{4,12},{6,14},{8,16},{10,18},{12,20},{14,22},{16,24},... | collective-permute-start | bytes 786440 | tf_op jit(solution)/shard_map/ppermute | solution.py:764
  10.1 11.8 %collective-permute-start.4 = (bf16[9,16,512]{2,1,0:T(8,128)(2,1)}, bf16[9,16,512]{2,1,0:T(8,128)(2,1)S(1)}, u32[]{:S(2)}, u32[]{:S(2)}) collective-permute-start(bf16[9,16,512]{2,1,0:T(8,128)(2,1)} %get-tuple-element.177), channel_id=1, source_target_pairs={{0,8},{2,10},{4,12},{6,14},{8,16},{10,18},{12,20},{14,22},{16,24},... | collective-permute-start | bytes 442376 | tf_op jit(solution)/shard_map/ppermute | solution.py:764
  22.8 14.2 %collective-permute-start.5 = (bf16[4,4,16,512]{3,2,1,0:T(8,128)(2,1)S(1)}, bf16[4,4,16,512]{3,2,1,0:T(8,128)(2,1)S(1)}, u32[]{:S(2)}, u32[]{:S(2)}) collective-permute-start(bf16[4,4,16,512]{3,2,1,0:T(8,128)(2,1)S(1)} %get-tuple-element.338), channel_id=1, source_target_pairs={{0,4},{2,6},{4,0},{6,2},{8,12},{10,14},{12,8},{14,10},{16,20},{18,... | collective-permute-start | bytes 786440 | tf_op jit(solution)/shard_map/ppermute | solution.py:761
  24.3 12.7 %collective-permute-start.6 = (bf16[4,4,16,512]{3,2,1,0:T(8,128)(2,1)S(1)}, bf16[4,4,16,512]{3,2,1,0:T(8,128)(2,1)S(1)}, u32[]{:S(2)}, u32[]{:S(2)}) collective-permute-start(bf16[4,4,16,512]{3,2,1,0:T(8,128)(2,1)S(1)} %get-tuple-element.338), channel_id=1, source_target_pairs={{0,1},{1,0},{2,3},{3,2},{4,5},{5,4},{6,7},{7,6},{8,9},{9,8},{10,11... | collective-permute-start | bytes 786440 | tf_op jit(solution)/shard_map/ppermute | solution.py:769
  25.8 11.2 %collective-permute-start.7 = (bf16[4,4,16,512]{3,2,1,0:T(8,128)(2,1)S(1)}, bf16[4,4,16,512]{3,2,1,0:T(8,128)(2,1)S(1)}, u32[]{:S(2)}, u32[]{:S(2)}) collective-permute-start(bf16[4,4,16,512]{3,2,1,0:T(8,128)(2,1)S(1)} %get-tuple-element.338), channel_id=1, source_target_pairs={{0,5},{1,4},{2,7},{3,6},{4,1},{5,0},{6,3},{7,2},{8,13},{9,12},{10,... | collective-permute-start | bytes 786440 | tf_op jit(solution)/shard_map/ppermute | solution.py:772
  26.3 10.7 %collective-permute-start.8 = (bf16[256,512]{1,0:T(8,128)(2,1)S(1)}, bf16[256,512]{1,0:T(8,128)(2,1)S(1)}, u32[]{:S(2)}, u32[]{:S(2)}) collective-permute-start(bf16[256,512]{1,0:T(8,128)(2,1)S(1)} %collective-permute-done.3), channel_id=1, source_target_pairs={{0,8},{2,10},{4,12},{6,14},{8,16},{10,18},{12,20},{14,22},{16,24},... | collective-permute-start | bytes 786440 | tf_op jit(solution)/shard_map/ppermute | solution.py:764
  27.8 9.2 %collective-permute-start.9 = (bf16[9,16,512]{2,1,0:T(8,128)(2,1)S(1)}, bf16[9,16,512]{2,1,0:T(8,128)(2,1)S(1)}, u32[]{:S(2)}, u32[]{:S(2)}) collective-permute-start(bf16[9,16,512]{2,1,0:T(8,128)(2,1)S(1)} %collective-permute-done.4), channel_id=1, source_target_pairs={{0,8},{2,10},{4,12},{6,14},{8,16},{10,18},{12,20},{14,22},{16,24},... | collective-permute-start | bytes 442376 | tf_op jit(solution)/shard_map/ppermute | solution.py:764
  37.2 4.3 %collective-permute-start.13 = (bf16[4,4,4,16,512]{4,3,2,1,0:T(8,128)(2,1)S(1)}, bf16[4,4,4,16,512]{4,3,2,1,0:T(8,128)(2,1)S(1)}, u32[]{:S(2)}, u32[]{:S(2)}) collective-permute-start(bf16[4,4,4,16,512]{4,3,2,1,0:T(8,128)(2,1)S(1)} %pad_maximum_fusion), channel_id=1, source_target_pairs={{0,2},{2,0},{4,6},{6,4},{8,10},{10,8},{12,14},{14,12},{16,18},{18,... | collective-permute-start | bytes 3145736 | tf_op jit(solution)/shard_map/ppermute | solution.py:758
  37.3 9.8 %collective-permute-start.12 = (bf16[2,9,16,512]{3,2,1,0:T(8,128)(2,1)S(1)}, bf16[2,9,16,512]{3,2,1,0:T(8,128)(2,1)S(1)}, u32[]{:S(2)}, u32[]{:S(2)}) collective-permute-start(bf16[2,9,16,512]{3,2,1,0:T(8,128)(2,1)S(1)} %pad_maximum_fusion.2.refs_4_), channel_id=1, source_target_pairs={{0,4},{2,6},{4,0},{6,2},{8,12},{10,14},{12,8},{14,10},{16,20},{18,... | collective-permute-start | bytes 884744 | tf_op jit(solution)/shard_map/ppermute | solution.py:761
  38.6 9.1 %collective-permute-start.15 = (bf16[2,9,16,512]{3,2,1,0:T(8,128)(2,1)S(1)}, bf16[2,9,16,512]{3,2,1,0:T(8,128)(2,1)S(1)}, u32[]{:S(2)}, u32[]{:S(2)}) collective-permute-start(bf16[2,9,16,512]{3,2,1,0:T(8,128)(2,1)S(1)} %pad_maximum_fusion.2.refs_4_), channel_id=1, source_target_pairs={{0,1},{1,0},{2,3},{3,2},{4,5},{5,4},{6,7},{7,6},{8,9},{9,8},{10,11... | collective-permute-start | bytes 884744 | tf_op jit(solution)/shard_map/ppermute | solution.py:769
  40.1 13.2 %collective-permute-start.10 = (bf16[256,512]{1,0:T(8,128)(2,1)S(1)}, bf16[256,512]{1,0:T(8,128)(2,1)S(1)}, u32[]{:S(2)}, u32[]{:S(2)}) collective-permute-start(bf16[256,512]{1,0:T(8,128)(2,1)S(1)} %collective-permute-done.8), channel_id=1, source_target_pairs={{0,8},{2,10},{4,12},{6,14},{8,16},{10,18},{12,20},{14,22},{16,24},... | collective-permute-start | bytes 786440 | tf_op jit(solution)/shard_map/ppermute | solution.py:764
  44.5 8.8 %collective-permute-start.14 = (bf16[4,256,128]{2,1,0:T(8,128)(2,1)S(1)}, bf16[4,256,128]{2,1,0:T(8,128)(2,1)S(1)}, u32[]{:S(2)}, u32[]{:S(2)}) collective-permute-start(bf16[4,256,128]{2,1,0:T(8,128)(2,1)S(1)} %get-tuple-element.192.refs_0_), channel_id=1, source_target_pairs={{0,4},{2,6},{4,0},{6,2},{8,12},{10,14},{12,8},{14,10},{16,20},{18,... | collective-permute-start | bytes 786440 | tf_op jit(solution)/shard_map/ppermute | solution.py:761
  46.1 7.2 %collective-permute-start.11 = (bf16[9,16,512]{2,1,0:T(8,128)(2,1)S(1)}, bf16[9,16,512]{2,1,0:T(8,128)(2,1)S(1)}, u32[]{:S(2)}, u32[]{:S(2)}) collective-permute-start(bf16[9,16,512]{2,1,0:T(8,128)(2,1)S(1)} %collective-permute-done.9.refs_0_), channel_id=1, source_target_pairs={{0,8},{2,10},{4,12},{6,14},{8,16},{10,18},{12,20},{14,22},{16,24},... | collective-permute-start | bytes 442376 | tf_op jit(solution)/shard_map/ppermute | solution.py:764
  47.1 20.0 %copy-start.12 = (bf16[2,9,16,512]{3,2,1,0:T(8,128)(2,1)}, bf16[2,9,16,512]{3,2,1,0:T(8,128)(2,1)S(1)}, u32[]{:S(2)}) copy-start(bf16[2,9,16,512]{3,2,1,0:T(8,128)(2,1)S(1)} %collective-permute-done.12.refs_5_) | copy-start | bytes 884740
  47.1 8.9 %collective-permute-start.16 = (bf16[4,256,128]{2,1,0:T(8,128)(2,1)S(1)}, bf16[4,256,128]{2,1,0:T(8,128)(2,1)S(1)}, u32[]{:S(2)}, u32[]{:S(2)}) collective-permute-start(bf16[4,256,128]{2,1,0:T(8,128)(2,1)S(1)} %get-tuple-element.192.refs_0_), channel_id=1, source_target_pairs={{0,2},{2,0},{4,6},{6,4},{8,10},{10,8},{12,14},{14,12},{16,18},{18,... | collective-permute-start | bytes 786440 | tf_op jit(solution)/shard_map/ppermute | solution.py:758
  47.7 20.0 %copy-start.13 = (bf16[2,9,16,512]{3,2,1,0:T(8,128)(2,1)}, bf16[2,9,16,512]{3,2,1,0:T(8,128)(2,1)S(1)}, u32[]{:S(2)}) copy-start(bf16[2,9,16,512]{3,2,1,0:T(8,128)(2,1)S(1)} %collective-permute-done.15.refs_6_) | copy-start | bytes 884740
  53.3 3.5 %collective-permute-start.17 = (bf16[4,256,128]{2,1,0:T(8,128)(2,1)S(1)}, bf16[4,256,128]{2,1,0:T(8,128)(2,1)S(1)}, u32[]{:S(2)}, u32[]{:S(2)}) collective-permute-start(bf16[4,256,128]{2,1,0:T(8,128)(2,1)S(1)} %collective-permute-done.14.refs_2_), channel_id=1, source_target_pairs={{0,2},{2,0},{4,6},{6,4},{8,10},{10,8},{12,14},{14,12},{16,18},{18,... | collective-permute-start | bytes 786440 | tf_op jit(solution)/shard_map/ppermute | solution.py:758
  53.3 13.7 %collective-permute-start.20 = (bf16[2,9,16,512]{3,2,1,0:T(8,128)(2,1)S(1)}, bf16[2,9,16,512]{3,2,1,0:T(8,128)(2,1)S(1)}, u32[]{:S(2)}, u32[]{:S(2)}) collective-permute-start(bf16[2,9,16,512]{3,2,1,0:T(8,128)(2,1)S(1)} %pad_maximum_fusion.2.refs_4_), channel_id=1, source_target_pairs={{0,2},{2,0},{4,6},{6,4},{8,10},{10,8},{12,14},{14,12},{16,18},{18,... | collective-permute-start | bytes 884744 | tf_op jit(solution)/shard_map/ppermute | solution.py:758
  54.2 12.9 %collective-permute-start.18 = (bf16[2,9,16,512]{3,2,1,0:T(8,128)(2,1)S(1)}, bf16[2,9,16,512]{3,2,1,0:T(8,128)(2,1)S(1)}, u32[]{:S(2)}, u32[]{:S(2)}) collective-permute-start(bf16[2,9,16,512]{3,2,1,0:T(8,128)(2,1)S(1)} %copy.41.refs_0_), channel_id=1, source_target_pairs={{0,4},{2,6},{4,0},{6,2},{8,12},{10,14},{12,8},{14,10},{16,20},{18,... | collective-permute-start | bytes 884744 | tf_op jit(solution)/shard_map/ppermute | solution.py:761
  54.9 12.2 %collective-permute-start.19 = (bf16[2,9,16,512]{3,2,1,0:T(8,128)(2,1)S(1)}, bf16[2,9,16,512]{3,2,1,0:T(8,128)(2,1)S(1)}, u32[]{:S(2)}, u32[]{:S(2)}) collective-permute-start(bf16[2,9,16,512]{3,2,1,0:T(8,128)(2,1)S(1)} %copy.41.refs_0_), channel_id=1, source_target_pairs={{0,1},{1,0},{2,3},{3,2},{4,5},{5,4},{6,7},{7,6},{8,9},{9,8},{10,11... | collective-permute-start | bytes 884744 | tf_op jit(solution)/shard_map/ppermute | solution.py:769
  56.1 11.0 %collective-permute-start.21 = (bf16[2,9,16,512]{3,2,1,0:T(8,128)(2,1)S(1)}, bf16[2,9,16,512]{3,2,1,0:T(8,128)(2,1)S(1)}, u32[]{:S(2)}, u32[]{:S(2)}) collective-permute-start(bf16[2,9,16,512]{3,2,1,0:T(8,128)(2,1)S(1)} %collective-permute-done.12.refs_5_), channel_id=1, source_target_pairs={{0,2},{2,0},{4,6},{6,4},{8,10},{10,8},{12,14},{14,12},{16,18},{18,... | collective-permute-start | bytes 884744 | tf_op jit(solution)/shard_map/ppermute | solution.py:758
  67.0 18.3 %copy-start.8 = (bf16[1,256,512]{2,1,0:T(8,128)(2,1)S(1)}, bf16[1,256,512]{2,1,0:T(8,128)(2,1)}, u32[]{:S(2)}) copy-start(bf16[1,256,512]{2,1,0:T(8,128)(2,1)} %param.39) | copy-start | bytes 786436
  67.0 17.6 %copy-start.14 = (bf16[2,9,16,512]{3,2,1,0:T(8,128)(2,1)}, bf16[2,9,16,512]{3,2,1,0:T(8,128)(2,1)S(1)}, u32[]{:S(2)}) copy-start(bf16[2,9,16,512]{3,2,1,0:T(8,128)(2,1)S(1)} %collective-permute-done.20.refs_12_) | copy-start | bytes 884740
  67.1 3.1 %collective-permute-start.22 = (f32[2,256,640]{2,1,0:T(8,128)S(1)}, f32[2,256,640]{2,1,0:T(8,128)S(1)}, u32[]{:S(2)}, u32[]{:S(2)}) collective-permute-start(f32[2,256,640]{2,1,0:T(8,128)S(1)} %get-tuple-element.207), channel_id=1, source_target_pairs={{0,2},{2,0},{4,6},{6,4},{8,10},{10,8},{12,14},{14,12},{16,18},{18,... | collective-permute-start | bytes 3932168 | tf_op jit(solution)/shard_map/ppermute | solution.py:758
  67.2 9.9 %collective-permute-start.26 = (bf16[2,9,16,512]{3,2,1,0:T(8,128)(2,1)S(1)}, bf16[2,9,16,512]{3,2,1,0:T(8,128)(2,1)S(1)}, u32[]{:S(2)}, u32[]{:S(2)}) collective-permute-start(bf16[2,9,16,512]{3,2,1,0:T(8,128)(2,1)S(1)} %collective-permute-done.12.refs_5_), channel_id=1, source_target_pairs={{0,1},{1,0},{2,3},{3,2},{4,5},{5,4},{6,7},{7,6},{8,9},{9,8},{10,11... | collective-permute-start | bytes 884744 | tf_op jit(solution)/shard_map/ppermute | solution.py:769
  67.2 9.8 %collective-permute-start.28 = (bf16[2,9,16,512]{3,2,1,0:T(8,128)(2,1)S(1)}, bf16[2,9,16,512]{3,2,1,0:T(8,128)(2,1)S(1)}, u32[]{:S(2)}, u32[]{:S(2)}) collective-permute-start(bf16[2,9,16,512]{3,2,1,0:T(8,128)(2,1)S(1)} %copy.41.refs_0_), channel_id=1, source_target_pairs={{0,2},{2,0},{4,6},{6,4},{8,10},{10,8},{12,14},{14,12},{16,18},{18,... | collective-permute-start | bytes 884744 | tf_op jit(solution)/shard_map/ppermute | solution.py:758
  67.7 9.9 %collective-permute-start.25 = (bf16[2,9,16,512]{3,2,1,0:T(8,128)(2,1)S(1)}, bf16[2,9,16,512]{3,2,1,0:T(8,128)(2,1)S(1)}, u32[]{:S(2)}, u32[]{:S(2)}) collective-permute-start(bf16[2,9,16,512]{3,2,1,0:T(8,128)(2,1)S(1)} %collective-permute-done.15.refs_6_), channel_id=1, source_target_pairs={{0,2},{2,0},{4,6},{6,4},{8,10},{10,8},{12,14},{14,12},{16,18},{18,... | collective-permute-start | bytes 884744 | tf_op jit(solution)/shard_map/ppermute | solution.py:758
  71.9 11.0 %collective-permute-start.23 = (bf16[256,640]{1,0:T(8,128)(2,1)S(1)}, bf16[256,640]{1,0:T(8,128)(2,1)S(1)}, u32[]{:S(2)}, u32[]{:S(2)}) collective-permute-start(bf16[256,640]{1,0:T(8,128)(2,1)S(1)} %get-tuple-element.208), channel_id=1, source_target_pairs={{0,4},{2,6},{4,0},{6,2},{8,12},{10,14},{12,8},{14,10},{16,20},{18,... | collective-permute-start | bytes 983048 | tf_op jit(solution)/shard_map/ppermute | solution.py:761
  71.9 11.0 %collective-permute-start.24 = (bf16[2,9,16,512]{3,2,1,0:T(8,128)(2,1)S(1)}, bf16[2,9,16,512]{3,2,1,0:T(8,128)(2,1)S(1)}, u32[]{:S(2)}, u32[]{:S(2)}) collective-permute-start(bf16[2,9,16,512]{3,2,1,0:T(8,128)(2,1)S(1)} %collective-permute-done.18.refs_1_), channel_id=1, source_target_pairs={{0,1},{1,0},{2,3},{3,2},{4,5},{5,4},{6,7},{7,6},{8,9},{9,8},{10,11... | collective-permute-start | bytes 884744 | tf_op jit(solution)/shard_map/ppermute | solution.py:769
  77.0 5.9 %collective-permute-start.29 = (bf16[2,9,16,512]{3,2,1,0:T(8,128)(2,1)S(1)}, bf16[2,9,16,512]{3,2,1,0:T(8,128)(2,1)S(1)}, u32[]{:S(2)}, u32[]{:S(2)}) collective-permute-start(bf16[2,9,16,512]{3,2,1,0:T(8,128)(2,1)S(1)} %collective-permute-done.18.refs_1_), channel_id=1, source_target_pairs={{0,2},{2,0},{4,6},{6,4},{8,10},{10,8},{12,14},{14,12},{16,18},{18,... | collective-permute-start | bytes 884744 | tf_op jit(solution)/shard_map/ppermute | solution.py:758
  77.1 5.8 %collective-permute-start.30 = (bf16[2,9,16,512]{3,2,1,0:T(8,128)(2,1)S(1)}, bf16[2,9,16,512]{3,2,1,0:T(8,128)(2,1)S(1)}, u32[]{:S(2)}, u32[]{:S(2)}) collective-permute-start(bf16[2,9,16,512]{3,2,1,0:T(8,128)(2,1)S(1)} %collective-permute-done.19.refs_2_), channel_id=1, source_target_pairs={{0,2},{2,0},{4,6},{6,4},{8,10},{10,8},{12,14},{14,12},{16,18},{18,... | collective-permute-start | bytes 884744 | tf_op jit(solution)/shard_map/ppermute | solution.py:758
  77.6 5.4 %collective-permute-start.27 = (bf16[2,9,16,512]{3,2,1,0:T(8,128)(2,1)S(1)}, bf16[2,9,16,512]{3,2,1,0:T(8,128)(2,1)S(1)}, u32[]{:S(2)}, u32[]{:S(2)}) collective-permute-start(bf16[2,9,16,512]{3,2,1,0:T(8,128)(2,1)S(1)} %collective-permute-done.26.refs_7_), channel_id=1, source_target_pairs={{0,2},{2,0},{4,6},{6,4},{8,10},{10,8},{12,14},{14,12},{16,18},{18,... | collective-permute-start | bytes 884744 | tf_op jit(solution)/shard_map/ppermute | solution.py:758
  83.0 1.6 collective-permute-start.31
  83.0 14.5 %collective-permute-start.32 = (bf16[1,256,512]{2,1,0:T(8,128)(2,1)S(1)}, bf16[1,256,512]{2,1,0:T(8,128)(2,1)S(1)}, u32[]{:S(2)}, u32[]{:S(2)}) collective-permute-start(bf16[1,256,512]{2,1,0:T(8,128)(2,1)S(1)} %get-tuple-element.234.refs_0_), channel_id=1, source_target_pairs={{0,4},{2,6},{4,0},{6,2},{8,12},{10,14},{12,8},{14,10},{16,20},{18,... | collective-permute-start | bytes 786440 | tf_op jit(solution)/shard_map/ppermute | solution.py:761
  97.6 1.9 %collective-permute-start.35 = (bf16[256,640]{1,0:T(8,128)(2,1)}, bf16[256,640]{1,0:T(8,128)(2,1)S(1)}, u32[]{:S(2)}, u32[]{:S(2)}) collective-permute-start(bf16[256,640]{1,0:T(8,128)(2,1)} %get-tuple-element.239.d_own), channel_id=1, source_target_pairs={{0,2},{2,0},{4,6},{6,4},{8,10},{10,8},{12,14},{14,12},{16,18},{18,... | collective-permute-start | bytes 983048 | tf_op jit(solution)/shard_map/ppermute | solution.py:758
  99.5 11.0 %collective-permute-start.40 = (bf16[4,9,16,512]{3,2,1,0:T(8,128)(2,1)}, bf16[4,9,16,512]{3,2,1,0:T(8,128)(2,1)S(1)}, u32[]{:S(2)}, u32[]{:S(2)}) collective-permute-start(bf16[4,9,16,512]{3,2,1,0:T(8,128)(2,1)} %get-tuple-element.251), channel_id=1, source_target_pairs={{0,2},{2,0},{4,6},{6,4},{8,10},{10,8},{12,14},{14,12},{16,18},{18,... | collective-permute-start | bytes 1769480 | tf_op jit(solution)/shard_map/ppermute | solution.py:758
  99.6 10.9 %collective-permute-start.39 = (bf16[4,9,16,512]{3,2,1,0:T(8,128)(2,1)}, bf16[4,9,16,512]{3,2,1,0:T(8,128)(2,1)S(1)}, u32[]{:S(2)}, u32[]{:S(2)}) collective-permute-start(bf16[4,9,16,512]{3,2,1,0:T(8,128)(2,1)} %get-tuple-element.249), channel_id=1, source_target_pairs={{0,2},{2,0},{4,6},{6,4},{8,10},{10,8},{12,14},{14,12},{16,18},{18,... | collective-permute-start | bytes 1769480 | tf_op jit(solution)/shard_map/ppermute | solution.py:758
  100.0 10.5 %collective-permute-start.38 = (bf16[4,9,16,512]{3,2,1,0:T(8,128)(2,1)}, bf16[4,9,16,512]{3,2,1,0:T(8,128)(2,1)S(1)}, u32[]{:S(2)}, u32[]{:S(2)}) collective-permute-start(bf16[4,9,16,512]{3,2,1,0:T(8,128)(2,1)} %get-tuple-element.247), channel_id=1, source_target_pairs={{0,2},{2,0},{4,6},{6,4},{8,10},{10,8},{12,14},{14,12},{16,18},{18,... | collective-permute-start | bytes 1769480 | tf_op jit(solution)/shard_map/ppermute | solution.py:758
  100.1 10.4 %collective-permute-start.37 = (bf16[4,9,16,512]{3,2,1,0:T(8,128)(2,1)}, bf16[4,9,16,512]{3,2,1,0:T(8,128)(2,1)S(1)}, u32[]{:S(2)}, u32[]{:S(2)}) collective-permute-start(bf16[4,9,16,512]{3,2,1,0:T(8,128)(2,1)} %get-tuple-element.245), channel_id=1, source_target_pairs={{0,2},{2,0},{4,6},{6,4},{8,10},{10,8},{12,14},{14,12},{16,18},{18,... | collective-permute-start | bytes 1769480 | tf_op jit(solution)/shard_map/ppermute | solution.py:758
  100.5 10.0 %collective-permute-start.36 = (bf16[256,640]{1,0:T(8,128)(2,1)}, bf16[256,640]{1,0:T(8,128)(2,1)S(1)}, u32[]{:S(2)}, u32[]{:S(2)}) collective-permute-start(bf16[256,640]{1,0:T(8,128)(2,1)} %get-tuple-element.239.d_own), channel_id=1, source_target_pairs={{0,4},{2,6},{4,0},{6,2},{8,12},{10,14},{12,8},{14,10},{16,20},{18,... | collective-permute-start | bytes 983048 | tf_op jit(solution)/shard_map/ppermute | solution.py:761
  110.5 1.7 collective-permute-start.41
  110.7 15.8 %collective-permute-start.44 = (bf16[4,9,16,512]{3,2,1,0:T(8,128)(2,1)S(1)}, bf16[4,9,16,512]{3,2,1,0:T(8,128)(2,1)S(1)}, u32[]{:S(2)}, u32[]{:S(2)}) collective-permute-start(bf16[4,9,16,512]{3,2,1,0:T(8,128)(2,1)S(1)} %join.3), channel_id=1, source_target_pairs={{0,4},{2,6},{4,0},{6,2},{8,12},{10,14},{12,8},{14,10},{16,20},{18,... | collective-permute-start | bytes 1769480 | tf_op jit(solution)/shard_map/ppermute | solution.py:761
  111.5 15.5 %collective-permute-start.43 = (bf16[4,9,16,512]{3,2,1,0:T(8,128)(2,1)S(1)}, bf16[4,9,16,512]{3,2,1,0:T(8,128)(2,1)S(1)}, u32[]{:S(2)}, u32[]{:S(2)}) collective-permute-start(bf16[4,9,16,512]{3,2,1,0:T(8,128)(2,1)S(1)} %join.2), channel_id=1, source_target_pairs={{0,1},{1,0},{2,3},{3,2},{4,5},{5,4},{6,7},{7,6},{8,9},{9,8},{10,11... | collective-permute-start | bytes 1769480 | tf_op jit(solution)/shard_map/ppermute | solution.py:769
  117.4 9.6 %collective-permute-start.42 = (bf16[256,512]{1,0:T(8,128)(2,1)S(1)}, bf16[256,512]{1,0:T(8,128)(2,1)S(1)}, u32[]{:S(2)}, u32[]{:S(2)}) collective-permute-start(bf16[256,512]{1,0:T(8,128)(2,1)S(1)} %get-tuple-element.270), channel_id=1, source_target_pairs={{0,8},{2,10},{4,12},{6,14},{8,16},{10,18},{12,20},{14,22},{16,24},... | collective-permute-start | bytes 786440 | tf_op jit(solution)/shard_map/ppermute | solution.py:764
  127.1 11.0 %collective-permute-start.47 = (bf16[2,9,16,512]{3,2,1,0:T(8,128)(2,1)S(1)}, bf16[2,9,16,512]{3,2,1,0:T(8,128)(2,1)S(1)}, u32[]{:S(2)}, u32[]{:S(2)}) collective-permute-start(bf16[2,9,16,512]{3,2,1,0:T(8,128)(2,1)S(1)} %add.131), channel_id=1, source_target_pairs={{0,1},{1,0},{2,3},{3,2},{4,5},{5,4},{6,7},{7,6},{8,9},{9,8},{10,11... | collective-permute-start | bytes 884744 | tf_op jit(solution)/shard_map/ppermute | solution.py:769
  127.6 10.5 %collective-permute-start.46 = (bf16[2,9,16,512]{3,2,1,0:T(8,128)(2,1)S(1)}, bf16[2,9,16,512]{3,2,1,0:T(8,128)(2,1)S(1)}, u32[]{:S(2)}, u32[]{:S(2)}) collective-permute-start(bf16[2,9,16,512]{3,2,1,0:T(8,128)(2,1)S(1)} %add.130), channel_id=1, source_target_pairs={{0,4},{2,6},{4,0},{6,2},{8,12},{10,14},{12,8},{14,10},{16,20},{18,... | collective-permute-start | bytes 884744 | tf_op jit(solution)/shard_map/ppermute | solution.py:761
  129.2 8.9 %collective-permute-start.45 = (bf16[256,512]{1,0:T(8,128)(2,1)S(1)}, bf16[256,512]{1,0:T(8,128)(2,1)S(1)}, u32[]{:S(2)}, u32[]{:S(2)}) collective-permute-start(bf16[256,512]{1,0:T(8,128)(2,1)S(1)} %add.129), channel_id=1, source_target_pairs={{0,8},{2,10},{4,12},{6,14},{8,16},{10,18},{12,20},{14,22},{16,24},... | collective-permute-start | bytes 786440 | tf_op jit(solution)/shard_map/ppermute | solution.py:764
  130.4 7.7 %collective-permute-start.33 = (bf16[1,256,512]{2,1,0:T(8,128)(2,1)S(1)}, bf16[1,256,512]{2,1,0:T(8,128)(2,1)S(1)}, u32[]{:S(2)}, u32[]{:S(2)}) collective-permute-start(bf16[1,256,512]{2,1,0:T(8,128)(2,1)S(1)} %get-tuple-element.234.refs_0_), channel_id=1, source_target_pairs={{0,2},{2,0},{4,6},{6,4},{8,10},{10,8},{12,14},{14,12},{16,18},{18,... | collective-permute-start | bytes 786440 | tf_op jit(solution)/shard_map/ppermute | solution.py:758
  130.4 7.7 %collective-permute-start.34 = (bf16[1,256,512]{2,1,0:T(8,128)(2,1)S(1)}, bf16[1,256,512]{2,1,0:T(8,128)(2,1)S(1)}, u32[]{:S(2)}, u32[]{:S(2)}) collective-permute-start(bf16[1,256,512]{2,1,0:T(8,128)(2,1)S(1)} %collective-permute-done.32.refs_2_), channel_id=1, source_target_pairs={{0,2},{2,0},{4,6},{6,4},{8,10},{10,8},{12,14},{14,12},{16,18},{18,... | collective-permute-start | bytes 786440 | tf_op jit(solution)/shard_map/ppermute | solution.py:758
  140.8 2.4 %collective-permute-start.48 = (bf16[16,16,1664]{2,1,0:T(8,128)(2,1)S(1)}, bf16[16,16,1664]{2,1,0:T(8,128)(2,1)S(1)}, u32[]{:S(2)}, u32[]{:S(2)}) collective-permute-start(bf16[16,16,1664]{2,1,0:T(8,128)(2,1)S(1)} %get-tuple-element.297), channel_id=1, source_target_pairs={{0,2},{2,0},{4,6},{6,4},{8,10},{10,8},{12,14},{14,12},{16,18},{18,... | collective-permute-start | bytes 2555912 | tf_op jit(solution)/shard_map/ppermute | solution.py:758
  141.1 20.0 %collective-permute-start.52 = (bf16[25,16,512]{2,1,0:T(8,128)(2,1)S(1)}, bf16[25,16,512]{2,1,0:T(8,128)(2,1)S(1)}, u32[]{:S(2)}, u32[]{:S(2)}) collective-permute-start(bf16[25,16,512]{2,1,0:T(8,128)(2,1)S(1)} %lay.4), channel_id=1, source_target_pairs={{0,8},{2,10},{4,12},{6,14},{8,16},{10,18},{12,20},{14,22},{16,24},... | collective-permute-start | bytes 1228808 | tf_op jit(solution)/shard_map/ppermute | solution.py:764
  143.4 17.7 %collective-permute-start.49 = (bf16[4,16,1664]{2,1,0:T(8,128)(2,1)S(1)}, bf16[4,16,1664]{2,1,0:T(8,128)(2,1)S(1)}, u32[]{:S(2)}, u32[]{:S(2)}) collective-permute-start(bf16[4,16,1664]{2,1,0:T(8,128)(2,1)S(1)} %get-tuple-element.299), channel_id=1, source_target_pairs={{0,4},{2,6},{4,0},{6,2},{8,12},{10,14},{12,8},{14,10},{16,20},{18,... | collective-permute-start | bytes 638984 | tf_op jit(solution)/shard_map/ppermute | solution.py:761
  144.0 17.1 %collective-permute-start.50 = (bf16[4,16,1664]{2,1,0:T(8,128)(2,1)S(1)}, bf16[4,16,1664]{2,1,0:T(8,128)(2,1)S(1)}, u32[]{:S(2)}, u32[]{:S(2)}) collective-permute-start(bf16[4,16,1664]{2,1,0:T(8,128)(2,1)S(1)} %get-tuple-element.300), channel_id=1, source_target_pairs={{0,1},{1,0},{2,3},{3,2},{4,5},{5,4},{6,7},{7,6},{8,9},{9,8},{10,11... | collective-permute-start | bytes 638984 | tf_op jit(solution)/shard_map/ppermute | solution.py:769
  145.8 15.4 %collective-permute-start.51 = (bf16[4,16,1664]{2,1,0:T(8,128)(2,1)S(1)}, bf16[4,16,1664]{2,1,0:T(8,128)(2,1)S(1)}, u32[]{:S(2)}, u32[]{:S(2)}) collective-permute-start(bf16[4,16,1664]{2,1,0:T(8,128)(2,1)S(1)} %get-tuple-element.301), channel_id=1, source_target_pairs={{0,5},{1,4},{2,7},{3,6},{4,1},{5,0},{6,3},{7,2},{8,13},{9,12},{10,... | collective-permute-start | bytes 638984 | tf_op jit(solution)/shard_map/ppermute | solution.py:772
  147.0 14.2 %collective-permute-start.53 = (bf16[9,16,512]{2,1,0:T(8,128)(2,1)S(1)}, bf16[9,16,512]{2,1,0:T(8,128)(2,1)S(1)}, u32[]{:S(2)}, u32[]{:S(2)}) collective-permute-start(bf16[9,16,512]{2,1,0:T(8,128)(2,1)S(1)} %get-tuple-element.308), channel_id=1, source_target_pairs={{0,16},{2,18},{4,20},{6,22},{8,24},{10,26},{12,28},{14,30},{16,0},... | collective-permute-start | bytes 442376 | tf_op jit(solution)/shard_map/ppermute | solution.py:764
  162.0 2.0 %collective-permute-start.54 = (bf16[2,256,512]{2,1,0:T(8,128)(2,1)S(1)}, bf16[2,256,512]{2,1,0:T(8,128)(2,1)S(1)}, u32[]{:S(2)}, u32[]{:S(2)}) collective-permute-start(bf16[2,256,512]{2,1,0:T(8,128)(2,1)S(1)} %get-tuple-element.314), channel_id=1, source_target_pairs={{0,2},{2,0},{4,6},{6,4},{8,10},{10,8},{12,14},{14,12},{16,18},{18,... | collective-permute-start | bytes 1572872 | tf_op jit(solution)/shard_map/ppermute | solution.py:758
  164.1 12.7 %collective-permute-start.55 = (bf16[256,512]{1,0:T(8,128)(2,1)S(1)}, bf16[256,512]{1,0:T(8,128)(2,1)S(1)}, u32[]{:S(2)}, u32[]{:S(2)}) collective-permute-start(bf16[256,512]{1,0:T(8,128)(2,1)S(1)} %get-tuple-element.316), channel_id=1, source_target_pairs={{0,4},{2,6},{4,0},{6,2},{8,12},{10,14},{12,8},{14,10},{16,20},{18,... | collective-permute-start | bytes 786440 | tf_op jit(solution)/shard_map/ppermute | solution.py:761
  164.9 9.9 %collective-permute-start.56 = (bf16[13,16,512]{2,1,0:T(8,128)(2,1)S(1)}, bf16[13,16,512]{2,1,0:T(8,128)(2,1)S(1)}, u32[]{:S(2)}, u32[]{:S(2)}) collective-permute-start(bf16[13,16,512]{2,1,0:T(8,128)(2,1)S(1)} %lay.5), channel_id=1, source_target_pairs={{0,24},{2,26},{4,28},{6,30},{8,0},{10,2},{12,4},{14,6},{16,8},{18,... | collective-permute-start | bytes 638984 | tf_op jit(solution)/shard_map/ppermute | solution.py:764
  165.0 8.1 %collective-permute-start.58 = (bf16[4,16,512]{2,1,0:T(8,128)(2,1)S(1)}, bf16[4,16,512]{2,1,0:T(8,128)(2,1)S(1)}, u32[]{:S(2)}, u32[]{:S(2)}) collective-permute-start(bf16[4,16,512]{2,1,0:T(8,128)(2,1)S(1)} %lay.7), channel_id=1, source_target_pairs={{0,8},{2,10},{4,12},{6,14},{8,16},{10,18},{12,20},{14,22},{16,24},... | collective-permute-start | bytes 196616 | tf_op jit(solution)/shard_map/ppermute | solution.py:764
  167.1 7.2 %collective-permute-start.57 = (bf16[4,16,512]{2,1,0:T(8,128)(2,1)S(1)}, bf16[4,16,512]{2,1,0:T(8,128)(2,1)S(1)}, u32[]{:S(2)}, u32[]{:S(2)}) collective-permute-start(bf16[4,16,512]{2,1,0:T(8,128)(2,1)S(1)} %lay.6), channel_id=1, source_target_pairs={{0,16},{2,18},{4,20},{6,22},{8,24},{10,26},{12,28},{14,30},{16,0},... | collective-permute-start | bytes 196616 | tf_op jit(solution)/shard_map/ppermute | solution.py:764
  (18 other events, 106.8 us)
